TPU v7x, 512 devices: a whole 4x4x16 slice. The times are simulated.
512 devices in a mesh: row: 4 (over y), col: 16 (over z_lo, core), layer: 8 (over z_hi, x).
Axes of the slice: x: 4, y: 4, z: 16 (z_hi: 2, z_lo: 8; z = z_hi * 8 + z_lo), core: 2. Of those that a mesh axis runs over, the one named last changes fastest.
Arguments:
- density: bfloat16 [512, 128, 2176], P(('row', 'col', 'layer')), as said below
- pattern: int32 [512, 17], P(('row', 'col', 'layer')), may hold values from 0 to 1, as said below
- keep_flags: int32 [512, 21], P(('row', 'col', 'layer')), may hold values from 0 to 1, as said below
Outputs:
- purified: float32 [512, 128, 2688], P(('row', 'col', 'layer'))
Inputs may be any that keep to these rules, and one draw needn't show every extreme that they name: `pattern`: flag of block row i at offset o (column o + 8) equals that of block row i + o modulo 512 at offset -o; offset 0 is always 1. `keep_flags`: flag of block row i at offset o (column o + 10) equals that of block row i + o modulo 512 at offset -o; offset 0 is always 1. `density`: Symmetric: the block of row i at offset o is the transpose of the block of row i + o modulo 512 at offset -o.
All inputs are finite; a program needn't handle non-finite values.
Results may differ from a plain program's by a relative error of at most 0.002.
Values may be sent and summed in bfloat16 or wider, within the bound.
No kernel may reach another device: no remote copies, remote signals or barrier semaphores. Data moves between devices by JAX's collectives and lax.ppermute only.
A program may use at most 64 MiB of HBM per device.

v0:
```python
import jax
import jax.numpy as jnp
from jax import lax
from jax.sharding import PartitionSpec as P

BAND_HALF = 8
KEEP_HALF = 10


def passed_along(block, axis, distance):
    devices = range(lax.axis_size(axis))
    route = [((i - distance) % len(devices), i) for i in devices]
    return lax.ppermute(block, axis, route)


def widen_flags(flags, extent, dtype):
    grown = jnp.broadcast_to(flags.astype(dtype)[..., None], flags.shape + (extent,))
    return grown.reshape(flags.shape[:-1] + (flags.shape[-1] * extent,))


def purify_row(own_strip, fetch_row, keep_row):
    extent = own_strip.shape[0]
    kept_mask = widen_flags(keep_row, extent, jnp.float32)[None, :]
    square_slots = []
    for out_offset in range(-KEEP_HALF, KEEP_HALF + 1):
        lowest = max(-BAND_HALF, out_offset - BAND_HALF)
        highest = min(BAND_HALF, out_offset + BAND_HALF)
        left_part = own_strip[:, (lowest + BAND_HALF) * extent : (highest + BAND_HALF + 1) * extent]
        right_part = jnp.concatenate(
            [
                fetch_row(offset)[
                    :,
                    (out_offset - offset + BAND_HALF)
                    * extent : (out_offset - offset + BAND_HALF + 1)
                    * extent,
                ]
                for offset in range(lowest, highest + 1)
            ],
            axis=0,
        )
        square_slots.append(jnp.dot(left_part, right_part, preferred_element_type=jnp.float32))
    square = kept_mask * jnp.concatenate(square_slots, axis=1)
    rounded = square.astype(jnp.bfloat16)
    cube_slots = []
    for out_offset in range(-KEEP_HALF, KEEP_HALF + 1):
        lowest = max(-KEEP_HALF, out_offset - BAND_HALF)
        highest = min(KEEP_HALF, out_offset + BAND_HALF)
        left_part = rounded[:, (lowest + KEEP_HALF) * extent : (highest + KEEP_HALF + 1) * extent]
        right_part = jnp.concatenate(
            [
                fetch_row(offset)[
                    :,
                    (out_offset - offset + BAND_HALF)
                    * extent : (out_offset - offset + BAND_HALF + 1)
                    * extent,
                ]
                for offset in range(lowest, highest + 1)
            ],
            axis=0,
        )
        cube_slots.append(jnp.dot(left_part, right_part, preferred_element_type=jnp.float32))
    cube_part = kept_mask * jnp.concatenate(cube_slots, axis=1)
    return kept_mask * (3.0 * square - 2.0 * cube_part)


def body(density, pattern, keep_flags):
    own_rows = density.shape[0]
    extent = density.shape[1]
    distance = (KEEP_HALF + own_rows - 1) // own_rows
    masked = density * widen_flags(pattern, extent, jnp.bfloat16)[:, None, :]
    later_rows = []
    earlier_rows = []
    for step_count in range(1, distance + 1):
        later_rows.append(passed_along(masked, ("row", "col", "layer"), -step_count))
        earlier_rows.append(passed_along(masked, ("row", "col", "layer"), step_count))
    pieces = earlier_rows[::-1] + [masked] + later_rows
    row_number = 0

    def fetch_row(offset, row_number=row_number):
        position = distance * own_rows + row_number + offset
        return pieces[position // own_rows][position % own_rows]

    results = [purify_row(masked[row_number], fetch_row, keep_flags[row_number])]
    return jnp.stack(results)


def solution(mesh):
    placed = (
        P(("row", "col", "layer"), None, None),
        P(("row", "col", "layer"), None),
        P(("row", "col", "layer"), None),
    )
    return jax.shard_map(
        body,
        mesh=mesh,
        in_specs=placed,
        out_specs=P(("row", "col", "layer"), None, None),
        check_vma=False,
    )
```

profile of v0, /device:TPU:13, one launch (start us, length us, event | category | flops | bytes accessed | tf_op | source)
XLA Modules:
  0.0 979.5 jit_solution(13230521083337141840)
XLA Ops:
  1.9 15.4 %collective-permute-start.6 = (bf16[1,128,2176]{2,1,0:T(8,128)(2,1)S(1)}, bf16[1,128,2176]{2,1,0:T(8,128)(2,1)S(1)}, u32[]{:S(2)}, u32[]{:S(2)}) collective-permute-start(bf16[1,128,2176]{2,1,0:T(8,128)(2,1)S(1)} %broadcast_multiply_fusion), channel_id=1, source_target_pairs={{510,0},{511,1},{0,2},{1,3},{2,4},{3,5},{4,6},{5,7},{6,8},{7,9},{8... | collective-permute-start | bytes 1671176 | tf_op jit(solution)/shard_map/ppermute | solution.py:13
  17.3 3.8 collective-permute-start.5
  21.1 3.2 collective-permute-start.17
  24.3 1.9 collective-permute-start.16
  26.2 4.1 collective-permute-start
  30.5 139.7 %collective-permute-done.16 = bf16[1,128,2176]{2,1,0:T(8,128)(2,1)S(1)} collective-permute-done((bf16[1,128,2176]{2,1,0:T(8,128)(2,1)S(1)}, bf16[1,128,2176]{2,1,0:T(8,128)(2,1)S(1)}, u32[]{:S(2)}, u32[]{:S(2)}) %collective-permute-start.16) | collective-permute-done | bytes 557088 | tf_op jit(solution)/shard_map/ppermute | solution.py:13
  170.3 194.8 %collective-permute-start.1 = (bf16[1,128,2176]{2,1,0:T(8,128)(2,1)S(1)}, bf16[1,128,2176]{2,1,0:T(8,128)(2,1)S(1)}, u32[]{:S(2)}, u32[]{:S(2)}) collective-permute-start(bf16[1,128,2176]{2,1,0:T(8,128)(2,1)S(1)} %broadcast_multiply_fusion), channel_id=1, source_target_pairs={{505,0},{506,1},{507,2},{508,3},{509,4},{510,5},{511,6},{0,7},{1,8... | collective-permute-start | bytes 1671176 | tf_op jit(solution)/shard_map/ppermute | solution.py:13
  365.1 1.9 collective-permute-start.4
  367.2 34.7 %collective-permute-start.3 = (bf16[1,128,2176]{2,1,0:T(8,128)(2,1)S(1)}, bf16[1,128,2176]{2,1,0:T(8,128)(2,1)S(1)}, u32[]{:S(2)}, u32[]{:S(2)}) collective-permute-start(bf16[1,128,2176]{2,1,0:T(8,128)(2,1)S(1)} %broadcast_multiply_fusion), channel_id=1, source_target_pairs={{507,0},{508,1},{509,2},{510,3},{511,4},{0,5},{1,6},{2,7},{3,8},{4... | collective-permute-start | bytes 1671176 | tf_op jit(solution)/shard_map/ppermute | solution.py:13
  402.0 15.3 %collective-permute-start.2 = (bf16[1,128,2176]{2,1,0:T(8,128)(2,1)S(1)}, bf16[1,128,2176]{2,1,0:T(8,128)(2,1)S(1)}, u32[]{:S(2)}, u32[]{:S(2)}) collective-permute-start(bf16[1,128,2176]{2,1,0:T(8,128)(2,1)S(1)} %broadcast_multiply_fusion), channel_id=1, source_target_pairs={{506,0},{507,1},{508,2},{509,3},{510,4},{511,5},{0,6},{1,7},{2,8},... | collective-permute-start | bytes 1671176 | tf_op jit(solution)/shard_map/ppermute | solution.py:13
  417.5 19.9 %collective-permute-done.2 = bf16[1,128,2176]{2,1,0:T(8,128)(2,1)S(1)} collective-permute-done((bf16[1,128,2176]{2,1,0:T(8,128)(2,1)S(1)}, bf16[1,128,2176]{2,1,0:T(8,128)(2,1)S(1)}, u32[]{:S(2)}, u32[]{:S(2)}) %collective-permute-start.2) | collective-permute-done | bytes 557088 | tf_op jit(solution)/shard_map/ppermute | solution.py:13
  439.6 6.2 collective-permute-start.8
  446.0 32.0 %collective-permute-start.9 = (bf16[1,128,2176]{2,1,0:T(8,128)(2,1)S(1)}, bf16[1,128,2176]{2,1,0:T(8,128)(2,1)S(1)}, u32[]{:S(2)}, u32[]{:S(2)}) collective-permute-start(bf16[1,128,2176]{2,1,0:T(8,128)(2,1)S(1)} %broadcast_multiply_fusion), channel_id=1, source_target_pairs={{2,0},{3,1},{4,2},{5,3},{6,4},{7,5},{8,6},{9,7},{10,8},{11,9},{12,... | collective-permute-start | bytes 1671176 | tf_op jit(solution)/shard_map/ppermute | solution.py:13
  478.3 1.9 collective-permute-start.10
  480.5 1.9 collective-permute-start.11
  482.6 27.6 %collective-permute-start.12 = (bf16[1,128,2176]{2,1,0:T(8,128)(2,1)S(1)}, bf16[1,128,2176]{2,1,0:T(8,128)(2,1)S(1)}, u32[]{:S(2)}, u32[]{:S(2)}) collective-permute-start(bf16[1,128,2176]{2,1,0:T(8,128)(2,1)S(1)} %broadcast_multiply_fusion), channel_id=1, source_target_pairs={{5,0},{6,1},{7,2},{8,3},{9,4},{10,5},{11,6},{12,7},{13,8},{14,9},{... | collective-permute-start | bytes 1671176 | tf_op jit(solution)/shard_map/ppermute | solution.py:13
  511.0 95.1 %collective-permute-done.8 = bf16[1,128,2176]{2,1,0:T(8,128)(2,1)S(1)} collective-permute-done((bf16[1,128,2176]{2,1,0:T(8,128)(2,1)S(1)}, bf16[1,128,2176]{2,1,0:T(8,128)(2,1)S(1)}, u32[]{:S(2)}, u32[]{:S(2)}) %collective-permute-start.8) | collective-permute-done | bytes 557088 | tf_op jit(solution)/shard_map/ppermute | solution.py:13
  606.1 1.9 collective-permute-start.13
  608.3 43.7 %collective-permute-done.9 = bf16[1,128,2176]{2,1,0:T(8,128)(2,1)S(1)} collective-permute-done((bf16[1,128,2176]{2,1,0:T(8,128)(2,1)S(1)}, bf16[1,128,2176]{2,1,0:T(8,128)(2,1)S(1)}, u32[]{:S(2)}, u32[]{:S(2)}) %collective-permute-start.9) | collective-permute-done | bytes 557088 | tf_op jit(solution)/shard_map/ppermute | solution.py:13
  656.0 228.6 %collective-permute-start.15 = (bf16[1,128,2176]{2,1,0:T(8,128)(2,1)S(1)}, bf16[1,128,2176]{2,1,0:T(8,128)(2,1)S(1)}, u32[]{:S(2)}, u32[]{:S(2)}) collective-permute-start(bf16[1,128,2176]{2,1,0:T(8,128)(2,1)S(1)} %broadcast_multiply_fusion), channel_id=1, source_target_pairs={{8,0},{9,1},{10,2},{11,3},{12,4},{13,5},{14,6},{15,7},{16,8},{17,9... | collective-permute-start | bytes 1671176 | tf_op jit(solution)/shard_map/ppermute | solution.py:13
  885.4 1.9 collective-permute-start.18
  888.0 2.1 collective-permute-start.19
  901.1 1.9 collective-permute-done.18
  903.9 70.2 %collective-permute-done.19 = bf16[1,128,2176]{2,1,0:T(8,128)(2,1)S(1)} collective-permute-done((bf16[1,128,2176]{2,1,0:T(8,128)(2,1)S(1)}, bf16[1,128,2176]{2,1,0:T(8,128)(2,1)S(1)}, u32[]{:S(2)}, u32[]{:S(2)}) %collective-permute-start.19) | collective-permute-done | bytes 557088 | tf_op jit(solution)/shard_map/ppermute | solution.py:13
  (155 shorter events, 28.5 us)
Async XLA Ops:
  0.0 30.4 %copy-start = (bf16[1,128,2176]{2,1,0:T(8,128)(2,1)S(1)}, bf16[1,128,2176]{2,1,0:T(8,128)(2,1)}, u32[]{:S(2)}) copy-start(bf16[1,128,2176]{2,1,0:T(8,128)(2,1)} %param.3) | copy-start | bytes 1671172
  0.0 30.4 %copy-start.1 = (s32[1,21]{1,0:T(1,128)S(1)}, s32[1,21]{1,0:T(1,128)}, u32[]{:S(2)}) copy-start(s32[1,21]{1,0:T(1,128)} %param.5) | copy-start | bytes 256
  1.9 478.5 %collective-permute-start.6 = (bf16[1,128,2176]{2,1,0:T(8,128)(2,1)S(1)}, bf16[1,128,2176]{2,1,0:T(8,128)(2,1)S(1)}, u32[]{:S(2)}, u32[]{:S(2)}) collective-permute-start(bf16[1,128,2176]{2,1,0:T(8,128)(2,1)S(1)} %broadcast_multiply_fusion), channel_id=1, source_target_pairs={{510,0},{511,1},{0,2},{1,3},{2,4},{3,5},{4,6},{5,7},{6,8},{7,9},{8... | collective-permute-start | bytes 1671176 | tf_op jit(solution)/shard_map/ppermute | solution.py:13
  17.3 461.0 %collective-permute-start.5 = (bf16[1,128,2176]{2,1,0:T(8,128)(2,1)S(1)}, bf16[1,128,2176]{2,1,0:T(8,128)(2,1)S(1)}, u32[]{:S(2)}, u32[]{:S(2)}) collective-permute-start(bf16[1,128,2176]{2,1,0:T(8,128)(2,1)S(1)} %broadcast_multiply_fusion), channel_id=1, source_target_pairs={{509,0},{510,1},{511,2},{0,3},{1,4},{2,5},{3,6},{4,7},{5,8},{6,9},... | collective-permute-start | bytes 1671176 | tf_op jit(solution)/shard_map/ppermute | solution.py:13
  21.1 344.0 %collective-permute-start.17 = (bf16[1,128,2176]{2,1,0:T(8,128)(2,1)S(1)}, bf16[1,128,2176]{2,1,0:T(8,128)(2,1)S(1)}, u32[]{:S(2)}, u32[]{:S(2)}) collective-permute-start(bf16[1,128,2176]{2,1,0:T(8,128)(2,1)S(1)} %broadcast_multiply_fusion), channel_id=1, source_target_pairs={{503,0},{504,1},{505,2},{506,3},{507,4},{508,5},{509,6},{510,7},{5... | collective-permute-start | bytes 1671176 | tf_op jit(solution)/shard_map/ppermute | solution.py:13
  24.3 146.0 %collective-permute-start.16 = (bf16[1,128,2176]{2,1,0:T(8,128)(2,1)S(1)}, bf16[1,128,2176]{2,1,0:T(8,128)(2,1)S(1)}, u32[]{:S(2)}, u32[]{:S(2)}) collective-permute-start(bf16[1,128,2176]{2,1,0:T(8,128)(2,1)S(1)} %broadcast_multiply_fusion), channel_id=1, source_target_pairs={{502,0},{503,1},{504,2},{505,3},{506,4},{507,5},{508,6},{509,7},{5... | collective-permute-start | bytes 1671176 | tf_op jit(solution)/shard_map/ppermute | solution.py:13
  26.2 340.9 %collective-permute-start = (bf16[1,128,2176]{2,1,0:T(8,128)(2,1)S(1)}, bf16[1,128,2176]{2,1,0:T(8,128)(2,1)S(1)}, u32[]{:S(2)}, u32[]{:S(2)}) collective-permute-start(bf16[1,128,2176]{2,1,0:T(8,128)(2,1)S(1)} %broadcast_multiply_fusion), channel_id=1, source_target_pairs={{504,0},{505,1},{506,2},{507,3},{508,4},{509,5},{510,6},{511,7},{0... | collective-permute-start | bytes 1671176 | tf_op jit(solution)/shard_map/ppermute | solution.py:13
  170.3 231.7 %collective-permute-start.1 = (bf16[1,128,2176]{2,1,0:T(8,128)(2,1)S(1)}, bf16[1,128,2176]{2,1,0:T(8,128)(2,1)S(1)}, u32[]{:S(2)}, u32[]{:S(2)}) collective-permute-start(bf16[1,128,2176]{2,1,0:T(8,128)(2,1)S(1)} %broadcast_multiply_fusion), channel_id=1, source_target_pairs={{505,0},{506,1},{507,2},{508,3},{509,4},{510,5},{511,6},{0,7},{1,8... | collective-permute-start | bytes 1671176 | tf_op jit(solution)/shard_map/ppermute | solution.py:13
  365.1 80.9 %collective-permute-start.4 = (bf16[1,128,2176]{2,1,0:T(8,128)(2,1)S(1)}, bf16[1,128,2176]{2,1,0:T(8,128)(2,1)S(1)}, u32[]{:S(2)}, u32[]{:S(2)}) collective-permute-start(bf16[1,128,2176]{2,1,0:T(8,128)(2,1)S(1)} %broadcast_multiply_fusion), channel_id=1, source_target_pairs={{508,0},{509,1},{510,2},{511,3},{0,4},{1,5},{2,6},{3,7},{4,8},{5,9... | collective-permute-start | bytes 1671176 | tf_op jit(solution)/shard_map/ppermute | solution.py:13
  367.2 72.4 %collective-permute-start.3 = (bf16[1,128,2176]{2,1,0:T(8,128)(2,1)S(1)}, bf16[1,128,2176]{2,1,0:T(8,128)(2,1)S(1)}, u32[]{:S(2)}, u32[]{:S(2)}) collective-permute-start(bf16[1,128,2176]{2,1,0:T(8,128)(2,1)S(1)} %broadcast_multiply_fusion), channel_id=1, source_target_pairs={{507,0},{508,1},{509,2},{510,3},{511,4},{0,5},{1,6},{2,7},{3,8},{4... | collective-permute-start | bytes 1671176 | tf_op jit(solution)/shard_map/ppermute | solution.py:13
  402.0 35.4 %collective-permute-start.2 = (bf16[1,128,2176]{2,1,0:T(8,128)(2,1)S(1)}, bf16[1,128,2176]{2,1,0:T(8,128)(2,1)S(1)}, u32[]{:S(2)}, u32[]{:S(2)}) collective-permute-start(bf16[1,128,2176]{2,1,0:T(8,128)(2,1)S(1)} %broadcast_multiply_fusion), channel_id=1, source_target_pairs={{506,0},{507,1},{508,2},{509,3},{510,4},{511,5},{0,6},{1,7},{2,8},... | collective-permute-start | bytes 1671176 | tf_op jit(solution)/shard_map/ppermute | solution.py:13
  437.4 45.2 %collective-permute-start.7 = (bf16[1,128,2176]{2,1,0:T(8,128)(2,1)S(1)}, bf16[1,128,2176]{2,1,0:T(8,128)(2,1)S(1)}, u32[]{:S(2)}, u32[]{:S(2)}) collective-permute-start(bf16[1,128,2176]{2,1,0:T(8,128)(2,1)S(1)} %broadcast_multiply_fusion), channel_id=1, source_target_pairs={{511,0},{0,1},{1,2},{2,3},{3,4},{4,5},{5,6},{6,7},{7,8},{8,9},{9,1... | collective-permute-start | bytes 1671176 | tf_op jit(solution)/shard_map/ppermute | solution.py:13
  439.6 166.5 %collective-permute-start.8 = (bf16[1,128,2176]{2,1,0:T(8,128)(2,1)S(1)}, bf16[1,128,2176]{2,1,0:T(8,128)(2,1)S(1)}, u32[]{:S(2)}, u32[]{:S(2)}) collective-permute-start(bf16[1,128,2176]{2,1,0:T(8,128)(2,1)S(1)} %broadcast_multiply_fusion), channel_id=1, source_target_pairs={{1,0},{2,1},{3,2},{4,3},{5,4},{6,5},{7,6},{8,7},{9,8},{10,9},{11,1... | collective-permute-start | bytes 1671176 | tf_op jit(solution)/shard_map/ppermute | solution.py:13
  446.0 206.0 %collective-permute-start.9 = (bf16[1,128,2176]{2,1,0:T(8,128)(2,1)S(1)}, bf16[1,128,2176]{2,1,0:T(8,128)(2,1)S(1)}, u32[]{:S(2)}, u32[]{:S(2)}) collective-permute-start(bf16[1,128,2176]{2,1,0:T(8,128)(2,1)S(1)} %broadcast_multiply_fusion), channel_id=1, source_target_pairs={{2,0},{3,1},{4,2},{5,3},{6,4},{7,5},{8,6},{9,7},{10,8},{11,9},{12,... | collective-permute-start | bytes 1671176 | tf_op jit(solution)/shard_map/ppermute | solution.py:13
  478.3 177.7 %collective-permute-start.10 = (bf16[1,128,2176]{2,1,0:T(8,128)(2,1)S(1)}, bf16[1,128,2176]{2,1,0:T(8,128)(2,1)S(1)}, u32[]{:S(2)}, u32[]{:S(2)}) collective-permute-start(bf16[1,128,2176]{2,1,0:T(8,128)(2,1)S(1)} %broadcast_multiply_fusion), channel_id=1, source_target_pairs={{3,0},{4,1},{5,2},{6,3},{7,4},{8,5},{9,6},{10,7},{11,8},{12,9},{13... | collective-permute-start | bytes 1671176 | tf_op jit(solution)/shard_map/ppermute | solution.py:13
  480.5 404.9 %collective-permute-start.11 = (bf16[1,128,2176]{2,1,0:T(8,128)(2,1)S(1)}, bf16[1,128,2176]{2,1,0:T(8,128)(2,1)S(1)}, u32[]{:S(2)}, u32[]{:S(2)}) collective-permute-start(bf16[1,128,2176]{2,1,0:T(8,128)(2,1)S(1)} %broadcast_multiply_fusion), channel_id=1, source_target_pairs={{4,0},{5,1},{6,2},{7,3},{8,4},{9,5},{10,6},{11,7},{12,8},{13,9},{1... | collective-permute-start | bytes 1671176 | tf_op jit(solution)/shard_map/ppermute | solution.py:13
  482.6 405.4 %collective-permute-start.12 = (bf16[1,128,2176]{2,1,0:T(8,128)(2,1)S(1)}, bf16[1,128,2176]{2,1,0:T(8,128)(2,1)S(1)}, u32[]{:S(2)}, u32[]{:S(2)}) collective-permute-start(bf16[1,128,2176]{2,1,0:T(8,128)(2,1)S(1)} %broadcast_multiply_fusion), channel_id=1, source_target_pairs={{5,0},{6,1},{7,2},{8,3},{9,4},{10,5},{11,6},{12,7},{13,8},{14,9},{... | collective-permute-start | bytes 1671176 | tf_op jit(solution)/shard_map/ppermute | solution.py:13
  606.1 284.8 %collective-permute-start.13 = (bf16[1,128,2176]{2,1,0:T(8,128)(2,1)S(1)}, bf16[1,128,2176]{2,1,0:T(8,128)(2,1)S(1)}, u32[]{:S(2)}, u32[]{:S(2)}) collective-permute-start(bf16[1,128,2176]{2,1,0:T(8,128)(2,1)S(1)} %broadcast_multiply_fusion), channel_id=1, source_target_pairs={{6,0},{7,1},{8,2},{9,3},{10,4},{11,5},{12,6},{13,7},{14,8},{15,9},... | collective-permute-start | bytes 1671176 | tf_op jit(solution)/shard_map/ppermute | solution.py:13
  652.0 239.6 %collective-permute-start.14 = (bf16[1,128,2176]{2,1,0:T(8,128)(2,1)S(1)}, bf16[1,128,2176]{2,1,0:T(8,128)(2,1)S(1)}, u32[]{:S(2)}, u32[]{:S(2)}) collective-permute-start(bf16[1,128,2176]{2,1,0:T(8,128)(2,1)S(1)} %broadcast_multiply_fusion), channel_id=1, source_target_pairs={{7,0},{8,1},{9,2},{10,3},{11,4},{12,5},{13,6},{14,7},{15,8},{16,9}... | collective-permute-start | bytes 1671176 | tf_op jit(solution)/shard_map/ppermute | solution.py:13
  656.0 236.4 %collective-permute-start.15 = (bf16[1,128,2176]{2,1,0:T(8,128)(2,1)S(1)}, bf16[1,128,2176]{2,1,0:T(8,128)(2,1)S(1)}, u32[]{:S(2)}, u32[]{:S(2)}) collective-permute-start(bf16[1,128,2176]{2,1,0:T(8,128)(2,1)S(1)} %broadcast_multiply_fusion), channel_id=1, source_target_pairs={{8,0},{9,1},{10,2},{11,3},{12,4},{13,5},{14,6},{15,7},{16,8},{17,9... | collective-permute-start | bytes 1671176 | tf_op jit(solution)/shard_map/ppermute | solution.py:13
  885.4 17.7 %collective-permute-start.18 = (bf16[1,128,2176]{2,1,0:T(8,128)(2,1)S(1)}, bf16[1,128,2176]{2,1,0:T(8,128)(2,1)S(1)}, u32[]{:S(2)}, u32[]{:S(2)}) collective-permute-start(bf16[1,128,2176]{2,1,0:T(8,128)(2,1)S(1)} %broadcast_multiply_fusion), channel_id=1, source_target_pairs={{9,0},{10,1},{11,2},{12,3},{13,4},{14,5},{15,6},{16,7},{17,8},{18,... | collective-permute-start | bytes 1671176 | tf_op jit(solution)/shard_map/ppermute | solution.py:13
  888.0 86.0 %collective-permute-start.19 = (bf16[1,128,2176]{2,1,0:T(8,128)(2,1)S(1)}, bf16[1,128,2176]{2,1,0:T(8,128)(2,1)S(1)}, u32[]{:S(2)}, u32[]{:S(2)}) collective-permute-start(bf16[1,128,2176]{2,1,0:T(8,128)(2,1)S(1)} %broadcast_multiply_fusion), channel_id=1, source_target_pairs={{10,0},{11,1},{12,2},{13,3},{14,4},{15,5},{16,6},{17,7},{18,8},{19... | collective-permute-start | bytes 1671176 | tf_op jit(solution)/shard_map/ppermute | solution.py:13
where the time goes:
time: 980 us; the launch traced here: 979 us
  starting transfers between devices  583 us (59%)
  waiting for transfers between devices  372 us (38%)
  matrix products  13.9 us (1%)
    ppermute x20, starting transfers between devices, passed_along(): return lax.ppermute(block, axis, route)  583 us
    ppermute x20, waiting for transfers between devices, passed_along(): return lax.ppermute(block, axis, route)  372 us
  transfers between devices with their start and end apart: 20, of which 7 were waited for; matrix products, arithmetic and copies ran while one was open for 2% of the time, Pallas kernels for 0%

commit v1 on v0

v1 whole, which is shorter than its diff:
```python
import functools

import jax
import jax.numpy as jnp
import numpy as np
from jax import lax
from jax.experimental import pallas as pl
from jax.experimental.pallas import tpu as pltpu
from jax.sharding import Mesh, PartitionSpec as P

BLK = 128
BAND_HALF = 8
KEEP_HALF = 10
KEPT = 21
AXES = ("y", "zl", "c", "zh", "x")
UPPER = BAND_HALF + 1
DUMMY = KEPT * UPPER


def canonical(row, offset, n):
    return (row % n, offset) if offset >= 0 else ((row + offset) % n, -offset)


def own_lists(core, p):
    if core == 0:
        same = list(range(-p, 1)) + list(range(-8, -4 - p))
        same += {0: [8], 1: [7, 8], 2: [7, 8], 3: [7, 8]}[p]
    else:
        same = list(range(0, 4 - p)) + list(range(8 - p, 9))
        same += {0: [-6, -5], 1: [-6], 2: [], 3: []}[p]
    mixed = list(range(-p - 4, -p)) + list(range(4 - p, 8 - p))
    return same, mixed


def make_plan(ny, nzl):
    n = ny * nzl * 16

    def place(y, zl, c, zh, x):
        return (((y % ny) * nzl + zl) * 2 + c) * 8 + zh * 4 + x

    coords = [(y, zl, c, zh, x) for y in range(ny) for zl in range(nzl) for c in range(2) for zh in range(2) for x in range(4)]

    def ring(y, zl, zh, step):
        z = zh * nzl + zl
        y += 1 if (step == 1 and zl == nzl - 1) else -1 if (step == -1 and zl == 0) else 0
        z = (z + step) % (2 * nzl)
        return y, z % nzl, z // nzl

    need = [{((i - KEEP_HALF + u) % n, o): u * UPPER + o for u in range(KEPT) for o in range(UPPER) if u + o < KEPT} for i in range(n)]
    same_side, share = [], []
    for i, (y, zl, c, zh, x) in enumerate(coords):
        same, mixed = own_lists(c, x)
        same_side.append(same)
        share.append(same + mixed)
    k1 = max(map(len, same_side))
    k2 = max(map(len, share))
    pad = lambda seq, k, fill=None: list(seq) + [fill] * (k - len(seq))
    own = [[canonical(i, o, n) for o in range(-8, 9)] for i in range(n)]
    sent1 = [pad([canonical(i, o, n) for o in same_side[i]], k1) for i in range(n)]
    sent2 = [pad([canonical(i, o, n) for o in share[i]], k2) for i in range(n)]
    peer = lambda i, **kw: place(*[{**dict(zip(AXES, coords[i])), **kw}[a] for a in AXES])
    flip = lambda i, a: peer(i, **{a: 1 - coords[i][AXES.index(a)]})
    got2 = [sum([sent2[peer(i, x=q)] for q in range(4)], []) for i in range(n)]
    got3 = [sum([sent1[flip(peer(i, x=q), "zh")] for q in range(4)], []) for i in range(n)]
    got2c = [got2[flip(i, "c")] for i in range(n)]
    got3c = [got3[flip(i, "c")] for i in range(n)]
    pairs_seam, pairs_z, pairs_far = [], [], []
    for i, (y, zl, c, zh, x) in enumerate(coords):
        if (zl, c, zh) in ((0, 0, 0), (nzl - 1, 1, 1)):
            pairs_seam.append((i, flip(i, "zh")))
        y2, zl2, zh2 = ring(y, zl, zh, 1 if c else -1)
        pairs_z.append((i, place(y2, zl2, 1 - c, zh2, x)))
        pairs_far.append((i, place(y2, zl2, c, zh2, x)))
    known = [set(own[i] + got2[i] + got3[i] + got2c[i] + got3c[i]) for i in range(n)]
    gathered = [own[i] + got2[i] + got2c[i] + got3[i] + got3c[i] for i in range(n)]

    def choose(pairs, sources, limit=None):
        sends = [[] for _ in range(n)]
        for s, d in pairs:
            have = set(sources(s))
            sends[s] = [b for b in need[d] if b in have and b not in known[d]]
        k = max(map(len, sends))
        sends = [pad(q, k) for q in sends]
        got = [[None] * k for _ in range(n)]
        for s, d in pairs:
            got[d] = sends[s]
            known[d] |= set(sends[s])
        return k, sends, got

    ks, sent_s, got_s = choose(pairs_seam, lambda s: own[s] + got2[s])
    kz, sent_z, got_z = choose(pairs_z, lambda s: gathered[s])
    pairs_far = [(s, d) for s, d in pairs_far if set(need[d]) - known[d]]
    kf, sent_f, got_f = choose(pairs_far, lambda s: gathered[s])
    for i in range(n):
        assert not (set(need[i]) - known[i])

    def where(lists, sources):
        return np.array([[src.index(b) if b is not None else 0 for b in q] for q, src in zip(lists, sources)], np.int32)

    spots = np.full((n, sum(map(len, (own[0], got2[0], got2c[0], got3[0], got3c[0], got_s[0], got_z[0], got_f[0])))), DUMMY, np.int32)
    for i in range(n):
        seen = set()
        for k, b in enumerate(own[i] + got2[i] + got2c[i] + got3[i] + got3c[i] + got_s[i] + got_z[i] + got_f[i]):
            if b is not None and b in need[i] and b not in seen:
                seen.add(b)
                spots[i, k] = need[i][b]
    first = np.concatenate([where(sent1, own), where(sent2, own)], axis=1)
    return dict(
        n=n, k1=k1, k2=k2, ks=ks, kz=kz, kf=kf, first=first, spots=spots,
        seam=where(sent_s, [o + g for o, g in zip(own, got2)]),
        z=where([a + b for a, b in zip(sent_z, sent_f)], gathered), pairs_seam=pairs_seam, pairs_z=pairs_z, pairs_far=pairs_far,
        pairs_zh=[(i, flip(i, "zh")) for i in range(n)], pairs_c=[(i, flip(i, "c")) for i in range(n)],
    )


def vmem(*shape, dtype=jnp.bfloat16):
    return jax.ShapeDtypeStruct(shape, dtype)


def whole():
    return pl.BlockSpec(memory_space=pltpu.VMEM)


def scalars():
    return pl.BlockSpec(memory_space=pltpu.SMEM)


def call(kernel, outs, n_scalar, n_vector, scratch=()):
    return pl.pallas_call(
        kernel,
        out_shape=outs,
        in_specs=[scalars()] * n_scalar + [whole()] * n_vector,
        out_specs=jax.tree.map(lambda _: whole(), outs),
        scratch_shapes=scratch,
        compiler_params=pltpu.CompilerParams(vmem_limit_bytes=48 << 20),
    )


def first_kernel(k1, k2, table, pattern, strip, masked, own, send1, send2):
    for slot in range(2 * BAND_HALF + 1):
        cols = slice(slot * BLK, (slot + 1) * BLK)
        block = strip[0, :, cols] * pattern[0, slot].astype(jnp.bfloat16)
        masked[:, cols] = block
        own[slot] = block if slot >= BAND_HALF else block.T

    def pack1(k, carry):
        send1[k] = own[table[k]]
        return carry

    def pack2(k, carry):
        block = own[table[k1 + k]]
        for q in range(4):
            send2[q, k] = block
        return carry

    lax.fori_loop(0, k1, pack1, 0)
    lax.fori_loop(0, k2, pack2, 0)


def gather_kernel(n_sources, table, *refs):
    sources, outs = refs[:n_sources], refs[n_sources:]
    start = 0
    for out in outs:

        def pack(k, carry, out=out, start=start):
            at = table[start + k]
            low = 0
            for source in sources:
                count = source.shape[0]

                @pl.when((at >= low) & (at < low + count))
                def _(source=source, low=low):
                    out[k] = source[at - low]

                low += count
            return carry

        lax.fori_loop(0, out.shape[0], pack, 0)
        start += out.shape[0]


def product(left, first, pool, v):
    last = KEPT - 1 - first
    total = None
    low, high = max(first, v - BAND_HALF), min(last, v)
    if low <= high:
        right = jnp.concatenate([pool[u * UPPER + v - u] for u in range(low, high + 1)], axis=0)
        total = jnp.dot(left[:, (low - first) * BLK : (high - first + 1) * BLK], right, preferred_element_type=jnp.float32)
    low, high = max(first, v + 1), min(last, v + BAND_HALF)
    if low <= high:
        right = jnp.concatenate([pool[v * UPPER + u - v] for u in range(low, high + 1)], axis=1)
        part = lax.dot_general(
            left[:, (low - first) * BLK : (high - first + 1) * BLK], right,
            (((1,), (1,)), ((), ())), preferred_element_type=jnp.float32)
        total = part if total is None else total + part
    return total


def final_kernel(spots, keep, masked, *refs):
    *sources, out, pool, square, rounded = refs
    low = 0
    for source in sources:

        def place(k, carry, source=source, low=low):
            at = spots[low + k]

            @pl.when(at < DUMMY)
            def _():
                pool[at] = source[k]

            return carry

        lax.fori_loop(0, source.shape[0], place, 0)
        low += source.shape[0]
    for v in range(KEPT):
        cols = slice(v * BLK, (v + 1) * BLK)
        value = product(masked, KEEP_HALF - BAND_HALF, pool, v) * keep[0, v].astype(jnp.float32)
        square[:, cols] = value
        rounded[:, cols] = value.astype(jnp.bfloat16)
    for v in range(KEPT):
        cols = slice(v * BLK, (v + 1) * BLK)
        flag = keep[0, v].astype(jnp.float32)
        cube = flag * product(rounded, 0, pool, v)
        out[0, :, cols] = flag * (3.0 * square[:, cols] - 2.0 * cube)


def solution(mesh):
    ny, nzl = mesh.shape["row"], mesh.shape["col"] // 2
    plan = make_plan(ny, nzl)
    fine = Mesh(mesh.devices.reshape(ny, nzl, 2, 2, 4), AXES)
    k1, k2, ks, kz, kf = (plan[k] for k in ("k1", "k2", "ks", "kz", "kf"))
    tables = np.concatenate([plan["first"], plan["seam"], plan["z"], plan["spots"]], axis=1)
    cuts = np.cumsum([k1 + k2, ks, kz + kf])

    def body(density, pattern, keep):
        mine = lax.dynamic_index_in_dim(jnp.asarray(tables), lax.axis_index(AXES), 0, keepdims=False)
        t_first, t_seam, t_z, t_spots = jnp.split(mine, cuts)
        masked, own, send1, send2 = call(
            lambda *r: first_kernel(k1, k2, *r),
            (vmem(BLK, 17 * BLK), vmem(17, BLK, BLK), vmem(k1, BLK, BLK), vmem(4, k2, BLK, BLK)), 2, 1,
        )(t_first, pattern, density)
        got1 = lax.ppermute(send1, AXES, plan["pairs_zh"])
        got2 = lax.all_to_all(send2, "x", 0, 0).reshape(4 * k2, BLK, BLK)
        send3 = jnp.broadcast_to(got1, (4, k1, BLK, BLK))
        got3 = lax.all_to_all(send3, "x", 0, 0).reshape(4 * k1, BLK, BLK)
        got2c = lax.ppermute(got2, AXES, plan["pairs_c"])
        send_s = call(functools.partial(gather_kernel, 2), vmem(ks, BLK, BLK), 1, 2)(t_seam, own, got2)
        got_s = lax.ppermute(send_s, AXES, plan["pairs_seam"])
        got3c = lax.ppermute(got3, AXES, plan["pairs_c"])
        send_z, send_f = call(functools.partial(gather_kernel, 5), (vmem(kz, BLK, BLK), vmem(kf, BLK, BLK)), 1, 5)(t_z, own, got2, got2c, got3, got3c)
        got_z = lax.ppermute(send_z, AXES, plan["pairs_z"])
        got_f = lax.ppermute(send_f, AXES, plan["pairs_far"])
        return call(
            final_kernel, vmem(1, BLK, KEPT * BLK, dtype=jnp.float32), 2, 9,
            [
                pltpu.VMEM((DUMMY, BLK, BLK), jnp.bfloat16),
                pltpu.VMEM((BLK, KEPT * BLK), jnp.float32),
                pltpu.VMEM((BLK, KEPT * BLK), jnp.bfloat16),
            ],
        )(t_spots, keep, masked, own, got2, got2c, got3, got3c, got_s, got_z, got_f)

    return jax.shard_map(
        body,
        mesh=fine,
        in_specs=(P(AXES, None, None), P(AXES, None), P(AXES, None)),
        out_specs=P(AXES, None, None),
        check_vma=False,
    )
```

time: 980 us -> 143 us (0.15)
  the two profiles are of different devices: /device:TPU:13 before, /device:TPU:1 now
where the time goes in v1:
time: 143 us; the launch traced here: 142 us
  starting transfers between devices  47.8 us (33%)
  blocking collectives  40.1 us (28%)
  waiting for transfers between devices  25.6 us (18%)
  Pallas kernels  21 us (15%)
  local copies, waits for them, and re-layouts  7.55 us (5%)
    all_to_all x1, blocking collectives, body(): got2 = lax.all_to_all(send2, 'x', 0, 0).reshape(4 * k2, BLK, BLK)  24.9 us
    ppermute x1, waiting for transfers between devices, body(): got_f = lax.ppermute(send_f, AXES, plan['pairs_far'])  18.2 us
    ppermute x1, starting transfers between devices, body(): got_z = lax.ppermute(send_z, AXES, plan['pairs_z'])  17.8 us
    ppermute x1, starting transfers between devices, body(): got1 = lax.ppermute(send1, AXES, plan['pairs_zh'])  15.4 us
    all_to_all x1, blocking collectives, body(): got3 = lax.all_to_all(send3, 'x', 0, 0).reshape(4 * k1, BLK, BLK)  15.2 us
    pallas_call x1, Pallas kernels, body(): call(final_kernel, vmem(1, BLK, KEPT * BLK, dtype=jnp.float32), 2, 9, [pl...  12.5 us
    ppermute x1, starting transfers between devices, body(): got2c = lax.ppermute(got2, AXES, plan['pairs_c'])  7.52 us
    ppermute x1, waiting for transfers between devices, body(): got1 = lax.ppermute(send1, AXES, plan['pairs_zh'])  5.96 us
  transfers between devices with their start and end apart: 6, of which 3 were waited for; matrix products, arithmetic and copies ran while one was open for 2% of the time, Pallas kernels for 1%

profile of v1, /device:TPU:1, one launch (start us, length us, event | category | flops | bytes accessed | tf_op | source)
XLA Modules:
  0.0 142.1 jit_solution(3397493451441826575)
XLA Ops:
  0.0 0.7 dynamic-slice_bitcast_fusion.2.r_0_
  0.7 1.1 copy-done.4
  1.7 0.7 copy-done.6
  2.4 1.1 shard_map.46
  3.5 24.9 %all_to_all.10 = bf16[4,15,128,128]{3,2,1,0:T(8,128)(2,1)S(1)} all-to-all(bf16[4,15,128,128]{3,2,1,0:T(8,128)(2,1)S(1)} %get-tuple-element.13), channel_id=1, replica_groups=mesh['y'=4,'zl'=8,'c'=2,'zh'=2,'x'=4] {'x'}, dimensions={0} | all-to-all | bytes 3932160 | tf_op jit(solution)/shard_map/all_to_all | solution.py:243
  28.4 7.5 %collective-permute-start = (bf16[60,128,128]{2,1,0:T(8,128)(2,1)S(1)}, bf16[60,128,128]{2,1,0:T(8,128)(2,1)}, u32[]{:S(2)}, u32[]{:S(2)}) collective-permute-start(bf16[60,128,128]{2,1,0:T(8,128)(2,1)S(1)} %bitcast.8), channel_id=1, source_target_pairs={{0,8},{1,9},{2,10},{3,11},{4,12},{5,13},{6,14},{7,15},{8,0},{9,1},... | collective-permute-start | bytes 5898248 | tf_op jit(solution)/shard_map/ppermute | solution.py:246
  35.9 15.4 %collective-permute-start.1 = (bf16[7,128,128]{2,1,0:T(8,128)(2,1)S(1)}, bf16[7,128,128]{2,1,0:T(8,128)(2,1)S(1)}, u32[]{:S(2)}, u32[]{:S(2)}) collective-permute-start(bf16[7,128,128]{2,1,0:T(8,128)(2,1)S(1)} %get-tuple-element.14), channel_id=1, source_target_pairs={{0,4},{1,5},{2,6},{3,7},{4,0},{5,1},{6,2},{7,3},{8,12},{9,13},{10,... | collective-permute-start | bytes 688136 | tf_op jit(solution)/shard_map/ppermute | solution.py:242
  51.4 6.0 %collective-permute-done.1 = bf16[7,128,128]{2,1,0:T(8,128)(2,1)S(1)} collective-permute-done((bf16[7,128,128]{2,1,0:T(8,128)(2,1)S(1)}, bf16[7,128,128]{2,1,0:T(8,128)(2,1)S(1)}, u32[]{:S(2)}, u32[]{:S(2)}) %collective-permute-start.1) | collective-permute-done | bytes 229408 | tf_op jit(solution)/shard_map/ppermute | solution.py:242
  57.4 0.2 broadcast_in_dim.3
  57.6 15.2 %all_to_all.11 = bf16[4,7,128,128]{3,2,1,0:T(8,128)(2,1)S(1)} all-to-all(bf16[4,7,128,128]{3,2,1,0:T(8,128)(2,1)S(1)} %broadcast_in_dim.3), channel_id=1, replica_groups=mesh['y'=4,'zl'=8,'c'=2,'zh'=2,'x'=4] {'x'}, dimensions={0} | all-to-all | bytes 1835008 | tf_op jit(solution)/shard_map/all_to_all | solution.py:245
  72.8 3.7 %collective-permute-start.2 = (bf16[28,128,128]{2,1,0:T(8,128)(2,1)S(1)}, bf16[28,128,128]{2,1,0:T(8,128)(2,1)}, u32[]{:S(2)}, u32[]{:S(2)}) collective-permute-start(bf16[28,128,128]{2,1,0:T(8,128)(2,1)S(1)} %bitcast.12), channel_id=1, source_target_pairs={{0,8},{1,9},{2,10},{3,11},{4,12},{5,13},{6,14},{7,15},{8,0},{9,1},... | collective-permute-start | bytes 2752520 | tf_op jit(solution)/shard_map/ppermute | solution.py:249
  76.5 0.8 dynamic-slice_bitcast_fusion.table
  77.3 1.4 %collective-permute-done.2.refs_4_ = bf16[28,128,128]{2,1,0:T(8,128)(2,1)} collective-permute-done((bf16[28,128,128]{2,1,0:T(8,128)(2,1)S(1)}, bf16[28,128,128]{2,1,0:T(8,128)(2,1)}, u32[]{:S(2)}, u32[]{:S(2)}) %collective-permute-start.2) | collective-permute-done | bytes 917536 | tf_op jit(solution)/shard_map/ppermute | solution.py:249
  78.7 5.8 %shard_map.48 = (bf16[54,128,128]{2,1,0:T(8,128)(2,1)}, bf16[3,128,128]{2,1,0:T(8,128)(2,1)S(1)}) custom-call(s32[57]{0:T(128)S(1)} %dynamic-slice_bitcast_fusion.table, bf16[17,128,128]{2,1,0:T(8,128)(2,1)S(1)} %get-tuple-element.12.refs_0_, bf16[60,128,128]{2,1,0:T(8,128)(2,1)} %bitcast.9, bf16[60,128,128]{2,1,0:T(8,128)(2,1)} %collective-permute-done.refs_2_, ...), custom_call_target="tpu_custom_call" | custom-call | tf_op jit(solution)/shard_map/pallas_call | solution.py:250
  84.5 17.8 %collective-permute-start.4 = (bf16[54,128,128]{2,1,0:T(8,128)(2,1)}, bf16[54,128,128]{2,1,0:T(8,128)(2,1)S(1)}, u32[]{:S(2)}, u32[]{:S(2)}) collective-permute-start(bf16[54,128,128]{2,1,0:T(8,128)(2,1)} %get-tuple-element.15), channel_id=1, source_target_pairs={{0,508},{1,509},{2,510},{3,511},{4,504},{5,505},{6,506},{7,507},{8... | collective-permute-start | bytes 5308424 | tf_op jit(solution)/shard_map/ppermute | solution.py:251
  102.3 0.8 dynamic-slice_bitcast_fusion.1.table
  103.0 1.5 %copy-done.1 = bf16[4,15,128,128]{3,2,1,0:T(8,128)(2,1)S(1)} copy-done((bf16[4,15,128,128]{3,2,1,0:T(8,128)(2,1)S(1)}, bf16[4,15,128,128]{3,2,1,0:T(8,128)(2,1)}, u32[]{:S(2)}) %copy-start.1) | copy-done | bytes 1966104
  104.6 1.6 %shard_map.47 = bf16[16,128,128]{2,1,0:T(8,128)(2,1)} custom-call(s32[16]{0:T(128)S(1)} %dynamic-slice_bitcast_fusion.1.table, bf16[17,128,128]{2,1,0:T(8,128)(2,1)S(1)} %get-tuple-element.12.refs_0_, bf16[60,128,128]{2,1,0:T(8,128)(2,1)S(1)} %bitcast.11), custom_call_target="tpu_custom_call" | custom-call | tf_op jit(solution)/shard_map/pallas_call | solution.py:247
  106.2 1.5 %collective-permute-start.3 = (bf16[16,128,128]{2,1,0:T(8,128)(2,1)}, bf16[16,128,128]{2,1,0:T(8,128)(2,1)}, u32[]{:S(2)}, u32[]{:S(2)}) collective-permute-start(bf16[16,128,128]{2,1,0:T(8,128)(2,1)} %shard_map.47), channel_id=1, source_target_pairs={{0,4},{1,5},{2,6},{3,7},{124,120},{125,121},{126,122},{127,123},{1... | collective-permute-start | bytes 1572872 | tf_op jit(solution)/shard_map/ppermute | solution.py:248
  107.7 1.9 %collective-permute-start.5 = (bf16[3,128,128]{2,1,0:T(8,128)(2,1)S(1)}, bf16[3,128,128]{2,1,0:T(8,128)(2,1)S(1)}, u32[]{:S(2)}, u32[]{:S(2)}) collective-permute-start(bf16[3,128,128]{2,1,0:T(8,128)(2,1)S(1)} %get-tuple-element.16), channel_id=1, source_target_pairs={{2,502},{3,503},{8,24},{9,25},{22,6},{23,7},{24,40},{25,41},{38,22... | collective-permute-start | bytes 294920 | tf_op jit(solution)/shard_map/ppermute | solution.py:252
  109.6 0.8 dynamic-slice_reduce_fusion.spots
  110.4 18.2 %collective-permute-done.5.refs_7_ = bf16[3,128,128]{2,1,0:T(8,128)(2,1)S(1)} collective-permute-done((bf16[3,128,128]{2,1,0:T(8,128)(2,1)S(1)}, bf16[3,128,128]{2,1,0:T(8,128)(2,1)S(1)}, u32[]{:S(2)}, u32[]{:S(2)}) %collective-permute-start.5) | collective-permute-done | bytes 98336 | tf_op jit(solution)/shard_map/ppermute | solution.py:252
  128.6 1.1 copy-done.3
  129.7 12.5 %shard_map.49 = f32[1,128,2688]{2,1,0:T(8,128)} custom-call(s32[266]{0:T(512)S(1)} %dynamic-slice_reduce_fusion.spots, s32[1,21]{1,0:T(1,128)S(1)} %copy-done.5, bf16[128,2176]{1,0:T(8,128)(2,1)S(1)} %copy-done.3, bf16[17,128,128]{2,1,0:T(8,128)(2,1)S(1)} %get-tuple-element.12.refs_0_, bf16[60,128,128]{2,1,0:T(8,128)(2,1)} %bitcast.10, ...), custom_call_target="tpu_custom_call" | custom-call | tf_op jit(solution)/shard_map/pallas_call | solution.py:253
  (13 shorter events, 0.0 us)
Async XLA Ops:
  0.7 1.1 copy-start.4
  1.7 0.7 copy-start.6
  3.5 24.9 %copy-start.2 = (bf16[128,2176]{1,0:T(8,128)(2,1)}, bf16[128,2176]{1,0:T(8,128)(2,1)S(1)}, u32[]{:S(2)}) copy-start(bf16[128,2176]{1,0:T(8,128)(2,1)S(1)} %get-tuple-element.11.masked) | copy-start | bytes 1671172
  28.4 50.3 %copy-start = (bf16[4,15,128,128]{3,2,1,0:T(8,128)(2,1)}, bf16[4,15,128,128]{3,2,1,0:T(8,128)(2,1)S(1)}, u32[]{:S(2)}) copy-start(bf16[4,15,128,128]{3,2,1,0:T(8,128)(2,1)S(1)} %all_to_all.10) | copy-start | bytes 5898244
  28.4 50.3 %collective-permute-start = (bf16[60,128,128]{2,1,0:T(8,128)(2,1)S(1)}, bf16[60,128,128]{2,1,0:T(8,128)(2,1)}, u32[]{:S(2)}, u32[]{:S(2)}) collective-permute-start(bf16[60,128,128]{2,1,0:T(8,128)(2,1)S(1)} %bitcast.8), channel_id=1, source_target_pairs={{0,8},{1,9},{2,10},{3,11},{4,12},{5,13},{6,14},{7,15},{8,0},{9,1},... | collective-permute-start | bytes 5898248 | tf_op jit(solution)/shard_map/ppermute | solution.py:246
  35.9 21.4 %collective-permute-start.1 = (bf16[7,128,128]{2,1,0:T(8,128)(2,1)S(1)}, bf16[7,128,128]{2,1,0:T(8,128)(2,1)S(1)}, u32[]{:S(2)}, u32[]{:S(2)}) collective-permute-start(bf16[7,128,128]{2,1,0:T(8,128)(2,1)S(1)} %get-tuple-element.14), channel_id=1, source_target_pairs={{0,4},{1,5},{2,6},{3,7},{4,0},{5,1},{6,2},{7,3},{8,12},{9,13},{10,... | collective-permute-start | bytes 688136 | tf_op jit(solution)/shard_map/ppermute | solution.py:242
  72.8 5.9 %collective-permute-start.2 = (bf16[28,128,128]{2,1,0:T(8,128)(2,1)S(1)}, bf16[28,128,128]{2,1,0:T(8,128)(2,1)}, u32[]{:S(2)}, u32[]{:S(2)}) collective-permute-start(bf16[28,128,128]{2,1,0:T(8,128)(2,1)S(1)} %bitcast.12), channel_id=1, source_target_pairs={{0,8},{1,9},{2,10},{3,11},{4,12},{5,13},{6,14},{7,15},{8,0},{9,1},... | collective-permute-start | bytes 2752520 | tf_op jit(solution)/shard_map/ppermute | solution.py:249
  84.5 44.1 %copy-start.5 = (s32[1,21]{1,0:T(1,128)S(1)}, s32[1,21]{1,0:T(1,128)}, u32[]{:S(2)}) copy-start(s32[1,21]{1,0:T(1,128)} %keep.1) | copy-start | bytes 256
  84.5 44.1 %collective-permute-start.4 = (bf16[54,128,128]{2,1,0:T(8,128)(2,1)}, bf16[54,128,128]{2,1,0:T(8,128)(2,1)S(1)}, u32[]{:S(2)}, u32[]{:S(2)}) collective-permute-start(bf16[54,128,128]{2,1,0:T(8,128)(2,1)} %get-tuple-element.15), channel_id=1, source_target_pairs={{0,508},{1,509},{2,510},{3,511},{4,504},{5,505},{6,506},{7,507},{8... | collective-permute-start | bytes 5308424 | tf_op jit(solution)/shard_map/ppermute | solution.py:251
  103.0 1.5 %copy-start.1 = (bf16[4,15,128,128]{3,2,1,0:T(8,128)(2,1)S(1)}, bf16[4,15,128,128]{3,2,1,0:T(8,128)(2,1)}, u32[]{:S(2)}) copy-start(bf16[4,15,128,128]{3,2,1,0:T(8,128)(2,1)} %copy-done) | copy-start | bytes 5898244
  106.2 4.2 %collective-permute-start.3 = (bf16[16,128,128]{2,1,0:T(8,128)(2,1)}, bf16[16,128,128]{2,1,0:T(8,128)(2,1)}, u32[]{:S(2)}, u32[]{:S(2)}) collective-permute-start(bf16[16,128,128]{2,1,0:T(8,128)(2,1)} %shard_map.47), channel_id=1, source_target_pairs={{0,4},{1,5},{2,6},{3,7},{124,120},{125,121},{126,122},{127,123},{1... | collective-permute-start | bytes 1572872 | tf_op jit(solution)/shard_map/ppermute | solution.py:248
  107.7 20.9 %collective-permute-start.5 = (bf16[3,128,128]{2,1,0:T(8,128)(2,1)S(1)}, bf16[3,128,128]{2,1,0:T(8,128)(2,1)S(1)}, u32[]{:S(2)}, u32[]{:S(2)}) collective-permute-start(bf16[3,128,128]{2,1,0:T(8,128)(2,1)S(1)} %get-tuple-element.16), channel_id=1, source_target_pairs={{2,502},{3,503},{8,24},{9,25},{22,6},{23,7},{24,40},{25,41},{38,22... | collective-permute-start | bytes 294920 | tf_op jit(solution)/shard_map/ppermute | solution.py:252
  128.6 1.1 copy-start.3

commit v2 on v1

v2 whole, which is shorter than its diff:
```python
import functools

import jax
import jax.numpy as jnp
import numpy as np
from jax import lax
from jax.experimental import pallas as pl
from jax.experimental.pallas import tpu as pltpu
from jax.sharding import Mesh, PartitionSpec as P

BLK = 128
BAND_HALF = 8
KEEP_HALF = 10
KEPT = 21
AXES = ("y", "zl", "c", "zh", "x")
UPPER = BAND_HALF + 1
DUMMY = KEPT * UPPER


def canonical(row, offset, n):
    return (row % n, offset) if offset >= 0 else ((row + offset) % n, -offset)


def own_lists(core, half, p):
    if core == 0:
        same = list(range(-p, 1)) + list(range(-8, -4 - p))
        same += ({0: [8], 1: [7, 8], 2: [6, 7], 3: [5, 6]} if half == 0 else {0: [8], 1: [7, 8], 2: [], 3: []})[p]
    else:
        same = list(range(0, 4 - p)) + list(range(8 - p, 9))
        same += ({0: [], 1: [], 2: [-8, -7], 3: [-8]} if half == 0 else {0: [-6, -5], 1: [-7, -6], 2: [-8, -7], 3: [-8]})[p]
    mixed = list(range(-p - 4, -p)) + list(range(4 - p, 8 - p))
    return same, mixed


def make_plan(ny, nzl):
    n = ny * nzl * 16

    def place(y, zl, c, zh, x):
        return (((y % ny) * nzl + zl) * 2 + c) * 8 + zh * 4 + x % 4

    coords = [(y, zl, c, zh, x) for y in range(ny) for zl in range(nzl) for c in range(2) for zh in range(2) for x in range(4)]

    def ring(y, zl, zh, step):
        z = zh * nzl + zl
        y += 1 if (step == 1 and zl == nzl - 1) else -1 if (step == -1 and zl == 0) else 0
        z = (z + step) % (2 * nzl)
        return y, z % nzl, z // nzl

    def pad(blocks, k):
        return list(blocks) + [None] * (k - len(blocks))

    need = [{((i - KEEP_HALF + u) % n, o): u * UPPER + o for u in range(KEPT) for o in range(UPPER) if u + o < KEPT} for i in range(n)]
    lists = [own_lists(c, zh, x) for y, zl, c, zh, x in coords]
    k1 = max(len(same) for same, _ in lists)
    k2 = max(len(same + mixed) for same, mixed in lists)
    own = [[canonical(i, o, n) for o in range(-8, 9)] for i in range(n)]
    sent1 = [pad([canonical(i, o, n) for o in same], k1) for i, (same, _) in enumerate(lists)]
    sent2 = [pad([canonical(i, o, n) for o in same + mixed], k2) for i, (same, mixed) in enumerate(lists)]
    moves = {}
    moves["zh"] = [(i, place(y, zl, c, 1 - zh, x)) for i, (y, zl, c, zh, x) in enumerate(coords)]
    moves["c"] = [(i, place(y, zl, 1 - c, zh, x)) for i, (y, zl, c, zh, x) in enumerate(coords)]
    for step in (1, 2, 3):
        moves[f"x{step}"] = [(i, place(y, zl, c, zh, x + step)) for i, (y, zl, c, zh, x) in enumerate(coords)]
    moves["seam"], moves["z"], moves["far"] = [], [], []
    for i, (y, zl, c, zh, x) in enumerate(coords):
        if (zl, c, zh) in ((0, 0, 0), (nzl - 1, 1, 1)):
            moves["seam"].append((i, place(y, zl, c, 1 - zh, x)))
        y2, zl2, zh2 = ring(y, zl, zh, 1 if c else -1)
        moves["z"].append((i, place(y2, zl2, 1 - c, zh2, x)))
        for step in (1, -1):
            y2, zl2, zh2 = ring(y, zl, zh, step)
            if (zh2 == 0 and x < 2 and step == 1) or (zh2 == 1 and x >= 2 and step == -1):
                moves["far"].append((i, place(y2, zl2, c, zh2, x)))

    def moved(sends, name):
        got = [[None] * len(sends[0]) for _ in range(n)]
        for s, d in moves[name]:
            got[d] = sends[s]
        return got

    def join(*parts):
        return [sum(row, []) for row in zip(*parts)]

    got1 = moved(sent1, "zh")
    got2 = [moved(sent2, f"x{s}") for s in (1, 2, 3)]
    got3 = [moved(got1, f"x{s}") for s in (1, 2, 3)]
    stock2 = join(own, *got2)
    stock3 = join(stock2, got1, *got3)
    got_c = moved(join(sent2, *got2, got1, *got3), "c")
    known = [set(row) for row in join(stock3, got_c)]

    def choose(name, stock):
        sends = [[] for _ in range(n)]
        for s, d in moves[name]:
            sends[s] = [b for b in need[d] if b not in known[d] and b in set(stock[s])]
        k = max(map(len, sends))
        sends = [pad(q, k) for q in sends]
        got = moved(sends, name)
        for d in range(n):
            known[d] |= set(got[d])
        return sends, got

    sent_s, got_s = choose("seam", stock2)
    sent_a, got_a = choose("z", stock2)
    sent_b, got_b = choose("z", stock3)
    sent_f, got_f = choose("far", stock3)
    assert all(set(need[d]) <= known[d] for d in range(n))

    def where(sends, stock):
        return np.array([[src.index(b) if b is not None else 0 for b in q] for q, src in zip(sends, stock)], np.int32)

    arrived = join(stock3, got_c, got_s, got_a, got_b, got_f)
    spots = np.full((n, len(arrived[0])), DUMMY, np.int32)
    for i in range(n):
        seen = set()
        for k, b in enumerate(arrived[i]):
            if b in need[i] and b not in seen:
                seen.add(b)
                spots[i, k] = need[i][b]
    parts = [where(sent1, own), where(sent2, own), where(sent_s, stock2), where(sent_a, stock2), where(sent_b, stock3), where(sent_f, stock3), spots]
    starts = np.cumsum([0] + [q.shape[1] for q in parts])
    return moves, np.concatenate(parts, axis=1), [q.shape[1] for q in parts], [int(q) for q in starts]


def vmem(*shape, dtype=jnp.bfloat16):
    return jax.ShapeDtypeStruct(shape, dtype)


def whole():
    return pl.BlockSpec(memory_space=pltpu.VMEM)


def scalars():
    return pl.BlockSpec(memory_space=pltpu.SMEM)


def call(kernel, outs, n_scalar, n_vector, scratch=()):
    return pl.pallas_call(
        kernel,
        out_shape=outs,
        in_specs=[scalars()] * n_scalar + [whole()] * n_vector,
        out_specs=jax.tree.map(lambda _: whole(), outs),
        scratch_shapes=scratch,
        compiler_params=pltpu.CompilerParams(vmem_limit_bytes=48 << 20),
    )


def first_kernel(start, table, pattern, strip, masked, own, send1, send2):
    for slot in range(2 * BAND_HALF + 1):
        cols = slice(slot * BLK, (slot + 1) * BLK)
        block = strip[0, :, cols] * pattern[0, slot].astype(jnp.bfloat16)
        masked[:, cols] = block
        own[slot] = block if slot >= BAND_HALF else block.T
    gather(start, table, [own], [send1, send2])


def gather(start, table, sources, outs):
    for out in outs:

        def pack(k, carry, out=out, start=start):
            at = table[start + k]
            low = 0
            for source in sources:
                count = source.shape[0]

                @pl.when((at >= low) & (at < low + count))
                def _(source=source, low=low):
                    out[k] = source[at - low]

                low += count
            return carry

        lax.fori_loop(0, out.shape[0], pack, 0)
        start += out.shape[0]


def concatenate(sources, out):
    low = 0
    for source in sources:
        out[low : low + source.shape[0]] = source[...]
        low += source.shape[0]


def second_kernel(start, table, own, x1, x2, x3, seam, z):
    gather(start, table, [own, x1, x2, x3], [seam, z])


def third_kernel(start, table, own, send2, x1, x2, x3, got1, w1, w2, w3, z, far, both):
    gather(start, table, [own, x1, x2, x3, got1, w1, w2, w3], [z, far])
    concatenate([send2, x1, x2, x3, got1, w1, w2, w3], both)


def product(left, first, pool, v):
    last = KEPT - 1 - first
    total = None
    low, high = max(first, v - BAND_HALF), min(last, v)
    if low <= high:
        right = jnp.concatenate([pool[u * UPPER + v - u] for u in range(low, high + 1)], axis=0)
        total = jnp.dot(left[:, (low - first) * BLK : (high - first + 1) * BLK], right, preferred_element_type=jnp.float32)
    low, high = max(first, v + 1), min(last, v + BAND_HALF)
    if low <= high:
        right = jnp.concatenate([pool[v * UPPER + u - v] for u in range(low, high + 1)], axis=1)
        part = lax.dot_general(
            left[:, (low - first) * BLK : (high - first + 1) * BLK], right,
            (((1,), (1,)), ((), ())), preferred_element_type=jnp.float32)
        total = part if total is None else total + part
    return total


def final_kernel(start, spots, keep, masked, *refs):
    *sources, out, pool, square, rounded = refs
    low = start
    for source in sources:

        def place(k, carry, source=source, low=low):
            at = spots[low + k]

            @pl.when(at < DUMMY)
            def _():
                pool[at] = source[k]

            return carry

        lax.fori_loop(0, source.shape[0], place, 0)
        low += source.shape[0]
    for v in range(KEPT):
        cols = slice(v * BLK, (v + 1) * BLK)
        value = product(masked, KEEP_HALF - BAND_HALF, pool, v) * keep[0, v].astype(jnp.float32)
        square[:, cols] = value
        rounded[:, cols] = value.astype(jnp.bfloat16)
    for v in range(KEPT):
        cols = slice(v * BLK, (v + 1) * BLK)
        flag = keep[0, v].astype(jnp.float32)
        cube = flag * product(rounded, 0, pool, v)
        out[0, :, cols] = flag * (3.0 * square[:, cols] - 2.0 * cube)


def solution(mesh):
    ny, nzl = mesh.shape["row"], mesh.shape["col"] // 2
    moves, tables, counts, starts = make_plan(ny, nzl)
    k1, k2, ks, ka, kb, kf, _ = counts
    fine = Mesh(mesh.devices.reshape(ny, nzl, 2, 2, 4), AXES)

    def send(array, name):
        return lax.ppermute(array, AXES, moves[name])

    def body(density, pattern, keep):
        table = lax.dynamic_index_in_dim(jnp.asarray(tables), lax.axis_index(AXES), 0, keepdims=False)
        masked, own, send1, send2 = call(
            functools.partial(first_kernel, starts[0]),
            (vmem(BLK, 17 * BLK), vmem(17, BLK, BLK), vmem(k1, BLK, BLK), vmem(k2, BLK, BLK)), 2, 1,
        )(table, pattern, density)
        x = [send(send2, f"x{step}") for step in (1, 3, 2)]
        x = [x[0], x[2], x[1]]
        got1 = send(send1, "zh")
        *x, got1 = lax.optimization_barrier((*x, got1))
        w = [send(got1, f"x{step}") for step in (1, 3, 2)]
        w = [w[0], w[2], w[1]]
        send_s, send_a = call(
            functools.partial(second_kernel, starts[2]), (vmem(ks, BLK, BLK), vmem(ka, BLK, BLK)), 1, 4,
        )(table, own, *x)
        got_s, got_a = send(send_s, "seam"), send(send_a, "z")
        w1, w2, w3, got_s = lax.optimization_barrier((*w, got_s))
        send_b, send_f, both = call(
            functools.partial(third_kernel, starts[4]),
            (vmem(kb, BLK, BLK), vmem(kf, BLK, BLK), vmem(4 * (k1 + k2), BLK, BLK)), 1, 9,
        )(table, own, send2, *x, got1, w1, w2, w3)
        got_b, got_f, got_c = send(send_b, "z"), send(send_f, "far"), send(both, "c")
        return call(
            functools.partial(final_kernel, starts[6]), vmem(1, BLK, KEPT * BLK, dtype=jnp.float32), 2, 14,
            [
                pltpu.VMEM((DUMMY, BLK, BLK), jnp.bfloat16),
                pltpu.VMEM((BLK, KEPT * BLK), jnp.float32),
                pltpu.VMEM((BLK, KEPT * BLK), jnp.bfloat16),
            ],
        )(table, keep, masked, own, *x, got1, w1, w2, w3, got_c, got_s, got_a, got_b, got_f)

    return jax.shard_map(
        body,
        mesh=fine,
        in_specs=(P(AXES, None, None), P(AXES, None), P(AXES, None)),
        out_specs=P(AXES, None, None),
        check_vma=False,
    )
```

time: 143 us -> 127 us (0.89)
  blocking collectives: 40.1 us -> 0 us
  starting transfers between devices: 47.8 us -> 63.2 us
  waiting for transfers between devices: 25.6 us -> 39.9 us
  local copies, waits for them, and re-layouts: 7.55 us -> 4.01 us
  Pallas kernels: 21 us -> 18.8 us
    all_to_all x2 -> x0, blocking collectives: 40.1 us -> none  [the longest x1 24.9 us: body(): got2 = lax.all_to_all(send2, 'x', 0, 0).reshape(4 * k2, BLK, BLK)]
    ppermute x6 -> x12, starting transfers between devices: 47.8 us -> 63.2 us  [send(): return lax.ppermute(array, AXES, moves[name])]
    ppermute x6 -> x12, waiting for transfers between devices: 25.6 us -> 39.9 us  [send(): return lax.ppermute(array, AXES, moves[name])]
    split x4 -> x0, local copies, waits for them, and re-layouts: 3.03 us -> none  [body(): t_first, t_seam, t_z, t_spots = jnp.split(mine, cuts)]
    pallas_call x4, Pallas kernels: 21 us -> 18.8 us  [the longest x1 11.7 us: body(): call(functools.partial(final_kernel, starts[6]), vmem(1, BLK, KEPT * BLK,...]
    unnamed x14 -> x8, local copies, waits for them, and re-layouts: 4.32 us -> 3.28 us
  transfers between devices with their start and end apart: 6 -> 12, of which waited for: 3 -> 5; matrix products, arithmetic and copies ran while one was open for 2% -> 0% of each run, Pallas kernels for 1% -> 0%
where the time goes in v2:
time: 127 us; the launch traced here: 126 us
  starting transfers between devices  63.2 us (50%)
  waiting for transfers between devices  39.9 us (31%)
  Pallas kernels  18.8 us (15%)
  local copies, waits for them, and re-layouts  4.01 us (3%)
    ppermute x12, starting transfers between devices, send(): return lax.ppermute(array, AXES, moves[name])  63.2 us
    ppermute x12, waiting for transfers between devices, send(): return lax.ppermute(array, AXES, moves[name])  39.9 us
    pallas_call x1, Pallas kernels, body(): call(functools.partial(final_kernel, starts[6]), vmem(1, BLK, KEPT * BLK,...  11.7 us
    pallas_call x1, Pallas kernels, body(): call(functools.partial(third_kernel, starts[4]), (vmem(kb, BLK, BLK), vme...  3.88 us
    unnamed x8, local copies, waits for them, and re-layouts  3.28 us
  transfers between devices with their start and end apart: 12, of which 5 were waited for; matrix products, arithmetic and copies ran while one was open for 0% of the time, Pallas kernels for 0%

profile of v2, /device:TPU:1, one launch (start us, length us, event | category | flops | bytes accessed | tf_op | source)
XLA Modules:
  0.0 126.2 jit_solution(12364556018033564286)
XLA Ops:
  0.0 0.7 dynamic-slice_reduce_fusion.table.spots
  0.7 1.0 copy-done
  2.4 1.0 shard_map.46
  3.5 5.2 %collective-permute-start.2 = (bf16[15,128,128]{2,1,0:T(8,128)(2,1)S(1)}, bf16[15,128,128]{2,1,0:T(8,128)(2,1)S(1)}, u32[]{:S(2)}, u32[]{:S(2)}) collective-permute-start(bf16[15,128,128]{2,1,0:T(8,128)(2,1)S(1)} %get-tuple-element.24.send2), channel_id=1, source_target_pairs={{0,3},{1,0},{2,1},{3,2},{4,7},{5,4},{6,5},{7,6},{8,11},{9,8},{10,9... | collective-permute-start | bytes 1474568 | tf_op jit(solution)/shard_map/ppermute | solution.py:245
  8.7 2.4 %collective-permute-start.1 = (bf16[15,128,128]{2,1,0:T(8,128)(2,1)S(1)}, bf16[15,128,128]{2,1,0:T(8,128)(2,1)S(1)}, u32[]{:S(2)}, u32[]{:S(2)}) collective-permute-start(bf16[15,128,128]{2,1,0:T(8,128)(2,1)S(1)} %get-tuple-element.24.send2), channel_id=1, source_target_pairs={{0,2},{1,3},{2,0},{3,1},{4,6},{5,7},{6,4},{7,5},{8,10},{9,11},{10,... | collective-permute-start | bytes 1474568 | tf_op jit(solution)/shard_map/ppermute | solution.py:245
  11.2 2.5 %collective-permute-start = (bf16[15,128,128]{2,1,0:T(8,128)(2,1)S(1)}, bf16[15,128,128]{2,1,0:T(8,128)(2,1)S(1)}, u32[]{:S(2)}, u32[]{:S(2)}) collective-permute-start(bf16[15,128,128]{2,1,0:T(8,128)(2,1)S(1)} %get-tuple-element.24.send2), channel_id=1, source_target_pairs={{0,1},{1,2},{2,3},{3,0},{4,5},{5,6},{6,7},{7,4},{8,9},{9,10},{10,1... | collective-permute-start | bytes 1474568 | tf_op jit(solution)/shard_map/ppermute | solution.py:245
  13.7 15.4 %collective-permute-start.3 = (bf16[7,128,128]{2,1,0:T(8,128)(2,1)S(1)}, bf16[7,128,128]{2,1,0:T(8,128)(2,1)S(1)}, u32[]{:S(2)}, u32[]{:S(2)}) collective-permute-start(bf16[7,128,128]{2,1,0:T(8,128)(2,1)S(1)} %get-tuple-element.25), channel_id=1, source_target_pairs={{0,4},{1,5},{2,6},{3,7},{4,0},{5,1},{6,2},{7,3},{8,12},{9,13},{10,... | collective-permute-start | bytes 688136 | tf_op jit(solution)/shard_map/ppermute | solution.py:245
  29.1 4.4 %collective-permute-done.3.got1.refs_4_ = bf16[7,128,128]{2,1,0:T(8,128)(2,1)S(1)} collective-permute-done((bf16[7,128,128]{2,1,0:T(8,128)(2,1)S(1)}, bf16[7,128,128]{2,1,0:T(8,128)(2,1)S(1)}, u32[]{:S(2)}, u32[]{:S(2)}) %collective-permute-start.3) | collective-permute-done | bytes 229408 | tf_op jit(solution)/shard_map/ppermute | solution.py:245
  33.5 1.9 %collective-permute-done.x1.refs_1_ = bf16[15,128,128]{2,1,0:T(8,128)(2,1)S(1)} collective-permute-done((bf16[15,128,128]{2,1,0:T(8,128)(2,1)S(1)}, bf16[15,128,128]{2,1,0:T(8,128)(2,1)S(1)}, u32[]{:S(2)}, u32[]{:S(2)}) %collective-permute-start) | collective-permute-done | bytes 491552 | tf_op jit(solution)/shard_map/ppermute | solution.py:245
  35.5 2.2 %shard_map.47 = (bf16[16,128,128]{2,1,0:T(8,128)(2,1)S(1)}, bf16[34,128,128]{2,1,0:T(8,128)(2,1)S(1)}) custom-call(s32[356]{0:T(512)S(1)} %dynamic-slice_reduce_fusion.table.spots, bf16[17,128,128]{2,1,0:T(8,128)(2,1)S(1)} %get-tuple-element.23.own.refs_0_, bf16[15,128,128]{2,1,0:T(8,128)(2,1)S(1)} %collective-permute-done.x1.refs_1_, ...), custom_call_target="tpu_custom_call" | custom-call | tf_op jit(solution)/shard_map/pallas_call | solution.py:259
  37.7 0.7 collective-permute-start.7
  38.4 1.9 %collective-permute-start.6 = (bf16[7,128,128]{2,1,0:T(8,128)(2,1)S(1)}, bf16[7,128,128]{2,1,0:T(8,128)(2,1)S(1)}, u32[]{:S(2)}, u32[]{:S(2)}) collective-permute-start(bf16[7,128,128]{2,1,0:T(8,128)(2,1)S(1)} %collective-permute-done.3.got1.refs_4_), channel_id=1, source_target_pairs={{0,3},{1,0},{2,1},{3,2},{4,7},{5,4},{6,5},{7,6},{8,11},{9,8},{10,9... | collective-permute-start | bytes 688136 | tf_op jit(solution)/shard_map/ppermute | solution.py:245
  40.3 3.3 %collective-permute-start.5 = (bf16[7,128,128]{2,1,0:T(8,128)(2,1)S(1)}, bf16[7,128,128]{2,1,0:T(8,128)(2,1)S(1)}, u32[]{:S(2)}, u32[]{:S(2)}) collective-permute-start(bf16[7,128,128]{2,1,0:T(8,128)(2,1)S(1)} %collective-permute-done.3.got1.refs_4_), channel_id=1, source_target_pairs={{0,2},{1,3},{2,0},{3,1},{4,6},{5,7},{6,4},{7,5},{8,10},{9,11},{10,... | collective-permute-start | bytes 688136 | tf_op jit(solution)/shard_map/ppermute | solution.py:245
  43.6 2.2 %collective-permute-start.4 = (bf16[7,128,128]{2,1,0:T(8,128)(2,1)S(1)}, bf16[7,128,128]{2,1,0:T(8,128)(2,1)S(1)}, u32[]{:S(2)}, u32[]{:S(2)}) collective-permute-start(bf16[7,128,128]{2,1,0:T(8,128)(2,1)S(1)} %collective-permute-done.3.got1.refs_4_), channel_id=1, source_target_pairs={{0,1},{1,2},{2,3},{3,0},{4,5},{5,6},{6,7},{7,4},{8,9},{9,10},{10,1... | collective-permute-start | bytes 688136 | tf_op jit(solution)/shard_map/ppermute | solution.py:245
  45.8 2.7 %collective-permute-done.5.w2.refs_6_ = bf16[7,128,128]{2,1,0:T(8,128)(2,1)S(1)} collective-permute-done((bf16[7,128,128]{2,1,0:T(8,128)(2,1)S(1)}, bf16[7,128,128]{2,1,0:T(8,128)(2,1)S(1)}, u32[]{:S(2)}, u32[]{:S(2)}) %collective-permute-start.5) | collective-permute-done | bytes 229408 | tf_op jit(solution)/shard_map/ppermute | solution.py:245
  48.6 3.0 %collective-permute-done.4.w1.refs_5_ = bf16[7,128,128]{2,1,0:T(8,128)(2,1)S(1)} collective-permute-done((bf16[7,128,128]{2,1,0:T(8,128)(2,1)S(1)}, bf16[7,128,128]{2,1,0:T(8,128)(2,1)S(1)}, u32[]{:S(2)}, u32[]{:S(2)}) %collective-permute-start.4) | collective-permute-done | bytes 229408 | tf_op jit(solution)/shard_map/ppermute | solution.py:245
  51.5 3.9 %shard_map.48 = (bf16[17,128,128]{2,1,0:T(8,128)(2,1)S(1)}, bf16[11,128,128]{2,1,0:T(8,128)(2,1)S(1)}, bf16[88,128,128]{2,1,0:T(8,128)(2,1)}) custom-call(s32[356]{0:T(512)S(1)} %dynamic-slice_reduce_fusion.table.spots, bf16[17,128,128]{2,1,0:T(8,128)(2,1)S(1)} %get-tuple-element.23.own.refs_0_, bf16[15,128,128]{2,1,0:T(8,128)(2,1)S(1)} %get-tuple-element.24.send2, ...), custom_call_target="tpu_custom_call" | custom-call | tf_op jit(solution)/shard_map/pallas_call | solution.py:264
  55.4 19.0 %collective-permute-start.8 = (bf16[88,128,128]{2,1,0:T(8,128)(2,1)}, bf16[88,128,128]{2,1,0:T(8,128)(2,1)S(1)}, u32[]{:S(2)}, u32[]{:S(2)}) collective-permute-start(bf16[88,128,128]{2,1,0:T(8,128)(2,1)} %get-tuple-element.34), channel_id=1, source_target_pairs={{0,8},{1,9},{2,10},{3,11},{4,12},{5,13},{6,14},{7,15},{8,0},{9,1},... | collective-permute-start | bytes 8650760 | tf_op jit(solution)/shard_map/ppermute | solution.py:245
  74.5 4.8 %collective-permute-start.9 = (bf16[34,128,128]{2,1,0:T(8,128)(2,1)S(1)}, bf16[34,128,128]{2,1,0:T(8,128)(2,1)S(1)}, u32[]{:S(2)}, u32[]{:S(2)}) collective-permute-start(bf16[34,128,128]{2,1,0:T(8,128)(2,1)S(1)} %get-tuple-element.36), channel_id=1, source_target_pairs={{0,508},{1,509},{2,510},{3,511},{4,504},{5,505},{6,506},{7,507},{8... | collective-permute-start | bytes 3342344 | tf_op jit(solution)/shard_map/ppermute | solution.py:245
  79.3 1.9 %collective-permute-start.10 = (bf16[17,128,128]{2,1,0:T(8,128)(2,1)S(1)}, bf16[17,128,128]{2,1,0:T(8,128)(2,1)S(1)}, u32[]{:S(2)}, u32[]{:S(2)}) collective-permute-start(bf16[17,128,128]{2,1,0:T(8,128)(2,1)S(1)} %get-tuple-element.37), channel_id=1, source_target_pairs={{0,508},{1,509},{2,510},{3,511},{4,504},{5,505},{6,506},{7,507},{8... | collective-permute-start | bytes 1671176 | tf_op jit(solution)/shard_map/ppermute | solution.py:245
  81.2 3.7 %collective-permute-start.11 = (bf16[11,128,128]{2,1,0:T(8,128)(2,1)S(1)}, bf16[11,128,128]{2,1,0:T(8,128)(2,1)S(1)}, u32[]{:S(2)}, u32[]{:S(2)}) collective-permute-start(bf16[11,128,128]{2,1,0:T(8,128)(2,1)S(1)} %get-tuple-element.38), channel_id=1, source_target_pairs={{0,16},{1,17},{2,502},{3,503},{8,24},{9,25},{10,510},{11,511},{16,... | collective-permute-start | bytes 1081352 | tf_op jit(solution)/shard_map/ppermute | solution.py:245
  85.0 27.9 %collective-permute-done.11.refs_12_ = bf16[11,128,128]{2,1,0:T(8,128)(2,1)S(1)} collective-permute-done((bf16[11,128,128]{2,1,0:T(8,128)(2,1)S(1)}, bf16[11,128,128]{2,1,0:T(8,128)(2,1)S(1)}, u32[]{:S(2)}, u32[]{:S(2)}) %collective-permute-start.11) | collective-permute-done | bytes 360480 | tf_op jit(solution)/shard_map/ppermute | solution.py:245
  112.9 1.6 %copy-done.3 = bf16[88,128,128]{2,1,0:T(8,128)(2,1)} copy-done((bf16[88,128,128]{2,1,0:T(8,128)(2,1)}, bf16[88,128,128]{2,1,0:T(8,128)(2,1)S(1)}, u32[]{:S(2)}) %copy-start.3) | copy-done | bytes 2883608
  114.4 11.7 %shard_map.49 = f32[1,128,2688]{2,1,0:T(8,128)} custom-call(s32[356]{0:T(512)S(1)} %dynamic-slice_reduce_fusion.table.spots, s32[1,21]{1,0:T(1,128)S(1)} %copy-done.2, bf16[128,2176]{1,0:T(8,128)(2,1)S(1)} %get-tuple-element.22.masked, bf16[17,128,128]{2,1,0:T(8,128)(2,1)S(1)} %get-tuple-element.23.own.refs_0_, ...), custom_call_target="tpu_custom_call" | custom-call | tf_op jit(solution)/shard_map/pallas_call | solution.py:269
  (13 shorter events, 0.7 us)
Async XLA Ops:
  0.7 1.1 copy-start
  1.8 0.7 copy-start.1
  3.5 30.0 %collective-permute-start.2 = (bf16[15,128,128]{2,1,0:T(8,128)(2,1)S(1)}, bf16[15,128,128]{2,1,0:T(8,128)(2,1)S(1)}, u32[]{:S(2)}, u32[]{:S(2)}) collective-permute-start(bf16[15,128,128]{2,1,0:T(8,128)(2,1)S(1)} %get-tuple-element.24.send2), channel_id=1, source_target_pairs={{0,3},{1,0},{2,1},{3,2},{4,7},{5,4},{6,5},{7,6},{8,11},{9,8},{10,9... | collective-permute-start | bytes 1474568 | tf_op jit(solution)/shard_map/ppermute | solution.py:245
  8.7 24.8 %collective-permute-start.1 = (bf16[15,128,128]{2,1,0:T(8,128)(2,1)S(1)}, bf16[15,128,128]{2,1,0:T(8,128)(2,1)S(1)}, u32[]{:S(2)}, u32[]{:S(2)}) collective-permute-start(bf16[15,128,128]{2,1,0:T(8,128)(2,1)S(1)} %get-tuple-element.24.send2), channel_id=1, source_target_pairs={{0,2},{1,3},{2,0},{3,1},{4,6},{5,7},{6,4},{7,5},{8,10},{9,11},{10,... | collective-permute-start | bytes 1474568 | tf_op jit(solution)/shard_map/ppermute | solution.py:245
  11.2 24.3 %collective-permute-start = (bf16[15,128,128]{2,1,0:T(8,128)(2,1)S(1)}, bf16[15,128,128]{2,1,0:T(8,128)(2,1)S(1)}, u32[]{:S(2)}, u32[]{:S(2)}) collective-permute-start(bf16[15,128,128]{2,1,0:T(8,128)(2,1)S(1)} %get-tuple-element.24.send2), channel_id=1, source_target_pairs={{0,1},{1,2},{2,3},{3,0},{4,5},{5,6},{6,7},{7,4},{8,9},{9,10},{10,1... | collective-permute-start | bytes 1474568 | tf_op jit(solution)/shard_map/ppermute | solution.py:245
  13.7 19.8 %collective-permute-start.3 = (bf16[7,128,128]{2,1,0:T(8,128)(2,1)S(1)}, bf16[7,128,128]{2,1,0:T(8,128)(2,1)S(1)}, u32[]{:S(2)}, u32[]{:S(2)}) collective-permute-start(bf16[7,128,128]{2,1,0:T(8,128)(2,1)S(1)} %get-tuple-element.25), channel_id=1, source_target_pairs={{0,4},{1,5},{2,6},{3,7},{4,0},{5,1},{6,2},{7,3},{8,12},{9,13},{10,... | collective-permute-start | bytes 688136 | tf_op jit(solution)/shard_map/ppermute | solution.py:245
  37.6 76.8 %copy-start.2 = (s32[1,21]{1,0:T(1,128)S(1)}, s32[1,21]{1,0:T(1,128)}, u32[]{:S(2)}) copy-start(s32[1,21]{1,0:T(1,128)} %keep.1) | copy-start | bytes 256
  37.7 13.9 %collective-permute-start.7 = (bf16[16,128,128]{2,1,0:T(8,128)(2,1)S(1)}, bf16[16,128,128]{2,1,0:T(8,128)(2,1)S(1)}, u32[]{:S(2)}, u32[]{:S(2)}) collective-permute-start(bf16[16,128,128]{2,1,0:T(8,128)(2,1)S(1)} %get-tuple-element.30), channel_id=1, source_target_pairs={{0,4},{1,5},{2,6},{3,7},{124,120},{125,121},{126,122},{127,123},{1... | collective-permute-start | bytes 1572872 | tf_op jit(solution)/shard_map/ppermute | solution.py:245
  38.4 7.5 %collective-permute-start.6 = (bf16[7,128,128]{2,1,0:T(8,128)(2,1)S(1)}, bf16[7,128,128]{2,1,0:T(8,128)(2,1)S(1)}, u32[]{:S(2)}, u32[]{:S(2)}) collective-permute-start(bf16[7,128,128]{2,1,0:T(8,128)(2,1)S(1)} %collective-permute-done.3.got1.refs_4_), channel_id=1, source_target_pairs={{0,3},{1,0},{2,1},{3,2},{4,7},{5,4},{6,5},{7,6},{8,11},{9,8},{10,9... | collective-permute-start | bytes 688136 | tf_op jit(solution)/shard_map/ppermute | solution.py:245
  40.3 8.3 %collective-permute-start.5 = (bf16[7,128,128]{2,1,0:T(8,128)(2,1)S(1)}, bf16[7,128,128]{2,1,0:T(8,128)(2,1)S(1)}, u32[]{:S(2)}, u32[]{:S(2)}) collective-permute-start(bf16[7,128,128]{2,1,0:T(8,128)(2,1)S(1)} %collective-permute-done.3.got1.refs_4_), channel_id=1, source_target_pairs={{0,2},{1,3},{2,0},{3,1},{4,6},{5,7},{6,4},{7,5},{8,10},{9,11},{10,... | collective-permute-start | bytes 688136 | tf_op jit(solution)/shard_map/ppermute | solution.py:245
  43.6 8.0 %collective-permute-start.4 = (bf16[7,128,128]{2,1,0:T(8,128)(2,1)S(1)}, bf16[7,128,128]{2,1,0:T(8,128)(2,1)S(1)}, u32[]{:S(2)}, u32[]{:S(2)}) collective-permute-start(bf16[7,128,128]{2,1,0:T(8,128)(2,1)S(1)} %collective-permute-done.3.got1.refs_4_), channel_id=1, source_target_pairs={{0,1},{1,2},{2,3},{3,0},{4,5},{5,6},{6,7},{7,4},{8,9},{9,10},{10,1... | collective-permute-start | bytes 688136 | tf_op jit(solution)/shard_map/ppermute | solution.py:245
  55.4 57.4 %collective-permute-start.8 = (bf16[88,128,128]{2,1,0:T(8,128)(2,1)}, bf16[88,128,128]{2,1,0:T(8,128)(2,1)S(1)}, u32[]{:S(2)}, u32[]{:S(2)}) collective-permute-start(bf16[88,128,128]{2,1,0:T(8,128)(2,1)} %get-tuple-element.34), channel_id=1, source_target_pairs={{0,8},{1,9},{2,10},{3,11},{4,12},{5,13},{6,14},{7,15},{8,0},{9,1},... | collective-permute-start | bytes 8650760 | tf_op jit(solution)/shard_map/ppermute | solution.py:245
  74.5 38.4 %collective-permute-start.9 = (bf16[34,128,128]{2,1,0:T(8,128)(2,1)S(1)}, bf16[34,128,128]{2,1,0:T(8,128)(2,1)S(1)}, u32[]{:S(2)}, u32[]{:S(2)}) collective-permute-start(bf16[34,128,128]{2,1,0:T(8,128)(2,1)S(1)} %get-tuple-element.36), channel_id=1, source_target_pairs={{0,508},{1,509},{2,510},{3,511},{4,504},{5,505},{6,506},{7,507},{8... | collective-permute-start | bytes 3342344 | tf_op jit(solution)/shard_map/ppermute | solution.py:245
  79.3 33.6 %collective-permute-start.10 = (bf16[17,128,128]{2,1,0:T(8,128)(2,1)S(1)}, bf16[17,128,128]{2,1,0:T(8,128)(2,1)S(1)}, u32[]{:S(2)}, u32[]{:S(2)}) collective-permute-start(bf16[17,128,128]{2,1,0:T(8,128)(2,1)S(1)} %get-tuple-element.37), channel_id=1, source_target_pairs={{0,508},{1,509},{2,510},{3,511},{4,504},{5,505},{6,506},{7,507},{8... | collective-permute-start | bytes 1671176 | tf_op jit(solution)/shard_map/ppermute | solution.py:245
  81.2 31.6 %collective-permute-start.11 = (bf16[11,128,128]{2,1,0:T(8,128)(2,1)S(1)}, bf16[11,128,128]{2,1,0:T(8,128)(2,1)S(1)}, u32[]{:S(2)}, u32[]{:S(2)}) collective-permute-start(bf16[11,128,128]{2,1,0:T(8,128)(2,1)S(1)} %get-tuple-element.38), channel_id=1, source_target_pairs={{0,16},{1,17},{2,502},{3,503},{8,24},{9,25},{10,510},{11,511},{16,... | collective-permute-start | bytes 1081352 | tf_op jit(solution)/shard_map/ppermute | solution.py:245
  112.8 1.6 %copy-start.3 = (bf16[88,128,128]{2,1,0:T(8,128)(2,1)}, bf16[88,128,128]{2,1,0:T(8,128)(2,1)S(1)}, u32[]{:S(2)}) copy-start(bf16[88,128,128]{2,1,0:T(8,128)(2,1)S(1)} %collective-permute-done.8.refs_8_) | copy-start | bytes 8650756

commit v3 on v2

--- a/solution.py
+++ b/solution.py
@@ -21,15 +21,12 @@
     return (row % n, offset) if offset >= 0 else ((row + offset) % n, -offset)
 
 
-def own_lists(core, half, p):
-    if core == 0:
+def own_lists(lower, p):
+    if lower:
         same = list(range(-p, 1)) + list(range(-8, -4 - p))
-        same += ({0: [8], 1: [7, 8], 2: [6, 7], 3: [5, 6]} if half == 0 else {0: [8], 1: [7, 8], 2: [], 3: []})[p]
     else:
         same = list(range(0, 4 - p)) + list(range(8 - p, 9))
-        same += ({0: [], 1: [], 2: [-8, -7], 3: [-8]} if half == 0 else {0: [-6, -5], 1: [-7, -6], 2: [-8, -7], 3: [-8]})[p]
-    mixed = list(range(-p - 4, -p)) + list(range(4 - p, 8 - p))
-    return same, mixed
+    return same, list(range(-p - 4, -p)) + list(range(4 - p, 8 - p))
 
 
 def make_plan(ny, nzl):
@@ -50,12 +47,11 @@
         return list(blocks) + [None] * (k - len(blocks))
 
     need = [{((i - KEEP_HALF + u) % n, o): u * UPPER + o for u in range(KEPT) for o in range(UPPER) if u + o < KEPT} for i in range(n)]
-    lists = [own_lists(c, zh, x) for y, zl, c, zh, x in coords]
-    k1 = max(len(same) for same, _ in lists)
-    k2 = max(len(same + mixed) for same, mixed in lists)
+    lists = [own_lists(zh == 0, x) for y, zl, c, zh, x in coords]
+    over = [own_lists(zh == 1, x)[0] for y, zl, c, zh, x in coords]
     own = [[canonical(i, o, n) for o in range(-8, 9)] for i in range(n)]
-    sent1 = [pad([canonical(i, o, n) for o in same], k1) for i, (same, _) in enumerate(lists)]
-    sent2 = [pad([canonical(i, o, n) for o in same + mixed], k2) for i, (same, mixed) in enumerate(lists)]
+    sent1 = [[canonical(i, o, n) for o in same] for i, same in enumerate(over)]
+    sent2 = [[canonical(i, o, n) for o in same + mixed] for i, (same, mixed) in enumerate(lists)]
     moves = {}
     moves["zh"] = [(i, place(y, zl, c, 1 - zh, x)) for i, (y, zl, c, zh, x) in enumerate(coords)]
     moves["c"] = [(i, place(y, zl, 1 - c, zh, x)) for i, (y, zl, c, zh, x) in enumerate(coords)]
@@ -103,13 +99,14 @@
     sent_s, got_s = choose("seam", stock2)
     sent_a, got_a = choose("z", stock2)
     sent_b, got_b = choose("z", stock3)
+    sent_t, got_t = choose("seam", stock3)
     sent_f, got_f = choose("far", stock3)
     assert all(set(need[d]) <= known[d] for d in range(n))
 
     def where(sends, stock):
         return np.array([[src.index(b) if b is not None else 0 for b in q] for q, src in zip(sends, stock)], np.int32)
 
-    arrived = join(stock3, got_c, got_s, got_a, got_b, got_f)
+    arrived = join(stock3, got_c, got_s, got_a, got_b, got_t, got_f)
     spots = np.full((n, len(arrived[0])), DUMMY, np.int32)
     for i in range(n):
         seen = set()
@@ -117,7 +114,7 @@
             if b in need[i] and b not in seen:
                 seen.add(b)
                 spots[i, k] = need[i][b]
-    parts = [where(sent1, own), where(sent2, own), where(sent_s, stock2), where(sent_a, stock2), where(sent_b, stock3), where(sent_f, stock3), spots]
+    parts = [where(sent1, own), where(sent2, own), where(sent_s, stock2), where(sent_a, stock2), where(sent_b, stock3), where(sent_t, stock3), where(sent_f, stock3), spots]
     starts = np.cumsum([0] + [q.shape[1] for q in parts])
     return moves, np.concatenate(parts, axis=1), [q.shape[1] for q in parts], [int(q) for q in starts]
 
@@ -134,14 +131,14 @@
     return pl.BlockSpec(memory_space=pltpu.SMEM)
 
 
-def call(kernel, outs, n_scalar, n_vector, scratch=()):
+def call(kernel, outs, n_scalar, n_vector, scratch=(), mib=8):
     return pl.pallas_call(
         kernel,
         out_shape=outs,
         in_specs=[scalars()] * n_scalar + [whole()] * n_vector,
         out_specs=jax.tree.map(lambda _: whole(), outs),
         scratch_shapes=scratch,
-        compiler_params=pltpu.CompilerParams(vmem_limit_bytes=48 << 20),
+        compiler_params=pltpu.CompilerParams(vmem_limit_bytes=mib << 20),
     )
 
 
@@ -185,26 +182,41 @@
     gather(start, table, [own, x1, x2, x3], [seam, z])
 
 
-def third_kernel(start, table, own, send2, x1, x2, x3, got1, w1, w2, w3, z, far, both):
-    gather(start, table, [own, x1, x2, x3, got1, w1, w2, w3], [z, far])
+def third_kernel(start, table, own, send2, x1, x2, x3, got1, w1, w2, w3, z, seam, far, both):
+    gather(start, table, [own, x1, x2, x3, got1, w1, w2, w3], [z, seam, far])
     concatenate([send2, x1, x2, x3, got1, w1, w2, w3], both)
 
 
-def product(left, first, pool, v):
+def product(left, first, pool, v, width):
     last = KEPT - 1 - first
+    blank = jnp.zeros((BLK, BLK), jnp.bfloat16)
     total = None
-    low, high = max(first, v - BAND_HALF), min(last, v)
-    if low <= high:
-        right = jnp.concatenate([pool[u * UPPER + v - u] for u in range(low, high + 1)], axis=0)
-        total = jnp.dot(left[:, (low - first) * BLK : (high - first + 1) * BLK], right, preferred_element_type=jnp.float32)
-    low, high = max(first, v + 1), min(last, v + BAND_HALF)
-    if low <= high:
-        right = jnp.concatenate([pool[v * UPPER + u - v] for u in range(low, high + 1)], axis=1)
+    for upper in (True, False):
+
+        def block(u, col):
+            row, offset = (u, col - u) if upper else (col, u - col)
+            return pool[row * UPPER + offset] if (0 if upper else 1) <= offset <= BAND_HALF else blank
+
+        low, high = (v - BAND_HALF, v + width - 1) if upper else (v + 1, v + width - 1 + BAND_HALF)
+        low, high = max(first, low), min(last, high)
+        if low > high:
+            continue
+        across = [
+            jnp.concatenate([block(u, col) for u in range(low, high + 1)], axis=0 if upper else 1)
+            for col in range(v, v + width)
+        ]
         part = lax.dot_general(
-            left[:, (low - first) * BLK : (high - first + 1) * BLK], right,
-            (((1,), (1,)), ((), ())), preferred_element_type=jnp.float32)
+            left[:, (low - first) * BLK : (high - first + 1) * BLK],
+            jnp.concatenate(across, axis=1 if upper else 0),
+            (((1,), (0 if upper else 1,)), ((), ())),
+            preferred_element_type=jnp.float32,
+        )
         total = part if total is None else total + part
     return total
+
+
+def flags(keep, v, width):
+    return jnp.concatenate([jnp.full((1, BLK), keep[0, v + j].astype(jnp.float32)) for j in range(width)], axis=1)
 
 
 def final_kernel(start, spots, keep, masked, *refs):
@@ -223,22 +235,23 @@
 
         lax.fori_loop(0, source.shape[0], place, 0)
         low += source.shape[0]
-    for v in range(KEPT):
-        cols = slice(v * BLK, (v + 1) * BLK)
-        value = product(masked, KEEP_HALF - BAND_HALF, pool, v) * keep[0, v].astype(jnp.float32)
+    groups = [(v, min(2, KEPT - v)) for v in range(0, KEPT, 2)]
+    for v, width in groups:
+        cols = slice(v * BLK, (v + width) * BLK)
+        value = product(masked, KEEP_HALF - BAND_HALF, pool, v, width) * flags(keep, v, width)
         square[:, cols] = value
         rounded[:, cols] = value.astype(jnp.bfloat16)
-    for v in range(KEPT):
-        cols = slice(v * BLK, (v + 1) * BLK)
-        flag = keep[0, v].astype(jnp.float32)
-        cube = flag * product(rounded, 0, pool, v)
+    for v, width in groups:
+        cols = slice(v * BLK, (v + width) * BLK)
+        flag = flags(keep, v, width)
+        cube = flag * product(rounded, 0, pool, v, width)
         out[0, :, cols] = flag * (3.0 * square[:, cols] - 2.0 * cube)
 
 
 def solution(mesh):
     ny, nzl = mesh.shape["row"], mesh.shape["col"] // 2
     moves, tables, counts, starts = make_plan(ny, nzl)
-    k1, k2, ks, ka, kb, kf, _ = counts
+    k1, k2, ks, ka, kb, kt, kf, _ = counts
     fine = Mesh(mesh.devices.reshape(ny, nzl, 2, 2, 4), AXES)
 
     def send(array, name):
@@ -260,20 +273,20 @@
             functools.partial(second_kernel, starts[2]), (vmem(ks, BLK, BLK), vmem(ka, BLK, BLK)), 1, 4,
         )(table, own, *x)
         got_s, got_a = send(send_s, "seam"), send(send_a, "z")
-        w1, w2, w3, got_s = lax.optimization_barrier((*w, got_s))
-        send_b, send_f, both = call(
+        w1, w2, w3, got_s, got_a = lax.optimization_barrier((*w, got_s, got_a))
+        send_b, send_t, send_f, both = call(
             functools.partial(third_kernel, starts[4]),
-            (vmem(kb, BLK, BLK), vmem(kf, BLK, BLK), vmem(4 * (k1 + k2), BLK, BLK)), 1, 9,
+            (vmem(kb, BLK, BLK), vmem(kt, BLK, BLK), vmem(kf, BLK, BLK), vmem(4 * (k1 + k2), BLK, BLK)), 1, 9,
         )(table, own, send2, *x, got1, w1, w2, w3)
-        got_b, got_f, got_c = send(send_b, "z"), send(send_f, "far"), send(both, "c")
+        got_b, got_t, got_f, got_c = send(send_b, "z"), send(send_t, "seam"), send(send_f, "far"), send(both, "c")
         return call(
-            functools.partial(final_kernel, starts[6]), vmem(1, BLK, KEPT * BLK, dtype=jnp.float32), 2, 14,
+            functools.partial(final_kernel, starts[7]), vmem(1, BLK, KEPT * BLK, dtype=jnp.float32), 2, 15,
             [
                 pltpu.VMEM((DUMMY, BLK, BLK), jnp.bfloat16),
                 pltpu.VMEM((BLK, KEPT * BLK), jnp.float32),
                 pltpu.VMEM((BLK, KEPT * BLK), jnp.bfloat16),
-            ],
-        )(table, keep, masked, own, *x, got1, w1, w2, w3, got_c, got_s, got_a, got_b, got_f)
+            ], 24,
+        )(table, keep, masked, own, *x, got1, w1, w2, w3, got_c, got_s, got_a, got_b, got_t, got_f)
 
     return jax.shard_map(
         body,

time: 127 us -> 116 us (0.913)
  waiting for transfers between devices: 39.9 us -> 30 us
  starting transfers between devices: 63.2 us -> 66.3 us
  Pallas kernels: 18.8 us -> 16.1 us
  local copies, waits for them, and re-layouts: 4.01 us -> 2.43 us
    ppermute x12 -> x13, waiting for transfers between devices: 39.9 us -> 30 us  [send(): return lax.ppermute(array, AXES, moves[name])]
    ppermute x12 -> x13, starting transfers between devices: 63.2 us -> 66.3 us  [send(): return lax.ppermute(array, AXES, moves[name])]
    pallas_call x1, Pallas kernels: 11.7 us -> 9.52 us  [body(): call(functools.partial(final_kernel, starts[7]), vmem(1, BLK, KEPT * BLK,...]
    unnamed x8 -> x6, local copies, waits for them, and re-layouts: 3.28 us -> 1.71 us
  transfers between devices with their start and end apart: 12 -> 13, of which waited for: 5 -> 5; matrix products, arithmetic and copies ran while one was open for 0% -> 0% of each run, Pallas kernels for 0% -> 0%
where the time goes in v3:
time: 116 us; the launch traced here: 115 us
  starting transfers between devices  66.3 us (57%)
  waiting for transfers between devices  30 us (26%)
  Pallas kernels  16.1 us (14%)
  local copies, waits for them, and re-layouts  2.43 us (2%)
    ppermute x13, starting transfers between devices, send(): return lax.ppermute(array, AXES, moves[name])  66.3 us
    ppermute x13, waiting for transfers between devices, send(): return lax.ppermute(array, AXES, moves[name])  30 us
    pallas_call x1, Pallas kernels, body(): call(functools.partial(final_kernel, starts[7]), vmem(1, BLK, KEPT * BLK,...  9.52 us
    pallas_call x1, Pallas kernels, body(): call(functools.partial(third_kernel, starts[4]), (vmem(kb, BLK, BLK), vme...  2.98 us
    pallas_call x1, Pallas kernels, body(): call(functools.partial(second_kernel, starts[2]), (vmem(ks, BLK, BLK), vm...  2.59 us
  transfers between devices with their start and end apart: 13, of which 5 were waited for; matrix products, arithmetic and copies ran while one was open for 0% of the time, Pallas kernels for 0%

profile of v3, /device:TPU:1, one launch (start us, length us, event | category | flops | bytes accessed | tf_op | source)
XLA Modules:
  0.0 115.0 jit_solution(16253938086690815386)
XLA Ops:
  0.0 0.7 dynamic-slice_reduce_fusion.table.spots
  0.7 1.0 copy-done
  2.4 1.0 shard_map.46
  3.4 5.2 %collective-permute-start.2 = (bf16[13,128,128]{2,1,0:T(8,128)(2,1)S(1)}, bf16[13,128,128]{2,1,0:T(8,128)(2,1)S(1)}, u32[]{:S(2)}, u32[]{:S(2)}) collective-permute-start(bf16[13,128,128]{2,1,0:T(8,128)(2,1)S(1)} %get-tuple-element.26.send2), channel_id=1, source_target_pairs={{0,3},{1,0},{2,1},{3,2},{4,7},{5,4},{6,5},{7,6},{8,11},{9,8},{10,9... | collective-permute-start | bytes 1277960 | tf_op jit(solution)/shard_map/ppermute | solution.py:258
  8.7 2.4 %collective-permute-start.1 = (bf16[13,128,128]{2,1,0:T(8,128)(2,1)S(1)}, bf16[13,128,128]{2,1,0:T(8,128)(2,1)S(1)}, u32[]{:S(2)}, u32[]{:S(2)}) collective-permute-start(bf16[13,128,128]{2,1,0:T(8,128)(2,1)S(1)} %get-tuple-element.26.send2), channel_id=1, source_target_pairs={{0,2},{1,3},{2,0},{3,1},{4,6},{5,7},{6,4},{7,5},{8,10},{9,11},{10,... | collective-permute-start | bytes 1277960 | tf_op jit(solution)/shard_map/ppermute | solution.py:258
  11.1 2.5 %collective-permute-start = (bf16[13,128,128]{2,1,0:T(8,128)(2,1)S(1)}, bf16[13,128,128]{2,1,0:T(8,128)(2,1)S(1)}, u32[]{:S(2)}, u32[]{:S(2)}) collective-permute-start(bf16[13,128,128]{2,1,0:T(8,128)(2,1)S(1)} %get-tuple-element.26.send2), channel_id=1, source_target_pairs={{0,1},{1,2},{2,3},{3,0},{4,5},{5,6},{6,7},{7,4},{8,9},{9,10},{10,1... | collective-permute-start | bytes 1277960 | tf_op jit(solution)/shard_map/ppermute | solution.py:258
  13.6 15.4 %collective-permute-start.3 = (bf16[5,128,128]{2,1,0:T(8,128)(2,1)S(1)}, bf16[5,128,128]{2,1,0:T(8,128)(2,1)S(1)}, u32[]{:S(2)}, u32[]{:S(2)}) collective-permute-start(bf16[5,128,128]{2,1,0:T(8,128)(2,1)S(1)} %get-tuple-element.27), channel_id=1, source_target_pairs={{0,4},{1,5},{2,6},{3,7},{4,0},{5,1},{6,2},{7,3},{8,12},{9,13},{10,... | collective-permute-start | bytes 491528 | tf_op jit(solution)/shard_map/ppermute | solution.py:258
  29.1 3.0 %collective-permute-done.3.got1.refs_4_ = bf16[5,128,128]{2,1,0:T(8,128)(2,1)S(1)} collective-permute-done((bf16[5,128,128]{2,1,0:T(8,128)(2,1)S(1)}, bf16[5,128,128]{2,1,0:T(8,128)(2,1)S(1)}, u32[]{:S(2)}, u32[]{:S(2)}) %collective-permute-start.3) | collective-permute-done | bytes 163872 | tf_op jit(solution)/shard_map/ppermute | solution.py:258
  32.1 2.6 %shard_map.47 = (bf16[23,128,128]{2,1,0:T(8,128)(2,1)S(1)}, bf16[40,128,128]{2,1,0:T(8,128)(2,1)S(1)}) custom-call(s32[374]{0:T(512)S(1)} %dynamic-slice_reduce_fusion.table.spots, bf16[17,128,128]{2,1,0:T(8,128)(2,1)S(1)} %get-tuple-element.25.own.refs_0_, bf16[13,128,128]{2,1,0:T(8,128)(2,1)S(1)} %collective-permute-done.x1.refs_1_, ...), custom_call_target="tpu_custom_call" | custom-call | tf_op jit(solution)/shard_map/pallas_call | solution.py:272
  34.7 14.1 %collective-permute-start.8 = (bf16[40,128,128]{2,1,0:T(8,128)(2,1)S(1)}, bf16[40,128,128]{2,1,0:T(8,128)(2,1)S(1)}, u32[]{:S(2)}, u32[]{:S(2)}) collective-permute-start(bf16[40,128,128]{2,1,0:T(8,128)(2,1)S(1)} %get-tuple-element.33), channel_id=1, source_target_pairs={{0,508},{1,509},{2,510},{3,511},{4,504},{5,505},{6,506},{7,507},{8... | collective-permute-start | bytes 3932168 | tf_op jit(solution)/shard_map/ppermute | solution.py:258
  48.8 0.7 collective-permute-start.7
  49.5 4.0 %collective-permute-start.6 = (bf16[5,128,128]{2,1,0:T(8,128)(2,1)S(1)}, bf16[5,128,128]{2,1,0:T(8,128)(2,1)S(1)}, u32[]{:S(2)}, u32[]{:S(2)}) collective-permute-start(bf16[5,128,128]{2,1,0:T(8,128)(2,1)S(1)} %collective-permute-done.3.got1.refs_4_), channel_id=1, source_target_pairs={{0,3},{1,0},{2,1},{3,2},{4,7},{5,4},{6,5},{7,6},{8,11},{9,8},{10,9... | collective-permute-start | bytes 491528 | tf_op jit(solution)/shard_map/ppermute | solution.py:258
  53.5 3.1 %collective-permute-start.5 = (bf16[5,128,128]{2,1,0:T(8,128)(2,1)S(1)}, bf16[5,128,128]{2,1,0:T(8,128)(2,1)S(1)}, u32[]{:S(2)}, u32[]{:S(2)}) collective-permute-start(bf16[5,128,128]{2,1,0:T(8,128)(2,1)S(1)} %collective-permute-done.3.got1.refs_4_), channel_id=1, source_target_pairs={{0,2},{1,3},{2,0},{3,1},{4,6},{5,7},{6,4},{7,5},{8,10},{9,11},{10,... | collective-permute-start | bytes 491528 | tf_op jit(solution)/shard_map/ppermute | solution.py:258
  56.6 1.9 %collective-permute-start.4 = (bf16[5,128,128]{2,1,0:T(8,128)(2,1)S(1)}, bf16[5,128,128]{2,1,0:T(8,128)(2,1)S(1)}, u32[]{:S(2)}, u32[]{:S(2)}) collective-permute-start(bf16[5,128,128]{2,1,0:T(8,128)(2,1)S(1)} %collective-permute-done.3.got1.refs_4_), channel_id=1, source_target_pairs={{0,1},{1,2},{2,3},{3,0},{4,5},{5,6},{6,7},{7,4},{8,9},{9,10},{10,1... | collective-permute-start | bytes 491528 | tf_op jit(solution)/shard_map/ppermute | solution.py:258
  58.6 2.8 %collective-permute-done.5.w2.refs_6_ = bf16[5,128,128]{2,1,0:T(8,128)(2,1)S(1)} collective-permute-done((bf16[5,128,128]{2,1,0:T(8,128)(2,1)S(1)}, bf16[5,128,128]{2,1,0:T(8,128)(2,1)S(1)}, u32[]{:S(2)}, u32[]{:S(2)}) %collective-permute-start.5) | collective-permute-done | bytes 163872 | tf_op jit(solution)/shard_map/ppermute | solution.py:258
  61.3 2.9 %collective-permute-done.4.w1.refs_5_ = bf16[5,128,128]{2,1,0:T(8,128)(2,1)S(1)} collective-permute-done((bf16[5,128,128]{2,1,0:T(8,128)(2,1)S(1)}, bf16[5,128,128]{2,1,0:T(8,128)(2,1)S(1)}, u32[]{:S(2)}, u32[]{:S(2)}) %collective-permute-start.4) | collective-permute-done | bytes 163872 | tf_op jit(solution)/shard_map/ppermute | solution.py:258
  64.2 1.6 %collective-permute-done.8.refs_10_ = bf16[40,128,128]{2,1,0:T(8,128)(2,1)S(1)} collective-permute-done((bf16[40,128,128]{2,1,0:T(8,128)(2,1)S(1)}, bf16[40,128,128]{2,1,0:T(8,128)(2,1)S(1)}, u32[]{:S(2)}, u32[]{:S(2)}) %collective-permute-start.8) | collective-permute-done | bytes 1310752 | tf_op jit(solution)/shard_map/ppermute | solution.py:258
  65.8 3.0 %shard_map.48 = (bf16[17,128,128]{2,1,0:T(8,128)(2,1)S(1)}, bf16[8,128,128]{2,1,0:T(8,128)(2,1)S(1)}, bf16[16,128,128]{2,1,0:T(8,128)(2,1)S(1)}, bf16[72,128,128]{2,1,0:T(8,128)(2,1)S(1)}) custom-call(s32[374]{0:T(512)S(1)} %dynamic-slice_reduce_fusion.table.spots, bf16[17,128,128]{2,1,0:T(8,128)(2,1)S(1)} %get-tuple-element.25.own.refs_0_, ...), custom_call_target="tpu_custom_call" | custom-call | tf_op jit(solution)/shard_map/pallas_call | solution.py:277
  68.8 12.4 %collective-permute-start.9 = (bf16[72,128,128]{2,1,0:T(8,128)(2,1)S(1)}, bf16[72,128,128]{2,1,0:T(8,128)(2,1)S(1)}, u32[]{:S(2)}, u32[]{:S(2)}) collective-permute-start(bf16[72,128,128]{2,1,0:T(8,128)(2,1)S(1)} %get-tuple-element.37), channel_id=1, source_target_pairs={{0,8},{1,9},{2,10},{3,11},{4,12},{5,13},{6,14},{7,15},{8,0},{9,1},... | collective-permute-start | bytes 7077896 | tf_op jit(solution)/shard_map/ppermute | solution.py:258
  81.1 1.9 %collective-permute-start.10 = (bf16[17,128,128]{2,1,0:T(8,128)(2,1)S(1)}, bf16[17,128,128]{2,1,0:T(8,128)(2,1)S(1)}, u32[]{:S(2)}, u32[]{:S(2)}) collective-permute-start(bf16[17,128,128]{2,1,0:T(8,128)(2,1)S(1)} %get-tuple-element.40), channel_id=1, source_target_pairs={{0,508},{1,509},{2,510},{3,511},{4,504},{5,505},{6,506},{7,507},{8... | collective-permute-start | bytes 1671176 | tf_op jit(solution)/shard_map/ppermute | solution.py:258
  83.1 1.9 %collective-permute-start.12 = (bf16[16,128,128]{2,1,0:T(8,128)(2,1)S(1)}, bf16[16,128,128]{2,1,0:T(8,128)(2,1)S(1)}, u32[]{:S(2)}, u32[]{:S(2)}) collective-permute-start(bf16[16,128,128]{2,1,0:T(8,128)(2,1)S(1)} %get-tuple-element.42), channel_id=1, source_target_pairs={{0,16},{1,17},{2,502},{3,503},{8,24},{9,25},{10,510},{11,511},{16,... | collective-permute-start | bytes 1572872 | tf_op jit(solution)/shard_map/ppermute | solution.py:258
  85.0 0.7 collective-permute-start.11
  85.7 19.8 %collective-permute-done.12.refs_13_ = bf16[16,128,128]{2,1,0:T(8,128)(2,1)S(1)} collective-permute-done((bf16[16,128,128]{2,1,0:T(8,128)(2,1)S(1)}, bf16[16,128,128]{2,1,0:T(8,128)(2,1)S(1)}, u32[]{:S(2)}, u32[]{:S(2)}) %collective-permute-start.12) | collective-permute-done | bytes 524320 | tf_op jit(solution)/shard_map/ppermute | solution.py:258
  105.5 9.5 %shard_map.49 = f32[1,128,2688]{2,1,0:T(8,128)} custom-call(s32[374]{0:T(512)S(1)} %dynamic-slice_reduce_fusion.table.spots, s32[1,21]{1,0:T(1,128)S(1)} %copy-done.2, bf16[128,2176]{1,0:T(8,128)(2,1)S(1)} %get-tuple-element.24.masked, bf16[17,128,128]{2,1,0:T(8,128)(2,1)S(1)} %get-tuple-element.25.own.refs_0_, ...), custom_call_target="tpu_custom_call" | custom-call | tf_op jit(solution)/shard_map/pallas_call | solution.py:282
  (13 shorter events, 0.7 us)
Async XLA Ops:
  0.7 1.1 copy-start
  1.8 0.7 copy-start.1
  3.4 28.6 %collective-permute-start.2 = (bf16[13,128,128]{2,1,0:T(8,128)(2,1)S(1)}, bf16[13,128,128]{2,1,0:T(8,128)(2,1)S(1)}, u32[]{:S(2)}, u32[]{:S(2)}) collective-permute-start(bf16[13,128,128]{2,1,0:T(8,128)(2,1)S(1)} %get-tuple-element.26.send2), channel_id=1, source_target_pairs={{0,3},{1,0},{2,1},{3,2},{4,7},{5,4},{6,5},{7,6},{8,11},{9,8},{10,9... | collective-permute-start | bytes 1277960 | tf_op jit(solution)/shard_map/ppermute | solution.py:258
  8.7 23.4 %collective-permute-start.1 = (bf16[13,128,128]{2,1,0:T(8,128)(2,1)S(1)}, bf16[13,128,128]{2,1,0:T(8,128)(2,1)S(1)}, u32[]{:S(2)}, u32[]{:S(2)}) collective-permute-start(bf16[13,128,128]{2,1,0:T(8,128)(2,1)S(1)} %get-tuple-element.26.send2), channel_id=1, source_target_pairs={{0,2},{1,3},{2,0},{3,1},{4,6},{5,7},{6,4},{7,5},{8,10},{9,11},{10,... | collective-permute-start | bytes 1277960 | tf_op jit(solution)/shard_map/ppermute | solution.py:258
  11.1 21.0 %collective-permute-start = (bf16[13,128,128]{2,1,0:T(8,128)(2,1)S(1)}, bf16[13,128,128]{2,1,0:T(8,128)(2,1)S(1)}, u32[]{:S(2)}, u32[]{:S(2)}) collective-permute-start(bf16[13,128,128]{2,1,0:T(8,128)(2,1)S(1)} %get-tuple-element.26.send2), channel_id=1, source_target_pairs={{0,1},{1,2},{2,3},{3,0},{4,5},{5,6},{6,7},{7,4},{8,9},{9,10},{10,1... | collective-permute-start | bytes 1277960 | tf_op jit(solution)/shard_map/ppermute | solution.py:258
  13.6 18.4 %collective-permute-start.3 = (bf16[5,128,128]{2,1,0:T(8,128)(2,1)S(1)}, bf16[5,128,128]{2,1,0:T(8,128)(2,1)S(1)}, u32[]{:S(2)}, u32[]{:S(2)}) collective-permute-start(bf16[5,128,128]{2,1,0:T(8,128)(2,1)S(1)} %get-tuple-element.27), channel_id=1, source_target_pairs={{0,4},{1,5},{2,6},{3,7},{4,0},{5,1},{6,2},{7,3},{8,12},{9,13},{10,... | collective-permute-start | bytes 491528 | tf_op jit(solution)/shard_map/ppermute | solution.py:258
  34.7 31.1 %collective-permute-start.8 = (bf16[40,128,128]{2,1,0:T(8,128)(2,1)S(1)}, bf16[40,128,128]{2,1,0:T(8,128)(2,1)S(1)}, u32[]{:S(2)}, u32[]{:S(2)}) collective-permute-start(bf16[40,128,128]{2,1,0:T(8,128)(2,1)S(1)} %get-tuple-element.33), channel_id=1, source_target_pairs={{0,508},{1,509},{2,510},{3,511},{4,504},{5,505},{6,506},{7,507},{8... | collective-permute-start | bytes 3932168 | tf_op jit(solution)/shard_map/ppermute | solution.py:258
  48.7 56.7 %copy-start.2 = (s32[1,21]{1,0:T(1,128)S(1)}, s32[1,21]{1,0:T(1,128)}, u32[]{:S(2)}) copy-start(s32[1,21]{1,0:T(1,128)} %keep.1) | copy-start | bytes 256
  48.8 15.4 %collective-permute-start.7 = (bf16[23,128,128]{2,1,0:T(8,128)(2,1)S(1)}, bf16[23,128,128]{2,1,0:T(8,128)(2,1)S(1)}, u32[]{:S(2)}, u32[]{:S(2)}) collective-permute-start(bf16[23,128,128]{2,1,0:T(8,128)(2,1)S(1)} %get-tuple-element.32), channel_id=1, source_target_pairs={{0,4},{1,5},{2,6},{3,7},{124,120},{125,121},{126,122},{127,123},{1... | collective-permute-start | bytes 2261000 | tf_op jit(solution)/shard_map/ppermute | solution.py:258
  49.5 9.1 %collective-permute-start.6 = (bf16[5,128,128]{2,1,0:T(8,128)(2,1)S(1)}, bf16[5,128,128]{2,1,0:T(8,128)(2,1)S(1)}, u32[]{:S(2)}, u32[]{:S(2)}) collective-permute-start(bf16[5,128,128]{2,1,0:T(8,128)(2,1)S(1)} %collective-permute-done.3.got1.refs_4_), channel_id=1, source_target_pairs={{0,3},{1,0},{2,1},{3,2},{4,7},{5,4},{6,5},{7,6},{8,11},{9,8},{10,9... | collective-permute-start | bytes 491528 | tf_op jit(solution)/shard_map/ppermute | solution.py:258
  53.5 7.9 %collective-permute-start.5 = (bf16[5,128,128]{2,1,0:T(8,128)(2,1)S(1)}, bf16[5,128,128]{2,1,0:T(8,128)(2,1)S(1)}, u32[]{:S(2)}, u32[]{:S(2)}) collective-permute-start(bf16[5,128,128]{2,1,0:T(8,128)(2,1)S(1)} %collective-permute-done.3.got1.refs_4_), channel_id=1, source_target_pairs={{0,2},{1,3},{2,0},{3,1},{4,6},{5,7},{6,4},{7,5},{8,10},{9,11},{10,... | collective-permute-start | bytes 491528 | tf_op jit(solution)/shard_map/ppermute | solution.py:258
  56.6 7.6 %collective-permute-start.4 = (bf16[5,128,128]{2,1,0:T(8,128)(2,1)S(1)}, bf16[5,128,128]{2,1,0:T(8,128)(2,1)S(1)}, u32[]{:S(2)}, u32[]{:S(2)}) collective-permute-start(bf16[5,128,128]{2,1,0:T(8,128)(2,1)S(1)} %collective-permute-done.3.got1.refs_4_), channel_id=1, source_target_pairs={{0,1},{1,2},{2,3},{3,0},{4,5},{5,6},{6,7},{7,4},{8,9},{9,10},{10,1... | collective-permute-start | bytes 491528 | tf_op jit(solution)/shard_map/ppermute | solution.py:258
  68.8 36.7 %collective-permute-start.9 = (bf16[72,128,128]{2,1,0:T(8,128)(2,1)S(1)}, bf16[72,128,128]{2,1,0:T(8,128)(2,1)S(1)}, u32[]{:S(2)}, u32[]{:S(2)}) collective-permute-start(bf16[72,128,128]{2,1,0:T(8,128)(2,1)S(1)} %get-tuple-element.37), channel_id=1, source_target_pairs={{0,8},{1,9},{2,10},{3,11},{4,12},{5,13},{6,14},{7,15},{8,0},{9,1},... | collective-permute-start | bytes 7077896 | tf_op jit(solution)/shard_map/ppermute | solution.py:258
  81.1 24.3 %collective-permute-start.10 = (bf16[17,128,128]{2,1,0:T(8,128)(2,1)S(1)}, bf16[17,128,128]{2,1,0:T(8,128)(2,1)S(1)}, u32[]{:S(2)}, u32[]{:S(2)}) collective-permute-start(bf16[17,128,128]{2,1,0:T(8,128)(2,1)S(1)} %get-tuple-element.40), channel_id=1, source_target_pairs={{0,508},{1,509},{2,510},{3,511},{4,504},{5,505},{6,506},{7,507},{8... | collective-permute-start | bytes 1671176 | tf_op jit(solution)/shard_map/ppermute | solution.py:258
  83.1 22.4 %collective-permute-start.12 = (bf16[16,128,128]{2,1,0:T(8,128)(2,1)S(1)}, bf16[16,128,128]{2,1,0:T(8,128)(2,1)S(1)}, u32[]{:S(2)}, u32[]{:S(2)}) collective-permute-start(bf16[16,128,128]{2,1,0:T(8,128)(2,1)S(1)} %get-tuple-element.42), channel_id=1, source_target_pairs={{0,16},{1,17},{2,502},{3,503},{8,24},{9,25},{10,510},{11,511},{16,... | collective-permute-start | bytes 1572872 | tf_op jit(solution)/shard_map/ppermute | solution.py:258
  85.0 0.7 collective-permute-start.11

commit v4 on v3

--- a/solution.py
+++ b/solution.py
@@ -82,8 +82,10 @@
     got3 = [moved(got1, f"x{s}") for s in (1, 2, 3)]
     stock2 = join(own, *got2)
     stock3 = join(stock2, got1, *got3)
-    got_c = moved(join(sent2, *got2, got1, *got3), "c")
-    known = [set(row) for row in join(stock3, got_c)]
+    got_c = moved(join(sent2, *got2), "c")
+    got_d = moved(join(got1, *got3), "c")
+    stock4 = join(stock3, got_c)
+    known = [set(row) for row in join(stock4, got_d)]
 
     def choose(name, stock):
         sends = [[] for _ in range(n)]
@@ -98,15 +100,15 @@
 
     sent_s, got_s = choose("seam", stock2)
     sent_a, got_a = choose("z", stock2)
-    sent_b, got_b = choose("z", stock3)
-    sent_t, got_t = choose("seam", stock3)
-    sent_f, got_f = choose("far", stock3)
+    sent_b, got_b = choose("z", stock4)
+    sent_t, got_t = choose("seam", stock4)
+    sent_f, got_f = choose("far", stock4)
     assert all(set(need[d]) <= known[d] for d in range(n))
 
     def where(sends, stock):
         return np.array([[src.index(b) if b is not None else 0 for b in q] for q, src in zip(sends, stock)], np.int32)
 
-    arrived = join(stock3, got_c, got_s, got_a, got_b, got_t, got_f)
+    arrived = join(stock4, got_d, got_s, got_a, got_b, got_t, got_f)
     spots = np.full((n, len(arrived[0])), DUMMY, np.int32)
     for i in range(n):
         seen = set()
@@ -114,7 +116,7 @@
             if b in need[i] and b not in seen:
                 seen.add(b)
                 spots[i, k] = need[i][b]
-    parts = [where(sent1, own), where(sent2, own), where(sent_s, stock2), where(sent_a, stock2), where(sent_b, stock3), where(sent_t, stock3), where(sent_f, stock3), spots]
+    parts = [where(sent1, own), where(sent2, own), where(sent_s, stock2), where(sent_a, stock2), where(sent_b, stock4), where(sent_t, stock4), where(sent_f, stock4), spots]
     starts = np.cumsum([0] + [q.shape[1] for q in parts])
     return moves, np.concatenate(parts, axis=1), [q.shape[1] for q in parts], [int(q) for q in starts]
 
@@ -178,13 +180,14 @@
         low += source.shape[0]
 
 
-def second_kernel(start, table, own, x1, x2, x3, seam, z):
+def second_kernel(start, table, own, send2, x1, x2, x3, seam, z, both):
     gather(start, table, [own, x1, x2, x3], [seam, z])
-
-
-def third_kernel(start, table, own, send2, x1, x2, x3, got1, w1, w2, w3, z, seam, far, both):
-    gather(start, table, [own, x1, x2, x3, got1, w1, w2, w3], [z, seam, far])
-    concatenate([send2, x1, x2, x3, got1, w1, w2, w3], both)
+    concatenate([send2, x1, x2, x3], both)
+
+
+def third_kernel(start, table, own, x1, x2, x3, got1, w1, w2, w3, got_c, z, seam, far, both):
+    gather(start, table, [own, x1, x2, x3, got1, w1, w2, w3, got_c], [z, seam, far])
+    concatenate([got1, w1, w2, w3], both)
 
 
 def product(left, first, pool, v, width):
@@ -263,30 +266,29 @@
             functools.partial(first_kernel, starts[0]),
             (vmem(BLK, 17 * BLK), vmem(17, BLK, BLK), vmem(k1, BLK, BLK), vmem(k2, BLK, BLK)), 2, 1,
         )(table, pattern, density)
-        x = [send(send2, f"x{step}") for step in (1, 3, 2)]
-        x = [x[0], x[2], x[1]]
+        x = [send(send2, f"x{step}") for step in (1, 2, 3)]
         got1 = send(send1, "zh")
-        *x, got1 = lax.optimization_barrier((*x, got1))
-        w = [send(got1, f"x{step}") for step in (1, 3, 2)]
-        w = [w[0], w[2], w[1]]
-        send_s, send_a = call(
-            functools.partial(second_kernel, starts[2]), (vmem(ks, BLK, BLK), vmem(ka, BLK, BLK)), 1, 4,
-        )(table, own, *x)
-        got_s, got_a = send(send_s, "seam"), send(send_a, "z")
-        w1, w2, w3, got_s, got_a = lax.optimization_barrier((*w, got_s, got_a))
-        send_b, send_t, send_f, both = call(
+        send_s, send_a, both2 = call(
+            functools.partial(second_kernel, starts[2]),
+            (vmem(ks, BLK, BLK), vmem(ka, BLK, BLK), vmem(4 * k2, BLK, BLK)), 1, 5,
+        )(table, own, send2, *x)
+        got1, send_s, send_a, both2 = lax.optimization_barrier((got1, send_s, send_a, both2))
+        got_s, got_a, got_c = send(send_s, "seam"), send(send_a, "z"), send(both2, "c")
+        w = [send(got1, f"x{step}") for step in (1, 2, 3)]
+        *w, got_a, got_c, got_s = lax.optimization_barrier((*w, got_a, got_c, got_s))
+        send_b, send_t, send_f, both3 = call(
             functools.partial(third_kernel, starts[4]),
-            (vmem(kb, BLK, BLK), vmem(kt, BLK, BLK), vmem(kf, BLK, BLK), vmem(4 * (k1 + k2), BLK, BLK)), 1, 9,
-        )(table, own, send2, *x, got1, w1, w2, w3)
-        got_b, got_t, got_f, got_c = send(send_b, "z"), send(send_t, "seam"), send(send_f, "far"), send(both, "c")
+            (vmem(kb, BLK, BLK), vmem(kt, BLK, BLK), vmem(kf, BLK, BLK), vmem(4 * k1, BLK, BLK)), 1, 9,
+        )(table, own, *x, got1, *w, got_c)
+        got_b, got_t, got_f, got_d = send(send_b, "z"), send(send_t, "seam"), send(send_f, "far"), send(both3, "c")
         return call(
-            functools.partial(final_kernel, starts[7]), vmem(1, BLK, KEPT * BLK, dtype=jnp.float32), 2, 15,
+            functools.partial(final_kernel, starts[7]), vmem(1, BLK, KEPT * BLK, dtype=jnp.float32), 2, 16,
             [
                 pltpu.VMEM((DUMMY, BLK, BLK), jnp.bfloat16),
                 pltpu.VMEM((BLK, KEPT * BLK), jnp.float32),
                 pltpu.VMEM((BLK, KEPT * BLK), jnp.bfloat16),
             ], 24,
-        )(table, keep, masked, own, *x, got1, w1, w2, w3, got_c, got_s, got_a, got_b, got_t, got_f)
+        )(table, keep, masked, own, *x, got1, *w, got_c, got_d, got_s, got_a, got_b, got_t, got_f)
 
     return jax.shard_map(
         body,

time: 116 us -> 119 us (1.026)
  the two profiles are of different devices: /device:TPU:1 before, /device:TPU:2 now
where the time goes in v4:
time: 119 us
  starting transfers between devices  85 us (71%)
  Pallas kernels  16 us (13%)
  waiting for transfers between devices  15 us (13%)
  local copies, waits for them, and re-layouts  2.43 us (2%)
    ppermute x14, starting transfers between devices, send(): return lax.ppermute(array, AXES, moves[name])  85 us
    ppermute x14, waiting for transfers between devices, send(): return lax.ppermute(array, AXES, moves[name])  15 us
    pallas_call x1, Pallas kernels, body(): call(functools.partial(final_kernel, starts[7]), vmem(1, BLK, KEPT * BLK,...  9.46 us
    pallas_call x1, Pallas kernels, body(): call(functools.partial(third_kernel, starts[4]), (vmem(kb, BLK, BLK), vme...  2.87 us
    pallas_call x1, Pallas kernels, body(): call(functools.partial(second_kernel, starts[2]), (vmem(ks, BLK, BLK), vm...  2.7 us
  transfers between devices with their start and end apart: 14, of which 6 were waited for; matrix products, arithmetic and copies ran while one was open for 0% of the time, Pallas kernels for 2%

profile of v4, /device:TPU:2, one launch (start us, length us, event | category | flops | bytes accessed | tf_op | source)
XLA Modules:
  0.0 118.6 jit_solution(17584567789512412016)
XLA Ops:
  0.7 1.0 copy-done
  2.4 1.0 shard_map.46
  3.4 7.8 %collective-permute-start.2 = (bf16[13,128,128]{2,1,0:T(8,128)(2,1)S(1)}, bf16[13,128,128]{2,1,0:T(8,128)(2,1)S(1)}, u32[]{:S(2)}, u32[]{:S(2)}) collective-permute-start(bf16[13,128,128]{2,1,0:T(8,128)(2,1)S(1)} %get-tuple-element.28.send2), channel_id=1, source_target_pairs={{0,3},{1,0},{2,1},{3,2},{4,7},{5,4},{6,5},{7,6},{8,11},{9,8},{10,9... | collective-permute-start | bytes 1277960 | tf_op jit(solution)/shard_map/ppermute | solution.py:261
  11.3 1.9 %collective-permute-start.1 = (bf16[13,128,128]{2,1,0:T(8,128)(2,1)S(1)}, bf16[13,128,128]{2,1,0:T(8,128)(2,1)S(1)}, u32[]{:S(2)}, u32[]{:S(2)}) collective-permute-start(bf16[13,128,128]{2,1,0:T(8,128)(2,1)S(1)} %get-tuple-element.28.send2), channel_id=1, source_target_pairs={{0,2},{1,3},{2,0},{3,1},{4,6},{5,7},{6,4},{7,5},{8,10},{9,11},{10,... | collective-permute-start | bytes 1277960 | tf_op jit(solution)/shard_map/ppermute | solution.py:261
  13.2 3.4 %collective-permute-start = (bf16[13,128,128]{2,1,0:T(8,128)(2,1)S(1)}, bf16[13,128,128]{2,1,0:T(8,128)(2,1)S(1)}, u32[]{:S(2)}, u32[]{:S(2)}) collective-permute-start(bf16[13,128,128]{2,1,0:T(8,128)(2,1)S(1)} %get-tuple-element.28.send2), channel_id=1, source_target_pairs={{0,1},{1,2},{2,3},{3,0},{4,5},{5,6},{6,7},{7,4},{8,9},{9,10},{10,1... | collective-permute-start | bytes 1277960 | tf_op jit(solution)/shard_map/ppermute | solution.py:261
  16.6 13.1 %collective-permute-start.3 = (bf16[5,128,128]{2,1,0:T(8,128)(2,1)S(1)}, bf16[5,128,128]{2,1,0:T(8,128)(2,1)S(1)}, u32[]{:S(2)}, u32[]{:S(2)}) collective-permute-start(bf16[5,128,128]{2,1,0:T(8,128)(2,1)S(1)} %get-tuple-element.29), channel_id=1, source_target_pairs={{0,4},{1,5},{2,6},{3,7},{4,0},{5,1},{6,2},{7,3},{8,12},{9,13},{10,... | collective-permute-start | bytes 491528 | tf_op jit(solution)/shard_map/ppermute | solution.py:261
  29.8 2.7 %shard_map.47 = (bf16[23,128,128]{2,1,0:T(8,128)(2,1)S(1)}, bf16[40,128,128]{2,1,0:T(8,128)(2,1)S(1)}, bf16[52,128,128]{2,1,0:T(8,128)(2,1)S(1)}) custom-call(s32[366]{0:T(512)S(1)} %dynamic-slice_reduce_fusion.table.spots, bf16[17,128,128]{2,1,0:T(8,128)(2,1)S(1)} %get-tuple-element.27.own.refs_0_, bf16[13,128,128]{2,1,0:T(8,128)(2,1)S(1)} %get-tuple-element.28.send2, ...), custom_call_target="tpu_custom_call" | custom-call | tf_op jit(solution)/shard_map/pallas_call | solution.py:271
  32.5 0.8 collective-permute-done.3.got1.refs_4_
  33.3 2.0 %collective-permute-start.8 = (bf16[52,128,128]{2,1,0:T(8,128)(2,1)S(1)}, bf16[52,128,128]{2,1,0:T(8,128)(2,1)S(1)}, u32[]{:S(2)}, u32[]{:S(2)}) collective-permute-start(bf16[52,128,128]{2,1,0:T(8,128)(2,1)S(1)} %get-tuple-element.35), channel_id=1, source_target_pairs={{0,8},{1,9},{2,10},{3,11},{4,12},{5,13},{6,14},{7,15},{8,0},{9,1},... | collective-permute-start | bytes 5111816 | tf_op jit(solution)/shard_map/ppermute | solution.py:261
  35.4 17.2 %collective-permute-start.7 = (bf16[40,128,128]{2,1,0:T(8,128)(2,1)S(1)}, bf16[40,128,128]{2,1,0:T(8,128)(2,1)S(1)}, u32[]{:S(2)}, u32[]{:S(2)}) collective-permute-start(bf16[40,128,128]{2,1,0:T(8,128)(2,1)S(1)} %get-tuple-element.34), channel_id=1, source_target_pairs={{0,508},{1,509},{2,510},{3,511},{4,504},{5,505},{6,506},{7,507},{8... | collective-permute-start | bytes 3932168 | tf_op jit(solution)/shard_map/ppermute | solution.py:261
  52.6 6.6 %collective-permute-start.9 = (bf16[23,128,128]{2,1,0:T(8,128)(2,1)S(1)}, bf16[23,128,128]{2,1,0:T(8,128)(2,1)S(1)}, u32[]{:S(2)}, u32[]{:S(2)}) collective-permute-start(bf16[23,128,128]{2,1,0:T(8,128)(2,1)S(1)} %get-tuple-element.36), channel_id=1, source_target_pairs={{0,4},{1,5},{2,6},{3,7},{124,120},{125,121},{126,122},{127,123},{1... | collective-permute-start | bytes 2261000 | tf_op jit(solution)/shard_map/ppermute | solution.py:261
  59.2 2.1 %collective-permute-start.6 = (bf16[5,128,128]{2,1,0:T(8,128)(2,1)S(1)}, bf16[5,128,128]{2,1,0:T(8,128)(2,1)S(1)}, u32[]{:S(2)}, u32[]{:S(2)}) collective-permute-start(bf16[5,128,128]{2,1,0:T(8,128)(2,1)S(1)} %collective-permute-done.3.got1.refs_4_), channel_id=1, source_target_pairs={{0,3},{1,0},{2,1},{3,2},{4,7},{5,4},{6,5},{7,6},{8,11},{9,8},{10,9... | collective-permute-start | bytes 491528 | tf_op jit(solution)/shard_map/ppermute | solution.py:261
  61.3 3.6 %collective-permute-start.5 = (bf16[5,128,128]{2,1,0:T(8,128)(2,1)S(1)}, bf16[5,128,128]{2,1,0:T(8,128)(2,1)S(1)}, u32[]{:S(2)}, u32[]{:S(2)}) collective-permute-start(bf16[5,128,128]{2,1,0:T(8,128)(2,1)S(1)} %collective-permute-done.3.got1.refs_4_), channel_id=1, source_target_pairs={{0,2},{1,3},{2,0},{3,1},{4,6},{5,7},{6,4},{7,5},{8,10},{9,11},{10,... | collective-permute-start | bytes 491528 | tf_op jit(solution)/shard_map/ppermute | solution.py:261
  64.9 1.5 %collective-permute-done.6.w3.refs_7_ = bf16[5,128,128]{2,1,0:T(8,128)(2,1)S(1)} collective-permute-done((bf16[5,128,128]{2,1,0:T(8,128)(2,1)S(1)}, bf16[5,128,128]{2,1,0:T(8,128)(2,1)S(1)}, u32[]{:S(2)}, u32[]{:S(2)}) %collective-permute-start.6) | collective-permute-done | bytes 163872 | tf_op jit(solution)/shard_map/ppermute | solution.py:261
  66.4 2.6 %collective-permute-start.4 = (bf16[5,128,128]{2,1,0:T(8,128)(2,1)S(1)}, bf16[5,128,128]{2,1,0:T(8,128)(2,1)S(1)}, u32[]{:S(2)}, u32[]{:S(2)}) collective-permute-start(bf16[5,128,128]{2,1,0:T(8,128)(2,1)S(1)} %collective-permute-done.3.got1.refs_4_), channel_id=1, source_target_pairs={{0,1},{1,2},{2,3},{3,0},{4,5},{5,6},{6,7},{7,4},{8,9},{9,10},{10,1... | collective-permute-start | bytes 491528 | tf_op jit(solution)/shard_map/ppermute | solution.py:261
  69.0 1.1 collective-permute-done.5.w2.refs_6_
  70.0 3.6 %collective-permute-done.4.w1.refs_5_ = bf16[5,128,128]{2,1,0:T(8,128)(2,1)S(1)} collective-permute-done((bf16[5,128,128]{2,1,0:T(8,128)(2,1)S(1)}, bf16[5,128,128]{2,1,0:T(8,128)(2,1)S(1)}, u32[]{:S(2)}, u32[]{:S(2)}) %collective-permute-start.4) | collective-permute-done | bytes 163872 | tf_op jit(solution)/shard_map/ppermute | solution.py:261
  73.6 2.9 %shard_map.48 = (bf16[26,128,128]{2,1,0:T(8,128)(2,1)S(1)}, bf16[8,128,128]{2,1,0:T(8,128)(2,1)S(1)}, bf16[3,128,128]{2,1,0:T(8,128)(2,1)S(1)}, bf16[20,128,128]{2,1,0:T(8,128)(2,1)S(1)}) custom-call(s32[366]{0:T(512)S(1)} %dynamic-slice_reduce_fusion.table.spots, bf16[17,128,128]{2,1,0:T(8,128)(2,1)S(1)} %get-tuple-element.27.own.refs_0_, ...), custom_call_target="tpu_custom_call" | custom-call | tf_op jit(solution)/shard_map/pallas_call | solution.py:279
  76.5 8.1 %collective-permute-start.11 = (bf16[26,128,128]{2,1,0:T(8,128)(2,1)S(1)}, bf16[26,128,128]{2,1,0:T(8,128)(2,1)S(1)}, u32[]{:S(2)}, u32[]{:S(2)}) collective-permute-start(bf16[26,128,128]{2,1,0:T(8,128)(2,1)S(1)} %get-tuple-element.44), channel_id=1, source_target_pairs={{0,508},{1,509},{2,510},{3,511},{4,504},{5,505},{6,506},{7,507},{8... | collective-permute-start | bytes 2555912 | tf_op jit(solution)/shard_map/ppermute | solution.py:261
  84.6 1.9 %collective-permute-start.10 = (bf16[20,128,128]{2,1,0:T(8,128)(2,1)S(1)}, bf16[20,128,128]{2,1,0:T(8,128)(2,1)S(1)}, u32[]{:S(2)}, u32[]{:S(2)}) collective-permute-start(bf16[20,128,128]{2,1,0:T(8,128)(2,1)S(1)} %get-tuple-element.41), channel_id=1, source_target_pairs={{0,8},{1,9},{2,10},{3,11},{4,12},{5,13},{6,14},{7,15},{8,0},{9,1},... | collective-permute-start | bytes 1966088 | tf_op jit(solution)/shard_map/ppermute | solution.py:261
  86.5 12.8 %collective-permute-start.12 = (bf16[8,128,128]{2,1,0:T(8,128)(2,1)S(1)}, bf16[8,128,128]{2,1,0:T(8,128)(2,1)S(1)}, u32[]{:S(2)}, u32[]{:S(2)}) collective-permute-start(bf16[8,128,128]{2,1,0:T(8,128)(2,1)S(1)} %get-tuple-element.45), channel_id=1, source_target_pairs={{0,4},{1,5},{2,6},{3,7},{124,120},{125,121},{126,122},{127,123},{1... | collective-permute-start | bytes 786440 | tf_op jit(solution)/shard_map/ppermute | solution.py:261
  99.3 1.9 %collective-permute-start.13 = (bf16[3,128,128]{2,1,0:T(8,128)(2,1)S(1)}, bf16[3,128,128]{2,1,0:T(8,128)(2,1)S(1)}, u32[]{:S(2)}, u32[]{:S(2)}) collective-permute-start(bf16[3,128,128]{2,1,0:T(8,128)(2,1)S(1)} %get-tuple-element.46), channel_id=1, source_target_pairs={{0,16},{1,17},{2,502},{3,503},{8,24},{9,25},{10,510},{11,511},{16,... | collective-permute-start | bytes 294920 | tf_op jit(solution)/shard_map/ppermute | solution.py:261
  101.2 7.9 %collective-permute-done.13.refs_14_ = bf16[3,128,128]{2,1,0:T(8,128)(2,1)S(1)} collective-permute-done((bf16[3,128,128]{2,1,0:T(8,128)(2,1)S(1)}, bf16[3,128,128]{2,1,0:T(8,128)(2,1)S(1)}, u32[]{:S(2)}, u32[]{:S(2)}) %collective-permute-start.13) | collective-permute-done | bytes 98336 | tf_op jit(solution)/shard_map/ppermute | solution.py:261
  109.2 9.5 %shard_map.49 = f32[1,128,2688]{2,1,0:T(8,128)} custom-call(s32[366]{0:T(512)S(1)} %dynamic-slice_reduce_fusion.table.spots, s32[1,21]{1,0:T(1,128)S(1)} %copy-done.2, bf16[128,2176]{1,0:T(8,128)(2,1)S(1)} %get-tuple-element.26.masked, bf16[17,128,128]{2,1,0:T(8,128)(2,1)S(1)} %get-tuple-element.27.own.refs_0_, ...), custom_call_target="tpu_custom_call" | custom-call | tf_op jit(solution)/shard_map/pallas_call | solution.py:284
  (15 shorter events, 1.5 us)
Async XLA Ops:
  0.7 1.1 copy-start
  1.8 0.7 copy-start.1
  3.4 26.2 %collective-permute-start.2 = (bf16[13,128,128]{2,1,0:T(8,128)(2,1)S(1)}, bf16[13,128,128]{2,1,0:T(8,128)(2,1)S(1)}, u32[]{:S(2)}, u32[]{:S(2)}) collective-permute-start(bf16[13,128,128]{2,1,0:T(8,128)(2,1)S(1)} %get-tuple-element.28.send2), channel_id=1, source_target_pairs={{0,3},{1,0},{2,1},{3,2},{4,7},{5,4},{6,5},{7,6},{8,11},{9,8},{10,9... | collective-permute-start | bytes 1277960 | tf_op jit(solution)/shard_map/ppermute | solution.py:261
  11.3 18.4 %collective-permute-start.1 = (bf16[13,128,128]{2,1,0:T(8,128)(2,1)S(1)}, bf16[13,128,128]{2,1,0:T(8,128)(2,1)S(1)}, u32[]{:S(2)}, u32[]{:S(2)}) collective-permute-start(bf16[13,128,128]{2,1,0:T(8,128)(2,1)S(1)} %get-tuple-element.28.send2), channel_id=1, source_target_pairs={{0,2},{1,3},{2,0},{3,1},{4,6},{5,7},{6,4},{7,5},{8,10},{9,11},{10,... | collective-permute-start | bytes 1277960 | tf_op jit(solution)/shard_map/ppermute | solution.py:261
  13.2 16.6 %collective-permute-start = (bf16[13,128,128]{2,1,0:T(8,128)(2,1)S(1)}, bf16[13,128,128]{2,1,0:T(8,128)(2,1)S(1)}, u32[]{:S(2)}, u32[]{:S(2)}) collective-permute-start(bf16[13,128,128]{2,1,0:T(8,128)(2,1)S(1)} %get-tuple-element.28.send2), channel_id=1, source_target_pairs={{0,1},{1,2},{2,3},{3,0},{4,5},{5,6},{6,7},{7,4},{8,9},{9,10},{10,1... | collective-permute-start | bytes 1277960 | tf_op jit(solution)/shard_map/ppermute | solution.py:261
  16.6 16.7 %collective-permute-start.3 = (bf16[5,128,128]{2,1,0:T(8,128)(2,1)S(1)}, bf16[5,128,128]{2,1,0:T(8,128)(2,1)S(1)}, u32[]{:S(2)}, u32[]{:S(2)}) collective-permute-start(bf16[5,128,128]{2,1,0:T(8,128)(2,1)S(1)} %get-tuple-element.29), channel_id=1, source_target_pairs={{0,4},{1,5},{2,6},{3,7},{4,0},{5,1},{6,2},{7,3},{8,12},{9,13},{10,... | collective-permute-start | bytes 491528 | tf_op jit(solution)/shard_map/ppermute | solution.py:261
  33.3 75.8 %copy-start.2 = (s32[1,21]{1,0:T(1,128)S(1)}, s32[1,21]{1,0:T(1,128)}, u32[]{:S(2)}) copy-start(s32[1,21]{1,0:T(1,128)} %keep.1) | copy-start | bytes 256
  33.3 40.3 %collective-permute-start.8 = (bf16[52,128,128]{2,1,0:T(8,128)(2,1)S(1)}, bf16[52,128,128]{2,1,0:T(8,128)(2,1)S(1)}, u32[]{:S(2)}, u32[]{:S(2)}) collective-permute-start(bf16[52,128,128]{2,1,0:T(8,128)(2,1)S(1)} %get-tuple-element.35), channel_id=1, source_target_pairs={{0,8},{1,9},{2,10},{3,11},{4,12},{5,13},{6,14},{7,15},{8,0},{9,1},... | collective-permute-start | bytes 5111816 | tf_op jit(solution)/shard_map/ppermute | solution.py:261
  35.4 38.2 %collective-permute-start.7 = (bf16[40,128,128]{2,1,0:T(8,128)(2,1)S(1)}, bf16[40,128,128]{2,1,0:T(8,128)(2,1)S(1)}, u32[]{:S(2)}, u32[]{:S(2)}) collective-permute-start(bf16[40,128,128]{2,1,0:T(8,128)(2,1)S(1)} %get-tuple-element.34), channel_id=1, source_target_pairs={{0,508},{1,509},{2,510},{3,511},{4,504},{5,505},{6,506},{7,507},{8... | collective-permute-start | bytes 3932168 | tf_op jit(solution)/shard_map/ppermute | solution.py:261
  52.6 21.0 %collective-permute-start.9 = (bf16[23,128,128]{2,1,0:T(8,128)(2,1)S(1)}, bf16[23,128,128]{2,1,0:T(8,128)(2,1)S(1)}, u32[]{:S(2)}, u32[]{:S(2)}) collective-permute-start(bf16[23,128,128]{2,1,0:T(8,128)(2,1)S(1)} %get-tuple-element.36), channel_id=1, source_target_pairs={{0,4},{1,5},{2,6},{3,7},{124,120},{125,121},{126,122},{127,123},{1... | collective-permute-start | bytes 2261000 | tf_op jit(solution)/shard_map/ppermute | solution.py:261
  59.2 7.2 %collective-permute-start.6 = (bf16[5,128,128]{2,1,0:T(8,128)(2,1)S(1)}, bf16[5,128,128]{2,1,0:T(8,128)(2,1)S(1)}, u32[]{:S(2)}, u32[]{:S(2)}) collective-permute-start(bf16[5,128,128]{2,1,0:T(8,128)(2,1)S(1)} %collective-permute-done.3.got1.refs_4_), channel_id=1, source_target_pairs={{0,3},{1,0},{2,1},{3,2},{4,7},{5,4},{6,5},{7,6},{8,11},{9,8},{10,9... | collective-permute-start | bytes 491528 | tf_op jit(solution)/shard_map/ppermute | solution.py:261
  61.3 8.7 %collective-permute-start.5 = (bf16[5,128,128]{2,1,0:T(8,128)(2,1)S(1)}, bf16[5,128,128]{2,1,0:T(8,128)(2,1)S(1)}, u32[]{:S(2)}, u32[]{:S(2)}) collective-permute-start(bf16[5,128,128]{2,1,0:T(8,128)(2,1)S(1)} %collective-permute-done.3.got1.refs_4_), channel_id=1, source_target_pairs={{0,2},{1,3},{2,0},{3,1},{4,6},{5,7},{6,4},{7,5},{8,10},{9,11},{10,... | collective-permute-start | bytes 491528 | tf_op jit(solution)/shard_map/ppermute | solution.py:261
  66.4 7.2 %collective-permute-start.4 = (bf16[5,128,128]{2,1,0:T(8,128)(2,1)S(1)}, bf16[5,128,128]{2,1,0:T(8,128)(2,1)S(1)}, u32[]{:S(2)}, u32[]{:S(2)}) collective-permute-start(bf16[5,128,128]{2,1,0:T(8,128)(2,1)S(1)} %collective-permute-done.3.got1.refs_4_), channel_id=1, source_target_pairs={{0,1},{1,2},{2,3},{3,0},{4,5},{5,6},{6,7},{7,4},{8,9},{9,10},{10,1... | collective-permute-start | bytes 491528 | tf_op jit(solution)/shard_map/ppermute | solution.py:261
  76.5 32.7 %collective-permute-start.11 = (bf16[26,128,128]{2,1,0:T(8,128)(2,1)S(1)}, bf16[26,128,128]{2,1,0:T(8,128)(2,1)S(1)}, u32[]{:S(2)}, u32[]{:S(2)}) collective-permute-start(bf16[26,128,128]{2,1,0:T(8,128)(2,1)S(1)} %get-tuple-element.44), channel_id=1, source_target_pairs={{0,508},{1,509},{2,510},{3,511},{4,504},{5,505},{6,506},{7,507},{8... | collective-permute-start | bytes 2555912 | tf_op jit(solution)/shard_map/ppermute | solution.py:261
  84.6 24.6 %collective-permute-start.10 = (bf16[20,128,128]{2,1,0:T(8,128)(2,1)S(1)}, bf16[20,128,128]{2,1,0:T(8,128)(2,1)S(1)}, u32[]{:S(2)}, u32[]{:S(2)}) collective-permute-start(bf16[20,128,128]{2,1,0:T(8,128)(2,1)S(1)} %get-tuple-element.41), channel_id=1, source_target_pairs={{0,8},{1,9},{2,10},{3,11},{4,12},{5,13},{6,14},{7,15},{8,0},{9,1},... | collective-permute-start | bytes 1966088 | tf_op jit(solution)/shard_map/ppermute | solution.py:261
  86.5 22.7 %collective-permute-start.12 = (bf16[8,128,128]{2,1,0:T(8,128)(2,1)S(1)}, bf16[8,128,128]{2,1,0:T(8,128)(2,1)S(1)}, u32[]{:S(2)}, u32[]{:S(2)}) collective-permute-start(bf16[8,128,128]{2,1,0:T(8,128)(2,1)S(1)} %get-tuple-element.45), channel_id=1, source_target_pairs={{0,4},{1,5},{2,6},{3,7},{124,120},{125,121},{126,122},{127,123},{1... | collective-permute-start | bytes 786440 | tf_op jit(solution)/shard_map/ppermute | solution.py:261
  99.3 9.8 %collective-permute-start.13 = (bf16[3,128,128]{2,1,0:T(8,128)(2,1)S(1)}, bf16[3,128,128]{2,1,0:T(8,128)(2,1)S(1)}, u32[]{:S(2)}, u32[]{:S(2)}) collective-permute-start(bf16[3,128,128]{2,1,0:T(8,128)(2,1)S(1)} %get-tuple-element.46), channel_id=1, source_target_pairs={{0,16},{1,17},{2,502},{3,503},{8,24},{9,25},{10,510},{11,511},{16,... | collective-permute-start | bytes 294920 | tf_op jit(solution)/shard_map/ppermute | solution.py:261

commit v5 on v4

--- a/solution.py
+++ b/solution.py
@@ -21,12 +21,8 @@
     return (row % n, offset) if offset >= 0 else ((row + offset) % n, -offset)
 
 
-def own_lists(lower, p):
-    if lower:
-        same = list(range(-p, 1)) + list(range(-8, -4 - p))
-    else:
-        same = list(range(0, 4 - p)) + list(range(8 - p, 9))
-    return same, list(range(-p - 4, -p)) + list(range(4 - p, 8 - p))
+def own_lists(p):
+    return list(range(0, 4 - p)) + list(range(8 - p, 9)), list(range(-p - 4, -p)) + list(range(4 - p, 8 - p))
 
 
 def make_plan(ny, nzl):
@@ -47,10 +43,9 @@
         return list(blocks) + [None] * (k - len(blocks))
 
     need = [{((i - KEEP_HALF + u) % n, o): u * UPPER + o for u in range(KEPT) for o in range(UPPER) if u + o < KEPT} for i in range(n)]
-    lists = [own_lists(zh == 0, x) for y, zl, c, zh, x in coords]
-    over = [own_lists(zh == 1, x)[0] for y, zl, c, zh, x in coords]
+    lists = [own_lists(x) for y, zl, c, zh, x in coords]
     own = [[canonical(i, o, n) for o in range(-8, 9)] for i in range(n)]
-    sent1 = [[canonical(i, o, n) for o in same] for i, same in enumerate(over)]
+    sent1 = [[canonical(i, o, n) for o in same] for i, (same, _) in enumerate(lists)]
     sent2 = [[canonical(i, o, n) for o in same + mixed] for i, (same, mixed) in enumerate(lists)]
     moves = {}
     moves["zh"] = [(i, place(y, zl, c, 1 - zh, x)) for i, (y, zl, c, zh, x) in enumerate(coords)]
@@ -101,14 +96,13 @@
     sent_s, got_s = choose("seam", stock2)
     sent_a, got_a = choose("z", stock2)
     sent_b, got_b = choose("z", stock4)
-    sent_t, got_t = choose("seam", stock4)
     sent_f, got_f = choose("far", stock4)
     assert all(set(need[d]) <= known[d] for d in range(n))
 
     def where(sends, stock):
         return np.array([[src.index(b) if b is not None else 0 for b in q] for q, src in zip(sends, stock)], np.int32)
 
-    arrived = join(stock4, got_d, got_s, got_a, got_b, got_t, got_f)
+    arrived = join(stock4, got_s, got_a, got_d, got_b, got_f)
     spots = np.full((n, len(arrived[0])), DUMMY, np.int32)
     for i in range(n):
         seen = set()
@@ -116,7 +110,7 @@
             if b in need[i] and b not in seen:
                 seen.add(b)
                 spots[i, k] = need[i][b]
-    parts = [where(sent1, own), where(sent2, own), where(sent_s, stock2), where(sent_a, stock2), where(sent_b, stock4), where(sent_t, stock4), where(sent_f, stock4), spots]
+    parts = [where(sent1, own), where(sent2, own), where(sent_s, stock2), where(sent_a, stock2), where(sent_b, stock4), where(sent_f, stock4), spots]
     starts = np.cumsum([0] + [q.shape[1] for q in parts])
     return moves, np.concatenate(parts, axis=1), [q.shape[1] for q in parts], [int(q) for q in starts]
 
@@ -185,8 +179,8 @@
     concatenate([send2, x1, x2, x3], both)
 
 
-def third_kernel(start, table, own, x1, x2, x3, got1, w1, w2, w3, got_c, z, seam, far, both):
-    gather(start, table, [own, x1, x2, x3, got1, w1, w2, w3, got_c], [z, seam, far])
+def third_kernel(start, table, own, x1, x2, x3, got1, w1, w2, w3, got_c, z, far, both):
+    gather(start, table, [own, x1, x2, x3, got1, w1, w2, w3, got_c], [z, far])
     concatenate([got1, w1, w2, w3], both)
 
 
@@ -222,12 +216,10 @@
     return jnp.concatenate([jnp.full((1, BLK), keep[0, v + j].astype(jnp.float32)) for j in range(width)], axis=1)
 
 
-def final_kernel(start, spots, keep, masked, *refs):
-    *sources, out, pool, square, rounded = refs
-    low = start
+def place(low, spots, sources, pool):
     for source in sources:
 
-        def place(k, carry, source=source, low=low):
+        def put(k, carry, source=source, low=low):
             at = spots[low + k]
 
             @pl.when(at < DUMMY)
@@ -236,8 +228,17 @@
 
             return carry
 
-        lax.fori_loop(0, source.shape[0], place, 0)
+        lax.fori_loop(0, source.shape[0], put, 0)
         low += source.shape[0]
+
+
+def early_kernel(start, spots, *refs):
+    place(start, spots, refs[:-1], refs[-1])
+
+
+def final_kernel(start, spots, keep, masked, *refs):
+    *sources, _, out, pool, square, rounded = refs
+    place(start, spots, sources, pool)
     groups = [(v, min(2, KEPT - v)) for v in range(0, KEPT, 2)]
     for v, width in groups:
         cols = slice(v * BLK, (v + width) * BLK)
@@ -254,7 +255,7 @@
 def solution(mesh):
     ny, nzl = mesh.shape["row"], mesh.shape["col"] // 2
     moves, tables, counts, starts = make_plan(ny, nzl)
-    k1, k2, ks, ka, kb, kt, kf, _ = counts
+    k1, k2, ks, ka, kb, kf, _ = counts
     fine = Mesh(mesh.devices.reshape(ny, nzl, 2, 2, 4), AXES)
 
     def send(array, name):
@@ -276,19 +277,24 @@
         got_s, got_a, got_c = send(send_s, "seam"), send(send_a, "z"), send(both2, "c")
         w = [send(got1, f"x{step}") for step in (1, 2, 3)]
         *w, got_a, got_c, got_s = lax.optimization_barrier((*w, got_a, got_c, got_s))
-        send_b, send_t, send_f, both3 = call(
+        send_b, send_f, both3 = call(
             functools.partial(third_kernel, starts[4]),
-            (vmem(kb, BLK, BLK), vmem(kt, BLK, BLK), vmem(kf, BLK, BLK), vmem(4 * k1, BLK, BLK)), 1, 9,
+            (vmem(kb, BLK, BLK), vmem(kf, BLK, BLK), vmem(4 * k1, BLK, BLK)), 1, 9,
         )(table, own, *x, got1, *w, got_c)
-        got_b, got_t, got_f, got_d = send(send_b, "z"), send(send_t, "seam"), send(send_f, "far"), send(both3, "c")
-        return call(
-            functools.partial(final_kernel, starts[7]), vmem(1, BLK, KEPT * BLK, dtype=jnp.float32), 2, 16,
-            [
-                pltpu.VMEM((DUMMY, BLK, BLK), jnp.bfloat16),
-                pltpu.VMEM((BLK, KEPT * BLK), jnp.float32),
-                pltpu.VMEM((BLK, KEPT * BLK), jnp.bfloat16),
-            ], 24,
-        )(table, keep, masked, own, *x, got1, *w, got_c, got_d, got_s, got_a, got_b, got_t, got_f)
+        got_b, got_f, got_d = send(send_b, "z"), send(send_f, "far"), send(both3, "c")
+        first = [own, *x, got1, *w, got_c, got_s, got_a]
+        pool = call(functools.partial(early_kernel, starts[6]), vmem(DUMMY, BLK, BLK), 1, len(first))(table, *first)
+        late = starts[6] + sum(q.shape[0] for q in first)
+        purified, _ = pl.pallas_call(
+            functools.partial(final_kernel, late),
+            out_shape=(vmem(1, BLK, KEPT * BLK, dtype=jnp.float32), vmem(DUMMY, BLK, BLK)),
+            in_specs=[scalars()] * 2 + [whole()] * 5,
+            out_specs=(whole(), whole()),
+            scratch_shapes=[pltpu.VMEM((BLK, KEPT * BLK), jnp.float32), pltpu.VMEM((BLK, KEPT * BLK), jnp.bfloat16)],
+            input_output_aliases={6: 1},
+            compiler_params=pltpu.CompilerParams(vmem_limit_bytes=24 << 20),
+        )(table, keep, masked, got_d, got_b, got_f, pool)
+        return purified
 
     return jax.shard_map(
         body,

time: 119 us -> 113 us (0.950)
  the two profiles are of different devices: /device:TPU:2 before, /device:TPU:1 now
where the time goes in v5:
time: 113 us; the launch traced here: 112 us
  starting transfers between devices  70 us (62%)
  waiting for transfers between devices  22.7 us (20%)
  Pallas kernels  16.7 us (15%)
  local copies, waits for them, and re-layouts  2.43 us (2%)
    ppermute x13, starting transfers between devices, send(): return lax.ppermute(array, AXES, moves[name])  70 us
    ppermute x13, waiting for transfers between devices, send(): return lax.ppermute(array, AXES, moves[name])  22.7 us
    pallas_call x1, Pallas kernels, body(): pl.pallas_call(functools.partial(final_kernel, late), out_shape=(vmem(1,...  6.8 us
    pallas_call x1, Pallas kernels, body(): call(functools.partial(early_kernel, starts[6]), vmem(DUMMY, BLK, BLK), 1...  3.26 us
    pallas_call x1, Pallas kernels, body(): call(functools.partial(third_kernel, starts[4]), (vmem(kb, BLK, BLK), vme...  3.17 us
    pallas_call x1, Pallas kernels, body(): call(functools.partial(second_kernel, starts[2]), (vmem(ks, BLK, BLK), vm...  2.53 us
  transfers between devices with their start and end apart: 13, of which 5 were waited for; matrix products, arithmetic and copies ran while one was open for 0% of the time, Pallas kernels for 5%

profile of v5, /device:TPU:1, one launch (start us, length us, event | category | flops | bytes accessed | tf_op | source)
XLA Modules:
  0.0 112.1 jit_solution(8867890276858040908)
XLA Ops:
  0.0 0.7 dynamic-slice_reduce_fusion.table.spots
  0.7 1.0 copy-done
  2.4 1.0 shard_map.46
  3.4 5.2 %collective-permute-start.2 = (bf16[13,128,128]{2,1,0:T(8,128)(2,1)S(1)}, bf16[13,128,128]{2,1,0:T(8,128)(2,1)S(1)}, u32[]{:S(2)}, u32[]{:S(2)}) collective-permute-start(bf16[13,128,128]{2,1,0:T(8,128)(2,1)S(1)} %get-tuple-element.28.send2), channel_id=1, source_target_pairs={{0,3},{1,0},{2,1},{3,2},{4,7},{5,4},{6,5},{7,6},{8,11},{9,8},{10,9... | collective-permute-start | bytes 1277960 | tf_op jit(solution)/shard_map/ppermute | solution.py:262
  8.7 2.4 %collective-permute-start.1 = (bf16[13,128,128]{2,1,0:T(8,128)(2,1)S(1)}, bf16[13,128,128]{2,1,0:T(8,128)(2,1)S(1)}, u32[]{:S(2)}, u32[]{:S(2)}) collective-permute-start(bf16[13,128,128]{2,1,0:T(8,128)(2,1)S(1)} %get-tuple-element.28.send2), channel_id=1, source_target_pairs={{0,2},{1,3},{2,0},{3,1},{4,6},{5,7},{6,4},{7,5},{8,10},{9,11},{10,... | collective-permute-start | bytes 1277960 | tf_op jit(solution)/shard_map/ppermute | solution.py:262
  11.1 2.5 %collective-permute-start = (bf16[13,128,128]{2,1,0:T(8,128)(2,1)S(1)}, bf16[13,128,128]{2,1,0:T(8,128)(2,1)S(1)}, u32[]{:S(2)}, u32[]{:S(2)}) collective-permute-start(bf16[13,128,128]{2,1,0:T(8,128)(2,1)S(1)} %get-tuple-element.28.send2), channel_id=1, source_target_pairs={{0,1},{1,2},{2,3},{3,0},{4,5},{5,6},{6,7},{7,4},{8,9},{9,10},{10,1... | collective-permute-start | bytes 1277960 | tf_op jit(solution)/shard_map/ppermute | solution.py:262
  13.6 15.4 %collective-permute-start.3 = (bf16[5,128,128]{2,1,0:T(8,128)(2,1)S(1)}, bf16[5,128,128]{2,1,0:T(8,128)(2,1)S(1)}, u32[]{:S(2)}, u32[]{:S(2)}) collective-permute-start(bf16[5,128,128]{2,1,0:T(8,128)(2,1)S(1)} %get-tuple-element.29), channel_id=1, source_target_pairs={{0,4},{1,5},{2,6},{3,7},{4,0},{5,1},{6,2},{7,3},{8,12},{9,13},{10,... | collective-permute-start | bytes 491528 | tf_op jit(solution)/shard_map/ppermute | solution.py:262
  29.1 2.8 %collective-permute-done.x1.refs_1_ = bf16[13,128,128]{2,1,0:T(8,128)(2,1)S(1)} collective-permute-done((bf16[13,128,128]{2,1,0:T(8,128)(2,1)S(1)}, bf16[13,128,128]{2,1,0:T(8,128)(2,1)S(1)}, u32[]{:S(2)}, u32[]{:S(2)}) %collective-permute-start) | collective-permute-done | bytes 426016 | tf_op jit(solution)/shard_map/ppermute | solution.py:262
  31.9 2.5 %shard_map.47 = (bf16[18,128,128]{2,1,0:T(8,128)(2,1)S(1)}, bf16[40,128,128]{2,1,0:T(8,128)(2,1)S(1)}, bf16[52,128,128]{2,1,0:T(8,128)(2,1)S(1)}) custom-call(s32[366]{0:T(512)S(1)} %dynamic-slice_reduce_fusion.table.spots, bf16[17,128,128]{2,1,0:T(8,128)(2,1)S(1)} %get-tuple-element.27.own.refs_0_, bf16[13,128,128]{2,1,0:T(8,128)(2,1)S(1)} %get-tuple-element.28.send2, ...), custom_call_target="tpu_custom_call" | custom-call | tf_op jit(solution)/shard_map/pallas_call | solution.py:272
  34.4 3.4 %collective-permute-start.8 = (bf16[52,128,128]{2,1,0:T(8,128)(2,1)S(1)}, bf16[52,128,128]{2,1,0:T(8,128)(2,1)S(1)}, u32[]{:S(2)}, u32[]{:S(2)}) collective-permute-start(bf16[52,128,128]{2,1,0:T(8,128)(2,1)S(1)} %get-tuple-element.35), channel_id=1, source_target_pairs={{0,8},{1,9},{2,10},{3,11},{4,12},{5,13},{6,14},{7,15},{8,0},{9,1},... | collective-permute-start | bytes 5111816 | tf_op jit(solution)/shard_map/ppermute | solution.py:262
  37.9 10.2 %collective-permute-start.7 = (bf16[40,128,128]{2,1,0:T(8,128)(2,1)S(1)}, bf16[40,128,128]{2,1,0:T(8,128)(2,1)S(1)}, u32[]{:S(2)}, u32[]{:S(2)}) collective-permute-start(bf16[40,128,128]{2,1,0:T(8,128)(2,1)S(1)} %get-tuple-element.34), channel_id=1, source_target_pairs={{0,508},{1,509},{2,510},{3,511},{4,504},{5,505},{6,506},{7,507},{8... | collective-permute-start | bytes 3932168 | tf_op jit(solution)/shard_map/ppermute | solution.py:262
  48.8 4.0 %collective-permute-start.6 = (bf16[5,128,128]{2,1,0:T(8,128)(2,1)S(1)}, bf16[5,128,128]{2,1,0:T(8,128)(2,1)S(1)}, u32[]{:S(2)}, u32[]{:S(2)}) collective-permute-start(bf16[5,128,128]{2,1,0:T(8,128)(2,1)S(1)} %collective-permute-done.3.got1.refs_4_), channel_id=1, source_target_pairs={{0,3},{1,0},{2,1},{3,2},{4,7},{5,4},{6,5},{7,6},{8,11},{9,8},{10,9... | collective-permute-start | bytes 491528 | tf_op jit(solution)/shard_map/ppermute | solution.py:262
  52.7 3.1 %collective-permute-start.5 = (bf16[5,128,128]{2,1,0:T(8,128)(2,1)S(1)}, bf16[5,128,128]{2,1,0:T(8,128)(2,1)S(1)}, u32[]{:S(2)}, u32[]{:S(2)}) collective-permute-start(bf16[5,128,128]{2,1,0:T(8,128)(2,1)S(1)} %collective-permute-done.3.got1.refs_4_), channel_id=1, source_target_pairs={{0,2},{1,3},{2,0},{3,1},{4,6},{5,7},{6,4},{7,5},{8,10},{9,11},{10,... | collective-permute-start | bytes 491528 | tf_op jit(solution)/shard_map/ppermute | solution.py:262
  55.9 2.6 %collective-permute-start.4 = (bf16[5,128,128]{2,1,0:T(8,128)(2,1)S(1)}, bf16[5,128,128]{2,1,0:T(8,128)(2,1)S(1)}, u32[]{:S(2)}, u32[]{:S(2)}) collective-permute-start(bf16[5,128,128]{2,1,0:T(8,128)(2,1)S(1)} %collective-permute-done.3.got1.refs_4_), channel_id=1, source_target_pairs={{0,1},{1,2},{2,3},{3,0},{4,5},{5,6},{6,7},{7,4},{8,9},{9,10},{10,1... | collective-permute-start | bytes 491528 | tf_op jit(solution)/shard_map/ppermute | solution.py:262
  58.5 2.1 %collective-permute-done.5.w2.refs_6_ = bf16[5,128,128]{2,1,0:T(8,128)(2,1)S(1)} collective-permute-done((bf16[5,128,128]{2,1,0:T(8,128)(2,1)S(1)}, bf16[5,128,128]{2,1,0:T(8,128)(2,1)S(1)}, u32[]{:S(2)}, u32[]{:S(2)}) %collective-permute-start.5) | collective-permute-done | bytes 163872 | tf_op jit(solution)/shard_map/ppermute | solution.py:262
  60.6 2.9 %collective-permute-done.4.w1.refs_5_ = bf16[5,128,128]{2,1,0:T(8,128)(2,1)S(1)} collective-permute-done((bf16[5,128,128]{2,1,0:T(8,128)(2,1)S(1)}, bf16[5,128,128]{2,1,0:T(8,128)(2,1)S(1)}, u32[]{:S(2)}, u32[]{:S(2)}) %collective-permute-start.4) | collective-permute-done | bytes 163872 | tf_op jit(solution)/shard_map/ppermute | solution.py:262
  63.5 0.8 collective-permute-done.7.refs_10_
  64.2 3.2 %shard_map.48 = (bf16[32,128,128]{2,1,0:T(8,128)(2,1)S(1)}, bf16[10,128,128]{2,1,0:T(8,128)(2,1)S(1)}, bf16[20,128,128]{2,1,0:T(8,128)(2,1)S(1)}) custom-call(s32[366]{0:T(512)S(1)} %dynamic-slice_reduce_fusion.table.spots, bf16[17,128,128]{2,1,0:T(8,128)(2,1)S(1)} %get-tuple-element.27.own.refs_0_, ...), custom_call_target="tpu_custom_call" | custom-call | tf_op jit(solution)/shard_map/pallas_call | solution.py:280
  67.4 8.0 %collective-permute-start.11 = (bf16[32,128,128]{2,1,0:T(8,128)(2,1)S(1)}, bf16[32,128,128]{2,1,0:T(8,128)(2,1)S(1)}, u32[]{:S(2)}, u32[]{:S(2)}) collective-permute-start(bf16[32,128,128]{2,1,0:T(8,128)(2,1)S(1)} %get-tuple-element.42), channel_id=1, source_target_pairs={{0,508},{1,509},{2,510},{3,511},{4,504},{5,505},{6,506},{7,507},{8... | collective-permute-start | bytes 3145736 | tf_op jit(solution)/shard_map/ppermute | solution.py:262
  75.4 10.5 %collective-permute-start.10 = (bf16[20,128,128]{2,1,0:T(8,128)(2,1)S(1)}, bf16[20,128,128]{2,1,0:T(8,128)(2,1)S(1)}, u32[]{:S(2)}, u32[]{:S(2)}) collective-permute-start(bf16[20,128,128]{2,1,0:T(8,128)(2,1)S(1)} %get-tuple-element.41), channel_id=1, source_target_pairs={{0,8},{1,9},{2,10},{3,11},{4,12},{5,13},{6,14},{7,15},{8,0},{9,1},... | collective-permute-start | bytes 1966088 | tf_op jit(solution)/shard_map/ppermute | solution.py:262
  85.9 1.9 %collective-permute-start.12 = (bf16[10,128,128]{2,1,0:T(8,128)(2,1)S(1)}, bf16[10,128,128]{2,1,0:T(8,128)(2,1)S(1)}, u32[]{:S(2)}, u32[]{:S(2)}) collective-permute-start(bf16[10,128,128]{2,1,0:T(8,128)(2,1)S(1)} %get-tuple-element.43), channel_id=1, source_target_pairs={{0,16},{1,17},{2,502},{3,503},{8,24},{9,25},{10,510},{11,511},{16,... | collective-permute-start | bytes 983048 | tf_op jit(solution)/shard_map/ppermute | solution.py:262
  87.9 3.3 %shard_map.49.refs_3_ = bf16[189,128,128]{2,1,0:T(8,128)(2,1)S(1)} custom-call(s32[366]{0:T(512)S(1)} %dynamic-slice_reduce_fusion.table.spots, bf16[17,128,128]{2,1,0:T(8,128)(2,1)S(1)} %get-tuple-element.27.own.refs_0_, bf16[13,128,128]{2,1,0:T(8,128)(2,1)S(1)} %collective-permute-done.x1.refs_1_, ...), custom_call_target="tpu_custom_call" | custom-call | tf_op jit(solution)/shard_map/pallas_call | solution.py:286
  91.1 14.2 %collective-permute-done.12.refs_2_ = bf16[10,128,128]{2,1,0:T(8,128)(2,1)S(1)} collective-permute-done((bf16[10,128,128]{2,1,0:T(8,128)(2,1)S(1)}, bf16[10,128,128]{2,1,0:T(8,128)(2,1)S(1)}, u32[]{:S(2)}, u32[]{:S(2)}) %collective-permute-start.12) | collective-permute-done | bytes 327712 | tf_op jit(solution)/shard_map/ppermute | solution.py:262
  105.3 6.8 %shard_map.50 = (f32[1,128,2688]{2,1,0:T(8,128)}, bf16[189,128,128]{2,1,0:T(8,128)(2,1)S(1)}) custom-call(s32[366]{0:T(512)S(1)} %dynamic-slice_reduce_fusion.table.spots, s32[1,21]{1,0:T(1,128)S(1)} %copy-done.2, bf16[128,2176]{1,0:T(8,128)(2,1)S(1)} %get-tuple-element.26.masked, ...), custom_call_target="tpu_custom_call", output_to_operand_aliasing={{1}: (6, {})} | custom-call | tf_op jit(solution)/shard_map/pallas_call | solution.py:288
  (14 shorter events, 1.4 us)
Async XLA Ops:
  0.7 1.1 copy-start
  1.8 0.7 copy-start.1
  3.4 25.6 %collective-permute-start.2 = (bf16[13,128,128]{2,1,0:T(8,128)(2,1)S(1)}, bf16[13,128,128]{2,1,0:T(8,128)(2,1)S(1)}, u32[]{:S(2)}, u32[]{:S(2)}) collective-permute-start(bf16[13,128,128]{2,1,0:T(8,128)(2,1)S(1)} %get-tuple-element.28.send2), channel_id=1, source_target_pairs={{0,3},{1,0},{2,1},{3,2},{4,7},{5,4},{6,5},{7,6},{8,11},{9,8},{10,9... | collective-permute-start | bytes 1277960 | tf_op jit(solution)/shard_map/ppermute | solution.py:262
  8.7 20.4 %collective-permute-start.1 = (bf16[13,128,128]{2,1,0:T(8,128)(2,1)S(1)}, bf16[13,128,128]{2,1,0:T(8,128)(2,1)S(1)}, u32[]{:S(2)}, u32[]{:S(2)}) collective-permute-start(bf16[13,128,128]{2,1,0:T(8,128)(2,1)S(1)} %get-tuple-element.28.send2), channel_id=1, source_target_pairs={{0,2},{1,3},{2,0},{3,1},{4,6},{5,7},{6,4},{7,5},{8,10},{9,11},{10,... | collective-permute-start | bytes 1277960 | tf_op jit(solution)/shard_map/ppermute | solution.py:262
  11.1 20.8 %collective-permute-start = (bf16[13,128,128]{2,1,0:T(8,128)(2,1)S(1)}, bf16[13,128,128]{2,1,0:T(8,128)(2,1)S(1)}, u32[]{:S(2)}, u32[]{:S(2)}) collective-permute-start(bf16[13,128,128]{2,1,0:T(8,128)(2,1)S(1)} %get-tuple-element.28.send2), channel_id=1, source_target_pairs={{0,1},{1,2},{2,3},{3,0},{4,5},{5,6},{6,7},{7,4},{8,9},{9,10},{10,1... | collective-permute-start | bytes 1277960 | tf_op jit(solution)/shard_map/ppermute | solution.py:262
  13.6 20.8 %collective-permute-start.3 = (bf16[5,128,128]{2,1,0:T(8,128)(2,1)S(1)}, bf16[5,128,128]{2,1,0:T(8,128)(2,1)S(1)}, u32[]{:S(2)}, u32[]{:S(2)}) collective-permute-start(bf16[5,128,128]{2,1,0:T(8,128)(2,1)S(1)} %get-tuple-element.29), channel_id=1, source_target_pairs={{0,4},{1,5},{2,6},{3,7},{4,0},{5,1},{6,2},{7,3},{8,12},{9,13},{10,... | collective-permute-start | bytes 491528 | tf_op jit(solution)/shard_map/ppermute | solution.py:262
  34.4 29.8 %collective-permute-start.8 = (bf16[52,128,128]{2,1,0:T(8,128)(2,1)S(1)}, bf16[52,128,128]{2,1,0:T(8,128)(2,1)S(1)}, u32[]{:S(2)}, u32[]{:S(2)}) collective-permute-start(bf16[52,128,128]{2,1,0:T(8,128)(2,1)S(1)} %get-tuple-element.35), channel_id=1, source_target_pairs={{0,8},{1,9},{2,10},{3,11},{4,12},{5,13},{6,14},{7,15},{8,0},{9,1},... | collective-permute-start | bytes 5111816 | tf_op jit(solution)/shard_map/ppermute | solution.py:262
  37.9 26.4 %collective-permute-start.7 = (bf16[40,128,128]{2,1,0:T(8,128)(2,1)S(1)}, bf16[40,128,128]{2,1,0:T(8,128)(2,1)S(1)}, u32[]{:S(2)}, u32[]{:S(2)}) collective-permute-start(bf16[40,128,128]{2,1,0:T(8,128)(2,1)S(1)} %get-tuple-element.34), channel_id=1, source_target_pairs={{0,508},{1,509},{2,510},{3,511},{4,504},{5,505},{6,506},{7,507},{8... | collective-permute-start | bytes 3932168 | tf_op jit(solution)/shard_map/ppermute | solution.py:262
  48.0 15.4 %collective-permute-start.9 = (bf16[18,128,128]{2,1,0:T(8,128)(2,1)S(1)}, bf16[18,128,128]{2,1,0:T(8,128)(2,1)S(1)}, u32[]{:S(2)}, u32[]{:S(2)}) collective-permute-start(bf16[18,128,128]{2,1,0:T(8,128)(2,1)S(1)} %get-tuple-element.36), channel_id=1, source_target_pairs={{0,4},{1,5},{2,6},{3,7},{124,120},{125,121},{126,122},{127,123},{1... | collective-permute-start | bytes 1769480 | tf_op jit(solution)/shard_map/ppermute | solution.py:262
  48.8 7.1 %collective-permute-start.6 = (bf16[5,128,128]{2,1,0:T(8,128)(2,1)S(1)}, bf16[5,128,128]{2,1,0:T(8,128)(2,1)S(1)}, u32[]{:S(2)}, u32[]{:S(2)}) collective-permute-start(bf16[5,128,128]{2,1,0:T(8,128)(2,1)S(1)} %collective-permute-done.3.got1.refs_4_), channel_id=1, source_target_pairs={{0,3},{1,0},{2,1},{3,2},{4,7},{5,4},{6,5},{7,6},{8,11},{9,8},{10,9... | collective-permute-start | bytes 491528 | tf_op jit(solution)/shard_map/ppermute | solution.py:262
  52.7 7.9 %collective-permute-start.5 = (bf16[5,128,128]{2,1,0:T(8,128)(2,1)S(1)}, bf16[5,128,128]{2,1,0:T(8,128)(2,1)S(1)}, u32[]{:S(2)}, u32[]{:S(2)}) collective-permute-start(bf16[5,128,128]{2,1,0:T(8,128)(2,1)S(1)} %collective-permute-done.3.got1.refs_4_), channel_id=1, source_target_pairs={{0,2},{1,3},{2,0},{3,1},{4,6},{5,7},{6,4},{7,5},{8,10},{9,11},{10,... | collective-permute-start | bytes 491528 | tf_op jit(solution)/shard_map/ppermute | solution.py:262
  55.9 7.6 %collective-permute-start.4 = (bf16[5,128,128]{2,1,0:T(8,128)(2,1)S(1)}, bf16[5,128,128]{2,1,0:T(8,128)(2,1)S(1)}, u32[]{:S(2)}, u32[]{:S(2)}) collective-permute-start(bf16[5,128,128]{2,1,0:T(8,128)(2,1)S(1)} %collective-permute-done.3.got1.refs_4_), channel_id=1, source_target_pairs={{0,1},{1,2},{2,3},{3,0},{4,5},{5,6},{6,7},{7,4},{8,9},{9,10},{10,1... | collective-permute-start | bytes 491528 | tf_op jit(solution)/shard_map/ppermute | solution.py:262
  67.4 37.9 %collective-permute-start.11 = (bf16[32,128,128]{2,1,0:T(8,128)(2,1)S(1)}, bf16[32,128,128]{2,1,0:T(8,128)(2,1)S(1)}, u32[]{:S(2)}, u32[]{:S(2)}) collective-permute-start(bf16[32,128,128]{2,1,0:T(8,128)(2,1)S(1)} %get-tuple-element.42), channel_id=1, source_target_pairs={{0,508},{1,509},{2,510},{3,511},{4,504},{5,505},{6,506},{7,507},{8... | collective-permute-start | bytes 3145736 | tf_op jit(solution)/shard_map/ppermute | solution.py:262
  75.4 29.9 %collective-permute-start.10 = (bf16[20,128,128]{2,1,0:T(8,128)(2,1)S(1)}, bf16[20,128,128]{2,1,0:T(8,128)(2,1)S(1)}, u32[]{:S(2)}, u32[]{:S(2)}) collective-permute-start(bf16[20,128,128]{2,1,0:T(8,128)(2,1)S(1)} %get-tuple-element.41), channel_id=1, source_target_pairs={{0,8},{1,9},{2,10},{3,11},{4,12},{5,13},{6,14},{7,15},{8,0},{9,1},... | collective-permute-start | bytes 1966088 | tf_op jit(solution)/shard_map/ppermute | solution.py:262
  85.9 19.4 %copy-start.2 = (s32[1,21]{1,0:T(1,128)S(1)}, s32[1,21]{1,0:T(1,128)}, u32[]{:S(2)}) copy-start(s32[1,21]{1,0:T(1,128)} %keep.1) | copy-start | bytes 256
  85.9 19.4 %collective-permute-start.12 = (bf16[10,128,128]{2,1,0:T(8,128)(2,1)S(1)}, bf16[10,128,128]{2,1,0:T(8,128)(2,1)S(1)}, u32[]{:S(2)}, u32[]{:S(2)}) collective-permute-start(bf16[10,128,128]{2,1,0:T(8,128)(2,1)S(1)} %get-tuple-element.43), channel_id=1, source_target_pairs={{0,16},{1,17},{2,502},{3,503},{8,24},{9,25},{10,510},{11,511},{16,... | collective-permute-start | bytes 983048 | tf_op jit(solution)/shard_map/ppermute | solution.py:262

commit v6 on v5

--- a/solution.py
+++ b/solution.py
@@ -50,8 +50,6 @@
     moves = {}
     moves["zh"] = [(i, place(y, zl, c, 1 - zh, x)) for i, (y, zl, c, zh, x) in enumerate(coords)]
     moves["c"] = [(i, place(y, zl, 1 - c, zh, x)) for i, (y, zl, c, zh, x) in enumerate(coords)]
-    for step in (1, 2, 3):
-        moves[f"x{step}"] = [(i, place(y, zl, c, zh, x + step)) for i, (y, zl, c, zh, x) in enumerate(coords)]
     moves["seam"], moves["z"], moves["far"] = [], [], []
     for i, (y, zl, c, zh, x) in enumerate(coords):
         if (zl, c, zh) in ((0, 0, 0), (nzl - 1, 1, 1)):
@@ -73,12 +71,12 @@
         return [sum(row, []) for row in zip(*parts)]
 
     got1 = moved(sent1, "zh")
-    got2 = [moved(sent2, f"x{s}") for s in (1, 2, 3)]
-    got3 = [moved(got1, f"x{s}") for s in (1, 2, 3)]
+    got2 = [[sum([sent2[i - i % 4 + q] for q in range(4)], []) for i in range(n)]]
+    got3 = [[sum([got1[i - i % 4 + q] for q in range(4)], []) for i in range(n)]]
     stock2 = join(own, *got2)
-    stock3 = join(stock2, got1, *got3)
-    got_c = moved(join(sent2, *got2), "c")
-    got_d = moved(join(got1, *got3), "c")
+    stock3 = join(stock2, *got3)
+    got_c = moved(join(*got2), "c")
+    got_d = moved(join(*got3), "c")
     stock4 = join(stock3, got_c)
     known = [set(row) for row in join(stock4, got_d)]
 
@@ -144,7 +142,16 @@
         block = strip[0, :, cols] * pattern[0, slot].astype(jnp.bfloat16)
         masked[:, cols] = block
         own[slot] = block if slot >= BAND_HALF else block.T
-    gather(start, table, [own], [send1, send2])
+    gather(start, table, [own], [send1])
+    start += send1.shape[0]
+
+    def pack(k, carry):
+        block = own[table[start + k]]
+        for peer in range(4):
+            send2[peer, k] = block
+        return carry
+
+    lax.fori_loop(0, send2.shape[1], pack, 0)
 
 
 def gather(start, table, sources, outs):
@@ -167,21 +174,8 @@
         start += out.shape[0]
 
 
-def concatenate(sources, out):
-    low = 0
-    for source in sources:
-        out[low : low + source.shape[0]] = source[...]
-        low += source.shape[0]
-
-
-def second_kernel(start, table, own, send2, x1, x2, x3, seam, z, both):
-    gather(start, table, [own, x1, x2, x3], [seam, z])
-    concatenate([send2, x1, x2, x3], both)
-
-
-def third_kernel(start, table, own, x1, x2, x3, got1, w1, w2, w3, got_c, z, far, both):
-    gather(start, table, [own, x1, x2, x3, got1, w1, w2, w3, got_c], [z, far])
-    concatenate([got1, w1, w2, w3], both)
+def gather_kernel(n_sources, start, table, *refs):
+    gather(start, table, refs[:n_sources], refs[n_sources:])
 
 
 def product(left, first, pool, v, width):
@@ -261,28 +255,29 @@
     def send(array, name):
         return lax.ppermute(array, AXES, moves[name])
 
+    def spread(copies):
+        return lax.all_to_all(copies, "x", 0, 0).reshape(-1, BLK, BLK)
+
     def body(density, pattern, keep):
         table = lax.dynamic_index_in_dim(jnp.asarray(tables), lax.axis_index(AXES), 0, keepdims=False)
         masked, own, send1, send2 = call(
             functools.partial(first_kernel, starts[0]),
-            (vmem(BLK, 17 * BLK), vmem(17, BLK, BLK), vmem(k1, BLK, BLK), vmem(k2, BLK, BLK)), 2, 1,
+            (vmem(BLK, 17 * BLK), vmem(17, BLK, BLK), vmem(k1, BLK, BLK), vmem(4, k2, BLK, BLK)), 2, 1,
         )(table, pattern, density)
-        x = [send(send2, f"x{step}") for step in (1, 2, 3)]
         got1 = send(send1, "zh")
-        send_s, send_a, both2 = call(
-            functools.partial(second_kernel, starts[2]),
-            (vmem(ks, BLK, BLK), vmem(ka, BLK, BLK), vmem(4 * k2, BLK, BLK)), 1, 5,
-        )(table, own, send2, *x)
-        got1, send_s, send_a, both2 = lax.optimization_barrier((got1, send_s, send_a, both2))
-        got_s, got_a, got_c = send(send_s, "seam"), send(send_a, "z"), send(both2, "c")
-        w = [send(got1, f"x{step}") for step in (1, 2, 3)]
-        *w, got_a, got_c, got_s = lax.optimization_barrier((*w, got_a, got_c, got_s))
-        send_b, send_f, both3 = call(
-            functools.partial(third_kernel, starts[4]),
-            (vmem(kb, BLK, BLK), vmem(kf, BLK, BLK), vmem(4 * k1, BLK, BLK)), 1, 9,
-        )(table, own, *x, got1, *w, got_c)
-        got_b, got_f, got_d = send(send_b, "z"), send(send_f, "far"), send(both3, "c")
-        first = [own, *x, got1, *w, got_c, got_s, got_a]
+        x = spread(send2)
+        send_s, send_a = call(
+            functools.partial(gather_kernel, 2, starts[2]), (vmem(ks, BLK, BLK), vmem(ka, BLK, BLK)), 1, 2,
+        )(table, own, x)
+        got1, send_s, send_a, x = lax.optimization_barrier((got1, send_s, send_a, x))
+        got_s, got_a, got_c = send(send_s, "seam"), send(send_a, "z"), send(x, "c")
+        w = spread(jnp.broadcast_to(got1, (4, k1, BLK, BLK)))
+        w, got_a, got_c, got_s = lax.optimization_barrier((w, got_a, got_c, got_s))
+        send_b, send_f = call(
+            functools.partial(gather_kernel, 4, starts[4]), (vmem(kb, BLK, BLK), vmem(kf, BLK, BLK)), 1, 4,
+        )(table, own, x, w, got_c)
+        got_b, got_f, got_d = send(send_b, "z"), send(send_f, "far"), send(w, "c")
+        first = [own, x, w, got_c, got_s, got_a]
         pool = call(functools.partial(early_kernel, starts[6]), vmem(DUMMY, BLK, BLK), 1, len(first))(table, *first)
         late = starts[6] + sum(q.shape[0] for q in first)
         purified, _ = pl.pallas_call(

time: 113 us -> 104 us (0.920)
  starting transfers between devices: 70 us -> 54.6 us
  blocking collectives: 0 us -> 12 us
  waiting for transfers between devices: 22.7 us -> 18.6 us
  Pallas kernels: 16.7 us -> 14.9 us
  local copies, waits for them, and re-layouts: 2.43 us -> 3.76 us
    ppermute x13 -> x7, starting transfers between devices: 70 us -> 49.8 us  [send(): return lax.ppermute(array, AXES, moves[name])]
    all_to_all x0 -> x1, blocking collectives: none -> 12 us  [spread(): return lax.all_to_all(copies, 'x', 0, 0).reshape(-1, BLK, BLK)]
    ppermute x13 -> x7, waiting for transfers between devices: 22.7 us -> 17.7 us  [send(): return lax.ppermute(array, AXES, moves[name])]
    all_to_all x0 -> x1, starting transfers between devices: none -> 4.84 us  [spread(): return lax.all_to_all(copies, 'x', 0, 0).reshape(-1, BLK, BLK)]
    pallas_call x2, Pallas kernels: 5.71 us -> 3.68 us  [the longest x1 1.92 us: body(): call(functools.partial(gather_kernel, 4, starts[4]), (vmem(kb, BLK, BLK),...]
    unnamed x6 -> x8, local copies, waits for them, and re-layouts: 1.71 us -> 2.9 us
  transfers between devices with their start and end apart: 13 -> 8, of which waited for: 5 -> 4; matrix products, arithmetic and copies ran while one was open for 0% -> 0% of each run, Pallas kernels for 5% -> 5%
where the time goes in v6:
time: 104 us
  starting transfers between devices  54.6 us (52%)
  waiting for transfers between devices  18.6 us (18%)
  Pallas kernels  14.9 us (14%)
  blocking collectives  12 us (12%)
  local copies, waits for them, and re-layouts  3.76 us (4%)
    ppermute x7, starting transfers between devices, send(): return lax.ppermute(array, AXES, moves[name])  49.8 us
    ppermute x7, waiting for transfers between devices, send(): return lax.ppermute(array, AXES, moves[name])  17.7 us
    all_to_all x1, blocking collectives, spread(): return lax.all_to_all(copies, 'x', 0, 0).reshape(-1, BLK, BLK)  12 us
    pallas_call x1, Pallas kernels, body(): pl.pallas_call(functools.partial(final_kernel, late), out_shape=(vmem(1,...  6.71 us
    all_to_all x1, starting transfers between devices, spread(): return lax.all_to_all(copies, 'x', 0, 0).reshape(-1, BLK, BLK)  4.84 us
    pallas_call x1, Pallas kernels, body(): call(functools.partial(early_kernel, starts[6]), vmem(DUMMY, BLK, BLK), 1...  3.46 us
    unnamed x8, local copies, waits for them, and re-layouts  2.9 us
  transfers between devices with their start and end apart: 8, of which 4 were waited for; matrix products, arithmetic and copies ran while one was open for 0% of the time, Pallas kernels for 5%

profile of v6, /device:TPU:1, one launch (start us, length us, event | category | flops | bytes accessed | tf_op | source)
XLA Modules:
  0.0 104.0 jit_solution(4337810605443585191)
XLA Ops:
  0.0 0.7 dynamic-slice_reduce_fusion.table.spots
  0.7 1.0 %copy-done.1 = bf16[1,128,2176]{2,1,0:T(8,128)(2,1)S(1)} copy-done((bf16[1,128,2176]{2,1,0:T(8,128)(2,1)S(1)}, bf16[1,128,2176]{2,1,0:T(8,128)(2,1)}, u32[]{:S(2)}) %copy-start.1) | copy-done | bytes 557080
  1.8 0.7 copy-done.2
  2.4 1.1 %shard_map.46 = (bf16[128,2176]{1,0:T(8,128)(2,1)S(1)}, bf16[17,128,128]{2,1,0:T(8,128)(2,1)S(1)}, bf16[5,128,128]{2,1,0:T(8,128)(2,1)S(1)}, bf16[4,13,128,128]{3,2,1,0:T(8,128)(2,1)S(1)}) custom-call(s32[379]{0:T(512)S(1)} %dynamic-slice_reduce_fusion.table.spots, s32[1,17]{1,0:T(1,128)S(1)} %copy-done.2, bf16[1,128,2176]{2,1,0:T(8,128)(2,1)S(1)} %copy-done.1), custom_call_target="tpu_custom_call" | custom-call | tf_op jit(solution)/shard_map/pallas_call | solution.py:263
  3.5 1.2 %copy-done = bf16[4,13,128,128]{3,2,1,0:T(8,128)(2,1)} copy-done((bf16[4,13,128,128]{3,2,1,0:T(8,128)(2,1)}, bf16[4,13,128,128]{3,2,1,0:T(8,128)(2,1)S(1)}, u32[]{:S(2)}) %copy-start) | copy-done | bytes 1703960
  4.7 4.8 %all-to-all-start = ((bf16[4,13,128,128]{3,2,1,0:T(8,128)(2,1)}), bf16[4,13,128,128]{3,2,1,0:T(8,128)(2,1)S(1)}, u32[]{:S(2)}, u32[]{:S(2)}) async-start(bf16[4,13,128,128]{3,2,1,0:T(8,128)(2,1)} %copy-done), calls=%async_computation | async-start | bytes 3407872 | tf_op jit(solution)/shard_map/all_to_all | solution.py:259
  9.6 15.4 %collective-permute-start = (bf16[5,128,128]{2,1,0:T(8,128)(2,1)S(1)}, bf16[5,128,128]{2,1,0:T(8,128)(2,1)S(1)}, u32[]{:S(2)}, u32[]{:S(2)}) collective-permute-start(bf16[5,128,128]{2,1,0:T(8,128)(2,1)S(1)} %get-tuple-element.23), channel_id=1, source_target_pairs={{0,4},{1,5},{2,6},{3,7},{4,0},{5,1},{6,2},{7,3},{8,12},{9,13},{10,... | collective-permute-start | bytes 491528 | tf_op jit(solution)/shard_map/ppermute | solution.py:256
  25.0 0.8 all-to-all-done
  25.8 1.8 %shard_map.47 = (bf16[18,128,128]{2,1,0:T(8,128)(2,1)S(1)}, bf16[40,128,128]{2,1,0:T(8,128)(2,1)S(1)}) custom-call(s32[379]{0:T(512)S(1)} %dynamic-slice_reduce_fusion.table.spots, bf16[17,128,128]{2,1,0:T(8,128)(2,1)S(1)} %get-tuple-element.24.refs_0_, bf16[52,128,128]{2,1,0:T(8,128)(2,1)S(1)} %bitcast.2), custom_call_target="tpu_custom_call" | custom-call | tf_op jit(solution)/shard_map/pallas_call | solution.py:269
  27.6 0.4 collective-permute-done
  28.0 8.3 %collective-permute-start.2 = (bf16[52,128,128]{2,1,0:T(8,128)(2,1)S(1)}, bf16[52,128,128]{2,1,0:T(8,128)(2,1)S(1)}, u32[]{:S(2)}, u32[]{:S(2)}) collective-permute-start(bf16[52,128,128]{2,1,0:T(8,128)(2,1)S(1)} %bitcast.3), channel_id=1, source_target_pairs={{0,8},{1,9},{2,10},{3,11},{4,12},{5,13},{6,14},{7,15},{8,0},{9,1},... | collective-permute-start | bytes 5111816 | tf_op jit(solution)/shard_map/ppermute | solution.py:256
  36.3 8.0 %collective-permute-start.1 = (bf16[40,128,128]{2,1,0:T(8,128)(2,1)S(1)}, bf16[40,128,128]{2,1,0:T(8,128)(2,1)S(1)}, u32[]{:S(2)}, u32[]{:S(2)}) collective-permute-start(bf16[40,128,128]{2,1,0:T(8,128)(2,1)S(1)} %get-tuple-element.29), channel_id=1, source_target_pairs={{0,508},{1,509},{2,510},{3,511},{4,504},{5,505},{6,506},{7,507},{8... | collective-permute-start | bytes 3932168 | tf_op jit(solution)/shard_map/ppermute | solution.py:256
  44.4 0.7 collective-permute-start.3
  45.1 0.1 broadcast_in_dim.3
  45.2 12.0 %all_to_all.10 = bf16[4,5,128,128]{3,2,1,0:T(8,128)(2,1)S(1)} all-to-all(bf16[4,5,128,128]{3,2,1,0:T(8,128)(2,1)S(1)} %broadcast_in_dim.3), channel_id=1, replica_groups=mesh['y'=4,'zl'=8,'c'=2,'zh'=2,'x'=4] {'x'}, dimensions={0} | all-to-all | bytes 1310720 | tf_op jit(solution)/shard_map/all_to_all | solution.py:259
  57.2 3.2 %collective-permute-done.1.refs_5_ = bf16[40,128,128]{2,1,0:T(8,128)(2,1)S(1)} collective-permute-done((bf16[40,128,128]{2,1,0:T(8,128)(2,1)S(1)}, bf16[40,128,128]{2,1,0:T(8,128)(2,1)S(1)}, u32[]{:S(2)}, u32[]{:S(2)}) %collective-permute-start.1) | collective-permute-done | bytes 1310752 | tf_op jit(solution)/shard_map/ppermute | solution.py:256
  60.4 1.9 %shard_map.48 = (bf16[32,128,128]{2,1,0:T(8,128)(2,1)S(1)}, bf16[10,128,128]{2,1,0:T(8,128)(2,1)S(1)}) custom-call(s32[379]{0:T(512)S(1)} %dynamic-slice_reduce_fusion.table.spots, bf16[17,128,128]{2,1,0:T(8,128)(2,1)S(1)} %get-tuple-element.24.refs_0_, bf16[52,128,128]{2,1,0:T(8,128)(2,1)S(1)} %bitcast.4, bf16[20,128,128]{2,1,0:T(8,128)(2,1)S(1)} %bitcast.6, ...), custom_call_target="tpu_custom_call" | custom-call | tf_op jit(solution)/shard_map/pallas_call | solution.py:276
  62.3 4.4 %collective-permute-start.5 = (bf16[32,128,128]{2,1,0:T(8,128)(2,1)S(1)}, bf16[32,128,128]{2,1,0:T(8,128)(2,1)S(1)}, u32[]{:S(2)}, u32[]{:S(2)}) collective-permute-start(bf16[32,128,128]{2,1,0:T(8,128)(2,1)S(1)} %get-tuple-element.34), channel_id=1, source_target_pairs={{0,508},{1,509},{2,510},{3,511},{4,504},{5,505},{6,506},{7,507},{8... | collective-permute-start | bytes 3145736 | tf_op jit(solution)/shard_map/ppermute | solution.py:256
  66.7 11.0 %collective-permute-start.4 = (bf16[20,128,128]{2,1,0:T(8,128)(2,1)S(1)}, bf16[20,128,128]{2,1,0:T(8,128)(2,1)S(1)}, u32[]{:S(2)}, u32[]{:S(2)}) collective-permute-start(bf16[20,128,128]{2,1,0:T(8,128)(2,1)S(1)} %bitcast.7), channel_id=1, source_target_pairs={{0,8},{1,9},{2,10},{3,11},{4,12},{5,13},{6,14},{7,15},{8,0},{9,1},... | collective-permute-start | bytes 1966088 | tf_op jit(solution)/shard_map/ppermute | solution.py:256
  77.7 0.0 copy-start.3
  77.8 1.9 %collective-permute-start.6 = (bf16[10,128,128]{2,1,0:T(8,128)(2,1)S(1)}, bf16[10,128,128]{2,1,0:T(8,128)(2,1)S(1)}, u32[]{:S(2)}, u32[]{:S(2)}) collective-permute-start(bf16[10,128,128]{2,1,0:T(8,128)(2,1)S(1)} %get-tuple-element.35), channel_id=1, source_target_pairs={{0,16},{1,17},{2,502},{3,503},{8,24},{9,25},{10,510},{11,511},{16,... | collective-permute-start | bytes 983048 | tf_op jit(solution)/shard_map/ppermute | solution.py:256
  79.7 3.5 %shard_map.49.refs_3_ = bf16[189,128,128]{2,1,0:T(8,128)(2,1)S(1)} custom-call(s32[379]{0:T(512)S(1)} %dynamic-slice_reduce_fusion.table.spots, bf16[17,128,128]{2,1,0:T(8,128)(2,1)S(1)} %get-tuple-element.24.refs_0_, bf16[52,128,128]{2,1,0:T(8,128)(2,1)S(1)} %bitcast.5, bf16[20,128,128]{2,1,0:T(8,128)(2,1)S(1)} %bitcast.8, ...), custom_call_target="tpu_custom_call" | custom-call | tf_op jit(solution)/shard_map/pallas_call | solution.py:281
  83.1 14.1 %collective-permute-done.6.refs_2_ = bf16[10,128,128]{2,1,0:T(8,128)(2,1)S(1)} collective-permute-done((bf16[10,128,128]{2,1,0:T(8,128)(2,1)S(1)}, bf16[10,128,128]{2,1,0:T(8,128)(2,1)S(1)}, u32[]{:S(2)}, u32[]{:S(2)}) %collective-permute-start.6) | collective-permute-done | bytes 327712 | tf_op jit(solution)/shard_map/ppermute | solution.py:256
  97.3 6.7 %shard_map.50 = (f32[1,128,2688]{2,1,0:T(8,128)}, bf16[189,128,128]{2,1,0:T(8,128)(2,1)S(1)}) custom-call(s32[379]{0:T(512)S(1)} %dynamic-slice_reduce_fusion.table.spots, s32[1,21]{1,0:T(1,128)S(1)} %copy-done.3, bf16[128,2176]{1,0:T(8,128)(2,1)S(1)} %get-tuple-element.22.masked, ...), custom_call_target="tpu_custom_call", output_to_operand_aliasing={{1}: (6, {})} | custom-call | tf_op jit(solution)/shard_map/pallas_call | solution.py:283
  (8 shorter events, 0.0 us)
Async XLA Ops:
  0.7 1.1 %copy-start.1 = (bf16[1,128,2176]{2,1,0:T(8,128)(2,1)S(1)}, bf16[1,128,2176]{2,1,0:T(8,128)(2,1)}, u32[]{:S(2)}) copy-start(bf16[1,128,2176]{2,1,0:T(8,128)(2,1)} %strip.1) | copy-start | bytes 1671172
  1.8 0.7 copy-start.2
  3.5 1.2 %copy-start = (bf16[4,13,128,128]{3,2,1,0:T(8,128)(2,1)}, bf16[4,13,128,128]{3,2,1,0:T(8,128)(2,1)S(1)}, u32[]{:S(2)}) copy-start(bf16[4,13,128,128]{3,2,1,0:T(8,128)(2,1)S(1)} %get-tuple-element.25) | copy-start | bytes 5111812
  4.7 21.1 %all-to-all-start = ((bf16[4,13,128,128]{3,2,1,0:T(8,128)(2,1)}), bf16[4,13,128,128]{3,2,1,0:T(8,128)(2,1)S(1)}, u32[]{:S(2)}, u32[]{:S(2)}) async-start(bf16[4,13,128,128]{3,2,1,0:T(8,128)(2,1)} %copy-done), calls=%async_computation | async-start | bytes 3407872 | tf_op jit(solution)/shard_map/all_to_all | solution.py:259
  9.6 18.4 %collective-permute-start = (bf16[5,128,128]{2,1,0:T(8,128)(2,1)S(1)}, bf16[5,128,128]{2,1,0:T(8,128)(2,1)S(1)}, u32[]{:S(2)}, u32[]{:S(2)}) collective-permute-start(bf16[5,128,128]{2,1,0:T(8,128)(2,1)S(1)} %get-tuple-element.23), channel_id=1, source_target_pairs={{0,4},{1,5},{2,6},{3,7},{4,0},{5,1},{6,2},{7,3},{8,12},{9,13},{10,... | collective-permute-start | bytes 491528 | tf_op jit(solution)/shard_map/ppermute | solution.py:256
  28.0 32.4 %collective-permute-start.2 = (bf16[52,128,128]{2,1,0:T(8,128)(2,1)S(1)}, bf16[52,128,128]{2,1,0:T(8,128)(2,1)S(1)}, u32[]{:S(2)}, u32[]{:S(2)}) collective-permute-start(bf16[52,128,128]{2,1,0:T(8,128)(2,1)S(1)} %bitcast.3), channel_id=1, source_target_pairs={{0,8},{1,9},{2,10},{3,11},{4,12},{5,13},{6,14},{7,15},{8,0},{9,1},... | collective-permute-start | bytes 5111816 | tf_op jit(solution)/shard_map/ppermute | solution.py:256
  36.3 24.1 %collective-permute-start.1 = (bf16[40,128,128]{2,1,0:T(8,128)(2,1)S(1)}, bf16[40,128,128]{2,1,0:T(8,128)(2,1)S(1)}, u32[]{:S(2)}, u32[]{:S(2)}) collective-permute-start(bf16[40,128,128]{2,1,0:T(8,128)(2,1)S(1)} %get-tuple-element.29), channel_id=1, source_target_pairs={{0,508},{1,509},{2,510},{3,511},{4,504},{5,505},{6,506},{7,507},{8... | collective-permute-start | bytes 3932168 | tf_op jit(solution)/shard_map/ppermute | solution.py:256
  44.4 12.8 %collective-permute-start.3 = (bf16[18,128,128]{2,1,0:T(8,128)(2,1)S(1)}, bf16[18,128,128]{2,1,0:T(8,128)(2,1)S(1)}, u32[]{:S(2)}, u32[]{:S(2)}) collective-permute-start(bf16[18,128,128]{2,1,0:T(8,128)(2,1)S(1)} %get-tuple-element.31), channel_id=1, source_target_pairs={{0,4},{1,5},{2,6},{3,7},{124,120},{125,121},{126,122},{127,123},{1... | collective-permute-start | bytes 1769480 | tf_op jit(solution)/shard_map/ppermute | solution.py:256
  62.3 34.9 %collective-permute-start.5 = (bf16[32,128,128]{2,1,0:T(8,128)(2,1)S(1)}, bf16[32,128,128]{2,1,0:T(8,128)(2,1)S(1)}, u32[]{:S(2)}, u32[]{:S(2)}) collective-permute-start(bf16[32,128,128]{2,1,0:T(8,128)(2,1)S(1)} %get-tuple-element.34), channel_id=1, source_target_pairs={{0,508},{1,509},{2,510},{3,511},{4,504},{5,505},{6,506},{7,507},{8... | collective-permute-start | bytes 3145736 | tf_op jit(solution)/shard_map/ppermute | solution.py:256
  66.7 30.5 %collective-permute-start.4 = (bf16[20,128,128]{2,1,0:T(8,128)(2,1)S(1)}, bf16[20,128,128]{2,1,0:T(8,128)(2,1)S(1)}, u32[]{:S(2)}, u32[]{:S(2)}) collective-permute-start(bf16[20,128,128]{2,1,0:T(8,128)(2,1)S(1)} %bitcast.7), channel_id=1, source_target_pairs={{0,8},{1,9},{2,10},{3,11},{4,12},{5,13},{6,14},{7,15},{8,0},{9,1},... | collective-permute-start | bytes 1966088 | tf_op jit(solution)/shard_map/ppermute | solution.py:256
  77.7 19.5 %copy-start.3 = (s32[1,21]{1,0:T(1,128)S(1)}, s32[1,21]{1,0:T(1,128)}, u32[]{:S(2)}) copy-start(s32[1,21]{1,0:T(1,128)} %keep.1) | copy-start | bytes 256
  77.8 19.5 %collective-permute-start.6 = (bf16[10,128,128]{2,1,0:T(8,128)(2,1)S(1)}, bf16[10,128,128]{2,1,0:T(8,128)(2,1)S(1)}, u32[]{:S(2)}, u32[]{:S(2)}) collective-permute-start(bf16[10,128,128]{2,1,0:T(8,128)(2,1)S(1)} %get-tuple-element.35), channel_id=1, source_target_pairs={{0,16},{1,17},{2,502},{3,503},{8,24},{9,25},{10,510},{11,511},{16,... | collective-permute-start | bytes 983048 | tf_op jit(solution)/shard_map/ppermute | solution.py:256

commit v7 on v6

--- a/solution.py
+++ b/solution.py
@@ -54,6 +54,8 @@
     for i, (y, zl, c, zh, x) in enumerate(coords):
         if (zl, c, zh) in ((0, 0, 0), (nzl - 1, 1, 1)):
             moves["seam"].append((i, place(y, zl, c, 1 - zh, x)))
+        if (zl, c, zh) == (nzl - 1, 0, 1):
+            moves["seam"].append((i, place(y + 1, 0, 0, 0, x)))
         y2, zl2, zh2 = ring(y, zl, zh, 1 if c else -1)
         moves["z"].append((i, place(y2, zl2, 1 - c, zh2, x)))
         for step in (1, -1):
@@ -108,9 +110,10 @@
             if b in need[i] and b not in seen:
                 seen.add(b)
                 spots[i, k] = need[i][b]
-    parts = [where(sent1, own), where(sent2, own), where(sent_s, stock2), where(sent_a, stock2), where(sent_b, stock4), where(sent_f, stock4), spots]
+    parts = [where(sent_s, stock2), where(sent_a, stock2), where(sent_b, stock4), where(sent_f, stock4), spots]
     starts = np.cumsum([0] + [q.shape[1] for q in parts])
-    return moves, np.concatenate(parts, axis=1), [q.shape[1] for q in parts], [int(q) for q in starts]
+    sizes = [len(lists[0][0]), len(sent2[0])] + [q.shape[1] for q in parts]
+    return moves, np.concatenate(parts, axis=1), sizes, [int(q) for q in starts]
 
 
 def vmem(*shape, dtype=jnp.bfloat16):
@@ -136,22 +139,22 @@
     )
 
 
-def first_kernel(start, table, pattern, strip, masked, own, send1, send2):
+def first_kernel(pattern, strip, masked, own, send1, send2):
     for slot in range(2 * BAND_HALF + 1):
         cols = slice(slot * BLK, (slot + 1) * BLK)
         block = strip[0, :, cols] * pattern[0, slot].astype(jnp.bfloat16)
         masked[:, cols] = block
         own[slot] = block if slot >= BAND_HALF else block.T
-    gather(start, table, [own], [send1])
-    start += send1.shape[0]
-
-    def pack(k, carry):
-        block = own[table[start + k]]
+    p = lax.axis_index("x")
+    for k in range(send2.shape[1]):
+        if k < 5:
+            offset = jnp.where(k < 4 - p, k, k + 4)
+            send1[k] = own[BAND_HALF + offset]
+        else:
+            offset = k - 9 - p if k < 9 else k - 5 - p
+        block = own[BAND_HALF + offset]
         for peer in range(4):
             send2[peer, k] = block
-        return carry
-
-    lax.fori_loop(0, send2.shape[1], pack, 0)
 
 
 def gather(start, table, sources, outs):
@@ -261,25 +264,25 @@
     def body(density, pattern, keep):
         table = lax.dynamic_index_in_dim(jnp.asarray(tables), lax.axis_index(AXES), 0, keepdims=False)
         masked, own, send1, send2 = call(
-            functools.partial(first_kernel, starts[0]),
-            (vmem(BLK, 17 * BLK), vmem(17, BLK, BLK), vmem(k1, BLK, BLK), vmem(4, k2, BLK, BLK)), 2, 1,
-        )(table, pattern, density)
+            first_kernel,
+            (vmem(BLK, 17 * BLK), vmem(17, BLK, BLK), vmem(k1, BLK, BLK), vmem(4, k2, BLK, BLK)), 1, 1,
+        )(pattern, density)
         got1 = send(send1, "zh")
         x = spread(send2)
         send_s, send_a = call(
-            functools.partial(gather_kernel, 2, starts[2]), (vmem(ks, BLK, BLK), vmem(ka, BLK, BLK)), 1, 2,
+            functools.partial(gather_kernel, 2, starts[0]), (vmem(ks, BLK, BLK), vmem(ka, BLK, BLK)), 1, 2,
         )(table, own, x)
         got1, send_s, send_a, x = lax.optimization_barrier((got1, send_s, send_a, x))
         got_s, got_a, got_c = send(send_s, "seam"), send(send_a, "z"), send(x, "c")
         w = spread(jnp.broadcast_to(got1, (4, k1, BLK, BLK)))
-        w, got_a, got_c, got_s = lax.optimization_barrier((w, got_a, got_c, got_s))
+        w, got_c, got_s = lax.optimization_barrier((w, got_c, got_s))
         send_b, send_f = call(
-            functools.partial(gather_kernel, 4, starts[4]), (vmem(kb, BLK, BLK), vmem(kf, BLK, BLK)), 1, 4,
+            functools.partial(gather_kernel, 4, starts[2]), (vmem(kb, BLK, BLK), vmem(kf, BLK, BLK)), 1, 4,
         )(table, own, x, w, got_c)
         got_b, got_f, got_d = send(send_b, "z"), send(send_f, "far"), send(w, "c")
         first = [own, x, w, got_c, got_s, got_a]
-        pool = call(functools.partial(early_kernel, starts[6]), vmem(DUMMY, BLK, BLK), 1, len(first))(table, *first)
-        late = starts[6] + sum(q.shape[0] for q in first)
+        pool = call(functools.partial(early_kernel, starts[4]), vmem(DUMMY, BLK, BLK), 1, len(first))(table, *first)
+        late = starts[4] + sum(q.shape[0] for q in first)
         purified, _ = pl.pallas_call(
             functools.partial(final_kernel, late),
             out_shape=(vmem(1, BLK, KEPT * BLK, dtype=jnp.float32), vmem(DUMMY, BLK, BLK)),

time: 104 us -> 102 us (0.981)
  waiting for transfers between devices: 18.6 us -> 12.9 us
  starting transfers between devices: 54.6 us -> 57.9 us
    ppermute x7, waiting for transfers between devices: 17.7 us -> 12.8 us  [send(): return lax.ppermute(array, AXES, moves[name])]
    ppermute x7, starting transfers between devices: 49.8 us -> 53.1 us  [send(): return lax.ppermute(array, AXES, moves[name])]
  transfers between devices with their start and end apart: 8 -> 8, of which waited for: 4 -> 3; matrix products, arithmetic and copies ran while one was open for 0% -> 1% of each run, Pallas kernels for 5% -> 7%
where the time goes in v7:
time: 102 us; the launch traced here: 101 us
  starting transfers between devices  57.9 us (57%)
  Pallas kernels  14.4 us (14%)
  waiting for transfers between devices  12.9 us (13%)
  blocking collectives  12 us (12%)
  local copies, waits for them, and re-layouts  3.77 us (4%)
    ppermute x7, starting transfers between devices, send(): return lax.ppermute(array, AXES, moves[name])  53.1 us
    ppermute x7, waiting for transfers between devices, send(): return lax.ppermute(array, AXES, moves[name])  12.8 us
    all_to_all x1, blocking collectives, spread(): return lax.all_to_all(copies, 'x', 0, 0).reshape(-1, BLK, BLK)  12 us
    pallas_call x1, Pallas kernels, body(): pl.pallas_call(functools.partial(final_kernel, late), out_shape=(vmem(1,...  6.67 us
    all_to_all x1, starting transfers between devices, spread(): return lax.all_to_all(copies, 'x', 0, 0).reshape(-1, BLK, BLK)  4.84 us
    pallas_call x1, Pallas kernels, body(): call(functools.partial(early_kernel, starts[4]), vmem(DUMMY, BLK, BLK), 1...  3.46 us
    unnamed x8, local copies, waits for them, and re-layouts  2.91 us
  transfers between devices with their start and end apart: 8, of which 3 were waited for; matrix products, arithmetic and copies ran while one was open for 1% of the time, Pallas kernels for 7%

profile of v7, /device:TPU:1, one launch (start us, length us, event | category | flops | bytes accessed | tf_op | source)
XLA Modules:
  0.0 101.1 jit_solution(5428936353628502275)
XLA Ops:
  0.0 1.1 %copy-done.1 = bf16[1,128,2176]{2,1,0:T(8,128)(2,1)S(1)} copy-done((bf16[1,128,2176]{2,1,0:T(8,128)(2,1)S(1)}, bf16[1,128,2176]{2,1,0:T(8,128)(2,1)}, u32[]{:S(2)}) %copy-start.1) | copy-done | bytes 557080
  1.1 0.7 copy-done.2
  1.7 1.0 shard_map.46
  2.7 1.2 %copy-done = bf16[4,13,128,128]{3,2,1,0:T(8,128)(2,1)} copy-done((bf16[4,13,128,128]{3,2,1,0:T(8,128)(2,1)}, bf16[4,13,128,128]{3,2,1,0:T(8,128)(2,1)S(1)}, u32[]{:S(2)}) %copy-start) | copy-done | bytes 1703960
  3.9 4.8 %all-to-all-start = ((bf16[4,13,128,128]{3,2,1,0:T(8,128)(2,1)}), bf16[4,13,128,128]{3,2,1,0:T(8,128)(2,1)S(1)}, u32[]{:S(2)}, u32[]{:S(2)}) async-start(bf16[4,13,128,128]{3,2,1,0:T(8,128)(2,1)} %copy-done), calls=%async_computation | async-start | bytes 3407872 | tf_op jit(solution)/shard_map/all_to_all | solution.py:262
  8.7 15.4 %collective-permute-start = (bf16[5,128,128]{2,1,0:T(8,128)(2,1)S(1)}, bf16[5,128,128]{2,1,0:T(8,128)(2,1)S(1)}, u32[]{:S(2)}, u32[]{:S(2)}) collective-permute-start(bf16[5,128,128]{2,1,0:T(8,128)(2,1)S(1)} %get-tuple-element.22), channel_id=1, source_target_pairs={{0,4},{1,5},{2,6},{3,7},{4,0},{5,1},{6,2},{7,3},{8,12},{9,13},{10,... | collective-permute-start | bytes 491528 | tf_op jit(solution)/shard_map/ppermute | solution.py:259
  24.2 0.7 dynamic-slice_reduce_fusion.table.spots
  24.9 0.1 all-to-all-done
  25.0 1.7 %shard_map.47 = (bf16[18,128,128]{2,1,0:T(8,128)(2,1)S(1)}, bf16[40,128,128]{2,1,0:T(8,128)(2,1)S(1)}) custom-call(s32[339]{0:T(512)S(1)} %dynamic-slice_reduce_fusion.table.spots, bf16[17,128,128]{2,1,0:T(8,128)(2,1)S(1)} %get-tuple-element.23.refs_0_, bf16[52,128,128]{2,1,0:T(8,128)(2,1)S(1)} %bitcast.2), custom_call_target="tpu_custom_call" | custom-call | tf_op jit(solution)/shard_map/pallas_call | solution.py:272
  26.8 0.4 collective-permute-done
  27.2 8.3 %collective-permute-start.1 = (bf16[52,128,128]{2,1,0:T(8,128)(2,1)S(1)}, bf16[52,128,128]{2,1,0:T(8,128)(2,1)S(1)}, u32[]{:S(2)}, u32[]{:S(2)}) collective-permute-start(bf16[52,128,128]{2,1,0:T(8,128)(2,1)S(1)} %bitcast.3), channel_id=1, source_target_pairs={{0,8},{1,9},{2,10},{3,11},{4,12},{5,13},{6,14},{7,15},{8,0},{9,1},... | collective-permute-start | bytes 5111816 | tf_op jit(solution)/shard_map/ppermute | solution.py:259
  35.5 8.0 %collective-permute-start.6 = (bf16[40,128,128]{2,1,0:T(8,128)(2,1)S(1)}, bf16[40,128,128]{2,1,0:T(8,128)(2,1)S(1)}, u32[]{:S(2)}, u32[]{:S(2)}) collective-permute-start(bf16[40,128,128]{2,1,0:T(8,128)(2,1)S(1)} %get-tuple-element.35), channel_id=1, source_target_pairs={{0,508},{1,509},{2,510},{3,511},{4,504},{5,505},{6,506},{7,507},{8... | collective-permute-start | bytes 3932168 | tf_op jit(solution)/shard_map/ppermute | solution.py:259
  43.6 0.7 collective-permute-start.2
  44.3 0.1 broadcast_in_dim.3
  44.4 12.0 %all_to_all.10 = bf16[4,5,128,128]{3,2,1,0:T(8,128)(2,1)S(1)} all-to-all(bf16[4,5,128,128]{3,2,1,0:T(8,128)(2,1)S(1)} %broadcast_in_dim.3), channel_id=1, replica_groups=mesh['y'=4,'zl'=8,'c'=2,'zh'=2,'x'=4] {'x'}, dimensions={0} | all-to-all | bytes 1310720 | tf_op jit(solution)/shard_map/all_to_all | solution.py:262
  56.4 0.0 collective-permute-done.2.refs_4_
  56.4 1.6 %shard_map.48 = (bf16[21,128,128]{2,1,0:T(8,128)(2,1)S(1)}, bf16[10,128,128]{2,1,0:T(8,128)(2,1)S(1)}) custom-call(s32[339]{0:T(512)S(1)} %dynamic-slice_reduce_fusion.table.spots, bf16[17,128,128]{2,1,0:T(8,128)(2,1)S(1)} %get-tuple-element.23.refs_0_, bf16[52,128,128]{2,1,0:T(8,128)(2,1)S(1)} %bitcast.4, bf16[20,128,128]{2,1,0:T(8,128)(2,1)S(1)} %bitcast.6, ...), custom_call_target="tpu_custom_call" | custom-call | tf_op jit(solution)/shard_map/pallas_call | solution.py:279
  57.9 5.8 %collective-permute-start.4 = (bf16[21,128,128]{2,1,0:T(8,128)(2,1)S(1)}, bf16[21,128,128]{2,1,0:T(8,128)(2,1)S(1)}, u32[]{:S(2)}, u32[]{:S(2)}) collective-permute-start(bf16[21,128,128]{2,1,0:T(8,128)(2,1)S(1)} %get-tuple-element.32), channel_id=1, source_target_pairs={{0,508},{1,509},{2,510},{3,511},{4,504},{5,505},{6,506},{7,507},{8... | collective-permute-start | bytes 2064392 | tf_op jit(solution)/shard_map/ppermute | solution.py:259
  63.8 12.9 %collective-permute-start.3 = (bf16[20,128,128]{2,1,0:T(8,128)(2,1)S(1)}, bf16[20,128,128]{2,1,0:T(8,128)(2,1)S(1)}, u32[]{:S(2)}, u32[]{:S(2)}) collective-permute-start(bf16[20,128,128]{2,1,0:T(8,128)(2,1)S(1)} %bitcast.7), channel_id=1, source_target_pairs={{0,8},{1,9},{2,10},{3,11},{4,12},{5,13},{6,14},{7,15},{8,0},{9,1},... | collective-permute-start | bytes 1966088 | tf_op jit(solution)/shard_map/ppermute | solution.py:259
  76.6 0.0 copy-start.3
  76.6 1.9 %collective-permute-start.5 = (bf16[10,128,128]{2,1,0:T(8,128)(2,1)S(1)}, bf16[10,128,128]{2,1,0:T(8,128)(2,1)S(1)}, u32[]{:S(2)}, u32[]{:S(2)}) collective-permute-start(bf16[10,128,128]{2,1,0:T(8,128)(2,1)S(1)} %get-tuple-element.33), channel_id=1, source_target_pairs={{0,16},{1,17},{2,502},{3,503},{8,24},{9,25},{10,510},{11,511},{16,... | collective-permute-start | bytes 983048 | tf_op jit(solution)/shard_map/ppermute | solution.py:259
  78.6 3.5 %shard_map.49.refs_3_ = bf16[189,128,128]{2,1,0:T(8,128)(2,1)S(1)} custom-call(s32[339]{0:T(512)S(1)} %dynamic-slice_reduce_fusion.table.spots, bf16[17,128,128]{2,1,0:T(8,128)(2,1)S(1)} %get-tuple-element.23.refs_0_, bf16[52,128,128]{2,1,0:T(8,128)(2,1)S(1)} %bitcast.5, bf16[20,128,128]{2,1,0:T(8,128)(2,1)S(1)} %bitcast.8, ...), custom_call_target="tpu_custom_call" | custom-call | tf_op jit(solution)/shard_map/pallas_call | solution.py:284
  82.0 12.4 %collective-permute-done.5.refs_2_ = bf16[10,128,128]{2,1,0:T(8,128)(2,1)S(1)} collective-permute-done((bf16[10,128,128]{2,1,0:T(8,128)(2,1)S(1)}, bf16[10,128,128]{2,1,0:T(8,128)(2,1)S(1)}, u32[]{:S(2)}, u32[]{:S(2)}) %collective-permute-start.5) | collective-permute-done | bytes 327712 | tf_op jit(solution)/shard_map/ppermute | solution.py:259
  94.4 6.7 %shard_map.50 = (f32[1,128,2688]{2,1,0:T(8,128)}, bf16[189,128,128]{2,1,0:T(8,128)(2,1)S(1)}) custom-call(s32[339]{0:T(512)S(1)} %dynamic-slice_reduce_fusion.table.spots, s32[1,21]{1,0:T(1,128)S(1)} %copy-done.3, bf16[128,2176]{1,0:T(8,128)(2,1)S(1)} %get-tuple-element.21.masked, ...), custom_call_target="tpu_custom_call", output_to_operand_aliasing={{1}: (6, {})} | custom-call | tf_op jit(solution)/shard_map/pallas_call | solution.py:286
  (8 shorter events, 0.0 us)
Async XLA Ops:
  0.0 1.1 %copy-start.1 = (bf16[1,128,2176]{2,1,0:T(8,128)(2,1)S(1)}, bf16[1,128,2176]{2,1,0:T(8,128)(2,1)}, u32[]{:S(2)}) copy-start(bf16[1,128,2176]{2,1,0:T(8,128)(2,1)} %strip.1) | copy-start | bytes 1671172
  1.1 0.7 copy-start.2
  2.7 1.2 %copy-start = (bf16[4,13,128,128]{3,2,1,0:T(8,128)(2,1)}, bf16[4,13,128,128]{3,2,1,0:T(8,128)(2,1)S(1)}, u32[]{:S(2)}) copy-start(bf16[4,13,128,128]{3,2,1,0:T(8,128)(2,1)S(1)} %get-tuple-element.24) | copy-start | bytes 5111812
  3.9 21.1 %all-to-all-start = ((bf16[4,13,128,128]{3,2,1,0:T(8,128)(2,1)}), bf16[4,13,128,128]{3,2,1,0:T(8,128)(2,1)S(1)}, u32[]{:S(2)}, u32[]{:S(2)}) async-start(bf16[4,13,128,128]{3,2,1,0:T(8,128)(2,1)} %copy-done), calls=%async_computation | async-start | bytes 3407872 | tf_op jit(solution)/shard_map/all_to_all | solution.py:262
  8.7 18.4 %collective-permute-start = (bf16[5,128,128]{2,1,0:T(8,128)(2,1)S(1)}, bf16[5,128,128]{2,1,0:T(8,128)(2,1)S(1)}, u32[]{:S(2)}, u32[]{:S(2)}) collective-permute-start(bf16[5,128,128]{2,1,0:T(8,128)(2,1)S(1)} %get-tuple-element.22), channel_id=1, source_target_pairs={{0,4},{1,5},{2,6},{3,7},{4,0},{5,1},{6,2},{7,3},{8,12},{9,13},{10,... | collective-permute-start | bytes 491528 | tf_op jit(solution)/shard_map/ppermute | solution.py:259
  27.2 29.2 %collective-permute-start.1 = (bf16[52,128,128]{2,1,0:T(8,128)(2,1)S(1)}, bf16[52,128,128]{2,1,0:T(8,128)(2,1)S(1)}, u32[]{:S(2)}, u32[]{:S(2)}) collective-permute-start(bf16[52,128,128]{2,1,0:T(8,128)(2,1)S(1)} %bitcast.3), channel_id=1, source_target_pairs={{0,8},{1,9},{2,10},{3,11},{4,12},{5,13},{6,14},{7,15},{8,0},{9,1},... | collective-permute-start | bytes 5111816 | tf_op jit(solution)/shard_map/ppermute | solution.py:259
  35.5 43.1 %collective-permute-start.6 = (bf16[40,128,128]{2,1,0:T(8,128)(2,1)S(1)}, bf16[40,128,128]{2,1,0:T(8,128)(2,1)S(1)}, u32[]{:S(2)}, u32[]{:S(2)}) collective-permute-start(bf16[40,128,128]{2,1,0:T(8,128)(2,1)S(1)} %get-tuple-element.35), channel_id=1, source_target_pairs={{0,508},{1,509},{2,510},{3,511},{4,504},{5,505},{6,506},{7,507},{8... | collective-permute-start | bytes 3932168 | tf_op jit(solution)/shard_map/ppermute | solution.py:259
  43.6 12.8 %collective-permute-start.2 = (bf16[18,128,128]{2,1,0:T(8,128)(2,1)S(1)}, bf16[18,128,128]{2,1,0:T(8,128)(2,1)S(1)}, u32[]{:S(2)}, u32[]{:S(2)}) collective-permute-start(bf16[18,128,128]{2,1,0:T(8,128)(2,1)S(1)} %get-tuple-element.29), channel_id=1, source_target_pairs={{0,4},{1,5},{2,6},{3,7},{116,128},{117,129},{118,130},{119,131},{1... | collective-permute-start | bytes 1769480 | tf_op jit(solution)/shard_map/ppermute | solution.py:259
  57.9 36.5 %collective-permute-start.4 = (bf16[21,128,128]{2,1,0:T(8,128)(2,1)S(1)}, bf16[21,128,128]{2,1,0:T(8,128)(2,1)S(1)}, u32[]{:S(2)}, u32[]{:S(2)}) collective-permute-start(bf16[21,128,128]{2,1,0:T(8,128)(2,1)S(1)} %get-tuple-element.32), channel_id=1, source_target_pairs={{0,508},{1,509},{2,510},{3,511},{4,504},{5,505},{6,506},{7,507},{8... | collective-permute-start | bytes 2064392 | tf_op jit(solution)/shard_map/ppermute | solution.py:259
  63.8 30.7 %collective-permute-start.3 = (bf16[20,128,128]{2,1,0:T(8,128)(2,1)S(1)}, bf16[20,128,128]{2,1,0:T(8,128)(2,1)S(1)}, u32[]{:S(2)}, u32[]{:S(2)}) collective-permute-start(bf16[20,128,128]{2,1,0:T(8,128)(2,1)S(1)} %bitcast.7), channel_id=1, source_target_pairs={{0,8},{1,9},{2,10},{3,11},{4,12},{5,13},{6,14},{7,15},{8,0},{9,1},... | collective-permute-start | bytes 1966088 | tf_op jit(solution)/shard_map/ppermute | solution.py:259
  76.6 17.8 %copy-start.3 = (s32[1,21]{1,0:T(1,128)S(1)}, s32[1,21]{1,0:T(1,128)}, u32[]{:S(2)}) copy-start(s32[1,21]{1,0:T(1,128)} %keep.1) | copy-start | bytes 256
  76.6 17.8 %collective-permute-start.5 = (bf16[10,128,128]{2,1,0:T(8,128)(2,1)S(1)}, bf16[10,128,128]{2,1,0:T(8,128)(2,1)S(1)}, u32[]{:S(2)}, u32[]{:S(2)}) collective-permute-start(bf16[10,128,128]{2,1,0:T(8,128)(2,1)S(1)} %get-tuple-element.33), channel_id=1, source_target_pairs={{0,16},{1,17},{2,502},{3,503},{8,24},{9,25},{10,510},{11,511},{16,... | collective-permute-start | bytes 983048 | tf_op jit(solution)/shard_map/ppermute | solution.py:259

commit v8 on v7

--- a/solution.py
+++ b/solution.py
@@ -102,7 +102,9 @@
     def where(sends, stock):
         return np.array([[src.index(b) if b is not None else 0 for b in q] for q, src in zip(sends, stock)], np.int32)
 
-    arrived = join(stock4, got_s, got_a, got_d, got_b, got_f)
+    width = max(len(sent_s[0]), len(sent_b[0]) + 1)
+    sent_s, got_s = [pad(q, width) for q in sent_s], [pad(q, width) for q in got_s]
+    arrived = join(stock4, got_a, got_d, got_b, got_f, got_s)
     spots = np.full((n, len(arrived[0])), DUMMY, np.int32)
     for i in range(n):
         seen = set()
@@ -273,25 +275,26 @@
             functools.partial(gather_kernel, 2, starts[0]), (vmem(ks, BLK, BLK), vmem(ka, BLK, BLK)), 1, 2,
         )(table, own, x)
         got1, send_s, send_a, x = lax.optimization_barrier((got1, send_s, send_a, x))
-        got_s, got_a, got_c = send(send_s, "seam"), send(send_a, "z"), send(x, "c")
+        got_a, got_c = send(send_a, "z"), send(x, "c")
         w = spread(jnp.broadcast_to(got1, (4, k1, BLK, BLK)))
-        w, got_c, got_s = lax.optimization_barrier((w, got_c, got_s))
+        w, got_c, send_s = lax.optimization_barrier((w, got_c, send_s))
+        got_s = send(send_s, "seam")
         send_b, send_f = call(
             functools.partial(gather_kernel, 4, starts[2]), (vmem(kb, BLK, BLK), vmem(kf, BLK, BLK)), 1, 4,
         )(table, own, x, w, got_c)
         got_b, got_f, got_d = send(send_b, "z"), send(send_f, "far"), send(w, "c")
-        first = [own, x, w, got_c, got_s, got_a]
+        first = [own, x, w, got_c, got_a]
         pool = call(functools.partial(early_kernel, starts[4]), vmem(DUMMY, BLK, BLK), 1, len(first))(table, *first)
         late = starts[4] + sum(q.shape[0] for q in first)
         purified, _ = pl.pallas_call(
             functools.partial(final_kernel, late),
             out_shape=(vmem(1, BLK, KEPT * BLK, dtype=jnp.float32), vmem(DUMMY, BLK, BLK)),
-            in_specs=[scalars()] * 2 + [whole()] * 5,
+            in_specs=[scalars()] * 2 + [whole()] * 6,
             out_specs=(whole(), whole()),
             scratch_shapes=[pltpu.VMEM((BLK, KEPT * BLK), jnp.float32), pltpu.VMEM((BLK, KEPT * BLK), jnp.bfloat16)],
-            input_output_aliases={6: 1},
+            input_output_aliases={7: 1},
             compiler_params=pltpu.CompilerParams(vmem_limit_bytes=24 << 20),
-        )(table, keep, masked, got_d, got_b, got_f, pool)
+        )(table, keep, masked, got_d, got_b, got_f, got_s, pool)
         return purified
 
     return jax.shard_map(

time: 102 us -> 103 us (level)
  transfers between devices with their start and end apart: 8 -> 8, of which waited for: 3 -> 3; matrix products, arithmetic and copies ran while one was open for 1% -> 1% of each run, Pallas kernels for 7% -> 6%
where the time goes in v8:
time: 103 us; the launch traced here: 102 us
  starting transfers between devices  58.5 us (57%)
  Pallas kernels  14.4 us (14%)
  waiting for transfers between devices  13.3 us (13%)
  blocking collectives  12 us (12%)
  local copies, waits for them, and re-layouts  3.77 us (4%)
    ppermute x7, starting transfers between devices, send(): return lax.ppermute(array, AXES, moves[name])  53.6 us
    ppermute x7, waiting for transfers between devices, send(): return lax.ppermute(array, AXES, moves[name])  13.2 us
    all_to_all x1, blocking collectives, spread(): return lax.all_to_all(copies, 'x', 0, 0).reshape(-1, BLK, BLK)  12 us
    pallas_call x1, Pallas kernels, body(): pl.pallas_call(functools.partial(final_kernel, late), out_shape=(vmem(1,...  6.87 us
    all_to_all x1, starting transfers between devices, spread(): return lax.all_to_all(copies, 'x', 0, 0).reshape(-1, BLK, BLK)  4.84 us
    pallas_call x1, Pallas kernels, body(): call(functools.partial(early_kernel, starts[4]), vmem(DUMMY, BLK, BLK), 1...  3.2 us
    unnamed x8, local copies, waits for them, and re-layouts  2.91 us
  transfers between devices with their start and end apart: 8, of which 3 were waited for; matrix products, arithmetic and copies ran while one was open for 1% of the time, Pallas kernels for 6%

profile of v8, /device:TPU:1, one launch (start us, length us, event | category | flops | bytes accessed | tf_op | source)
XLA Modules:
  0.0 102.1 jit_solution(16281512496199625406)
XLA Ops:
  0.0 1.1 %copy-done.1 = bf16[1,128,2176]{2,1,0:T(8,128)(2,1)S(1)} copy-done((bf16[1,128,2176]{2,1,0:T(8,128)(2,1)S(1)}, bf16[1,128,2176]{2,1,0:T(8,128)(2,1)}, u32[]{:S(2)}) %copy-start.1) | copy-done | bytes 557080
  1.1 0.7 copy-done.2
  1.7 1.0 shard_map.46
  2.7 1.2 %copy-done = bf16[4,13,128,128]{3,2,1,0:T(8,128)(2,1)} copy-done((bf16[4,13,128,128]{3,2,1,0:T(8,128)(2,1)}, bf16[4,13,128,128]{3,2,1,0:T(8,128)(2,1)S(1)}, u32[]{:S(2)}) %copy-start) | copy-done | bytes 1703960
  3.9 4.8 %all-to-all-start = ((bf16[4,13,128,128]{3,2,1,0:T(8,128)(2,1)}), bf16[4,13,128,128]{3,2,1,0:T(8,128)(2,1)S(1)}, u32[]{:S(2)}, u32[]{:S(2)}) async-start(bf16[4,13,128,128]{3,2,1,0:T(8,128)(2,1)} %copy-done), calls=%async_computation | async-start | bytes 3407872 | tf_op jit(solution)/shard_map/all_to_all | solution.py:264
  8.7 15.4 %collective-permute-start = (bf16[5,128,128]{2,1,0:T(8,128)(2,1)S(1)}, bf16[5,128,128]{2,1,0:T(8,128)(2,1)S(1)}, u32[]{:S(2)}, u32[]{:S(2)}) collective-permute-start(bf16[5,128,128]{2,1,0:T(8,128)(2,1)S(1)} %get-tuple-element.22), channel_id=1, source_target_pairs={{0,4},{1,5},{2,6},{3,7},{4,0},{5,1},{6,2},{7,3},{8,12},{9,13},{10,... | collective-permute-start | bytes 491528 | tf_op jit(solution)/shard_map/ppermute | solution.py:261
  24.2 0.7 dynamic-slice_reduce_fusion.table.spots
  24.9 0.1 all-to-all-done
  25.0 1.8 %shard_map.47 = (bf16[22,128,128]{2,1,0:T(8,128)(2,1)S(1)}, bf16[40,128,128]{2,1,0:T(8,128)(2,1)S(1)}) custom-call(s32[347]{0:T(512)S(1)} %dynamic-slice_reduce_fusion.table.spots, bf16[17,128,128]{2,1,0:T(8,128)(2,1)S(1)} %get-tuple-element.23.refs_0_, bf16[52,128,128]{2,1,0:T(8,128)(2,1)S(1)} %bitcast.2), custom_call_target="tpu_custom_call" | custom-call | tf_op jit(solution)/shard_map/pallas_call | solution.py:274
  26.9 0.3 collective-permute-done
  27.2 8.4 %collective-permute-start.1 = (bf16[52,128,128]{2,1,0:T(8,128)(2,1)S(1)}, bf16[52,128,128]{2,1,0:T(8,128)(2,1)S(1)}, u32[]{:S(2)}, u32[]{:S(2)}) collective-permute-start(bf16[52,128,128]{2,1,0:T(8,128)(2,1)S(1)} %bitcast.3), channel_id=1, source_target_pairs={{0,8},{1,9},{2,10},{3,11},{4,12},{5,13},{6,14},{7,15},{8,0},{9,1},... | collective-permute-start | bytes 5111816 | tf_op jit(solution)/shard_map/ppermute | solution.py:261
  35.6 8.0 %collective-permute-start.6 = (bf16[40,128,128]{2,1,0:T(8,128)(2,1)S(1)}, bf16[40,128,128]{2,1,0:T(8,128)(2,1)S(1)}, u32[]{:S(2)}, u32[]{:S(2)}) collective-permute-start(bf16[40,128,128]{2,1,0:T(8,128)(2,1)S(1)} %get-tuple-element.35), channel_id=1, source_target_pairs={{0,508},{1,509},{2,510},{3,511},{4,504},{5,505},{6,506},{7,507},{8... | collective-permute-start | bytes 3932168 | tf_op jit(solution)/shard_map/ppermute | solution.py:261
  43.6 0.1 broadcast_in_dim.3
  43.7 12.0 %all_to_all.10 = bf16[4,5,128,128]{3,2,1,0:T(8,128)(2,1)S(1)} all-to-all(bf16[4,5,128,128]{3,2,1,0:T(8,128)(2,1)S(1)} %broadcast_in_dim.3), channel_id=1, replica_groups=mesh['y'=4,'zl'=8,'c'=2,'zh'=2,'x'=4] {'x'}, dimensions={0} | all-to-all | bytes 1310720 | tf_op jit(solution)/shard_map/all_to_all | solution.py:264
  55.7 0.0 collective-permute-done.1.refs_3_
  55.7 0.7 collective-permute-start.5
  56.4 1.6 %shard_map.48 = (bf16[21,128,128]{2,1,0:T(8,128)(2,1)S(1)}, bf16[10,128,128]{2,1,0:T(8,128)(2,1)S(1)}) custom-call(s32[347]{0:T(512)S(1)} %dynamic-slice_reduce_fusion.table.spots, bf16[17,128,128]{2,1,0:T(8,128)(2,1)S(1)} %get-tuple-element.23.refs_0_, bf16[52,128,128]{2,1,0:T(8,128)(2,1)S(1)} %bitcast.4, bf16[20,128,128]{2,1,0:T(8,128)(2,1)S(1)} %bitcast.6, ...), custom_call_target="tpu_custom_call" | custom-call | tf_op jit(solution)/shard_map/pallas_call | solution.py:282
  57.9 5.8 %collective-permute-start.3 = (bf16[21,128,128]{2,1,0:T(8,128)(2,1)S(1)}, bf16[21,128,128]{2,1,0:T(8,128)(2,1)S(1)}, u32[]{:S(2)}, u32[]{:S(2)}) collective-permute-start(bf16[21,128,128]{2,1,0:T(8,128)(2,1)S(1)} %get-tuple-element.32), channel_id=1, source_target_pairs={{0,508},{1,509},{2,510},{3,511},{4,504},{5,505},{6,506},{7,507},{8... | collective-permute-start | bytes 2064392 | tf_op jit(solution)/shard_map/ppermute | solution.py:261
  63.8 13.4 %collective-permute-start.2 = (bf16[20,128,128]{2,1,0:T(8,128)(2,1)S(1)}, bf16[20,128,128]{2,1,0:T(8,128)(2,1)S(1)}, u32[]{:S(2)}, u32[]{:S(2)}) collective-permute-start(bf16[20,128,128]{2,1,0:T(8,128)(2,1)S(1)} %bitcast.7), channel_id=1, source_target_pairs={{0,8},{1,9},{2,10},{3,11},{4,12},{5,13},{6,14},{7,15},{8,0},{9,1},... | collective-permute-start | bytes 1966088 | tf_op jit(solution)/shard_map/ppermute | solution.py:261
  77.2 0.0 copy-start.3
  77.2 1.9 %collective-permute-start.4 = (bf16[10,128,128]{2,1,0:T(8,128)(2,1)S(1)}, bf16[10,128,128]{2,1,0:T(8,128)(2,1)S(1)}, u32[]{:S(2)}, u32[]{:S(2)}) collective-permute-start(bf16[10,128,128]{2,1,0:T(8,128)(2,1)S(1)} %get-tuple-element.33), channel_id=1, source_target_pairs={{0,16},{1,17},{2,502},{3,503},{8,24},{9,25},{10,510},{11,511},{16,... | collective-permute-start | bytes 983048 | tf_op jit(solution)/shard_map/ppermute | solution.py:261
  79.1 3.2 %shard_map.49.refs_4_ = bf16[189,128,128]{2,1,0:T(8,128)(2,1)S(1)} custom-call(s32[347]{0:T(512)S(1)} %dynamic-slice_reduce_fusion.table.spots, bf16[17,128,128]{2,1,0:T(8,128)(2,1)S(1)} %get-tuple-element.23.refs_0_, bf16[52,128,128]{2,1,0:T(8,128)(2,1)S(1)} %bitcast.5, bf16[20,128,128]{2,1,0:T(8,128)(2,1)S(1)} %bitcast.8, ...), custom_call_target="tpu_custom_call" | custom-call | tf_op jit(solution)/shard_map/pallas_call | solution.py:287
  82.3 12.9 %collective-permute-done.4.refs_2_ = bf16[10,128,128]{2,1,0:T(8,128)(2,1)S(1)} collective-permute-done((bf16[10,128,128]{2,1,0:T(8,128)(2,1)S(1)}, bf16[10,128,128]{2,1,0:T(8,128)(2,1)S(1)}, u32[]{:S(2)}, u32[]{:S(2)}) %collective-permute-start.4) | collective-permute-done | bytes 327712 | tf_op jit(solution)/shard_map/ppermute | solution.py:261
  95.3 6.9 %shard_map.50 = (f32[1,128,2688]{2,1,0:T(8,128)}, bf16[189,128,128]{2,1,0:T(8,128)(2,1)S(1)}) custom-call(s32[347]{0:T(512)S(1)} %dynamic-slice_reduce_fusion.table.spots, s32[1,21]{1,0:T(1,128)S(1)} %copy-done.3, bf16[128,2176]{1,0:T(8,128)(2,1)S(1)} %get-tuple-element.21.masked, ...), custom_call_target="tpu_custom_call", output_to_operand_aliasing={{1}: (7, {})} | custom-call | tf_op jit(solution)/shard_map/pallas_call | solution.py:289
  (8 shorter events, 0.0 us)
Async XLA Ops:
  0.0 1.1 %copy-start.1 = (bf16[1,128,2176]{2,1,0:T(8,128)(2,1)S(1)}, bf16[1,128,2176]{2,1,0:T(8,128)(2,1)}, u32[]{:S(2)}) copy-start(bf16[1,128,2176]{2,1,0:T(8,128)(2,1)} %strip.1) | copy-start | bytes 1671172
  1.1 0.7 copy-start.2
  2.7 1.2 %copy-start = (bf16[4,13,128,128]{3,2,1,0:T(8,128)(2,1)}, bf16[4,13,128,128]{3,2,1,0:T(8,128)(2,1)S(1)}, u32[]{:S(2)}) copy-start(bf16[4,13,128,128]{3,2,1,0:T(8,128)(2,1)S(1)} %get-tuple-element.24) | copy-start | bytes 5111812
  3.9 21.1 %all-to-all-start = ((bf16[4,13,128,128]{3,2,1,0:T(8,128)(2,1)}), bf16[4,13,128,128]{3,2,1,0:T(8,128)(2,1)S(1)}, u32[]{:S(2)}, u32[]{:S(2)}) async-start(bf16[4,13,128,128]{3,2,1,0:T(8,128)(2,1)} %copy-done), calls=%async_computation | async-start | bytes 3407872 | tf_op jit(solution)/shard_map/all_to_all | solution.py:264
  8.7 18.4 %collective-permute-start = (bf16[5,128,128]{2,1,0:T(8,128)(2,1)S(1)}, bf16[5,128,128]{2,1,0:T(8,128)(2,1)S(1)}, u32[]{:S(2)}, u32[]{:S(2)}) collective-permute-start(bf16[5,128,128]{2,1,0:T(8,128)(2,1)S(1)} %get-tuple-element.22), channel_id=1, source_target_pairs={{0,4},{1,5},{2,6},{3,7},{4,0},{5,1},{6,2},{7,3},{8,12},{9,13},{10,... | collective-permute-start | bytes 491528 | tf_op jit(solution)/shard_map/ppermute | solution.py:261
  27.2 28.5 %collective-permute-start.1 = (bf16[52,128,128]{2,1,0:T(8,128)(2,1)S(1)}, bf16[52,128,128]{2,1,0:T(8,128)(2,1)S(1)}, u32[]{:S(2)}, u32[]{:S(2)}) collective-permute-start(bf16[52,128,128]{2,1,0:T(8,128)(2,1)S(1)} %bitcast.3), channel_id=1, source_target_pairs={{0,8},{1,9},{2,10},{3,11},{4,12},{5,13},{6,14},{7,15},{8,0},{9,1},... | collective-permute-start | bytes 5111816 | tf_op jit(solution)/shard_map/ppermute | solution.py:261
  35.6 43.5 %collective-permute-start.6 = (bf16[40,128,128]{2,1,0:T(8,128)(2,1)S(1)}, bf16[40,128,128]{2,1,0:T(8,128)(2,1)S(1)}, u32[]{:S(2)}, u32[]{:S(2)}) collective-permute-start(bf16[40,128,128]{2,1,0:T(8,128)(2,1)S(1)} %get-tuple-element.35), channel_id=1, source_target_pairs={{0,508},{1,509},{2,510},{3,511},{4,504},{5,505},{6,506},{7,507},{8... | collective-permute-start | bytes 3932168 | tf_op jit(solution)/shard_map/ppermute | solution.py:261
  55.7 39.6 %collective-permute-start.5 = (bf16[22,128,128]{2,1,0:T(8,128)(2,1)S(1)}, bf16[22,128,128]{2,1,0:T(8,128)(2,1)S(1)}, u32[]{:S(2)}, u32[]{:S(2)}) collective-permute-start(bf16[22,128,128]{2,1,0:T(8,128)(2,1)S(1)} %get-tuple-element.34), channel_id=1, source_target_pairs={{0,4},{1,5},{2,6},{3,7},{116,128},{117,129},{118,130},{119,131},{1... | collective-permute-start | bytes 2162696 | tf_op jit(solution)/shard_map/ppermute | solution.py:261
  57.9 37.3 %collective-permute-start.3 = (bf16[21,128,128]{2,1,0:T(8,128)(2,1)S(1)}, bf16[21,128,128]{2,1,0:T(8,128)(2,1)S(1)}, u32[]{:S(2)}, u32[]{:S(2)}) collective-permute-start(bf16[21,128,128]{2,1,0:T(8,128)(2,1)S(1)} %get-tuple-element.32), channel_id=1, source_target_pairs={{0,508},{1,509},{2,510},{3,511},{4,504},{5,505},{6,506},{7,507},{8... | collective-permute-start | bytes 2064392 | tf_op jit(solution)/shard_map/ppermute | solution.py:261
  63.8 31.5 %collective-permute-start.2 = (bf16[20,128,128]{2,1,0:T(8,128)(2,1)S(1)}, bf16[20,128,128]{2,1,0:T(8,128)(2,1)S(1)}, u32[]{:S(2)}, u32[]{:S(2)}) collective-permute-start(bf16[20,128,128]{2,1,0:T(8,128)(2,1)S(1)} %bitcast.7), channel_id=1, source_target_pairs={{0,8},{1,9},{2,10},{3,11},{4,12},{5,13},{6,14},{7,15},{8,0},{9,1},... | collective-permute-start | bytes 1966088 | tf_op jit(solution)/shard_map/ppermute | solution.py:261
  77.2 18.1 %copy-start.3 = (s32[1,21]{1,0:T(1,128)S(1)}, s32[1,21]{1,0:T(1,128)}, u32[]{:S(2)}) copy-start(s32[1,21]{1,0:T(1,128)} %keep.1) | copy-start | bytes 256
  77.2 18.1 %collective-permute-start.4 = (bf16[10,128,128]{2,1,0:T(8,128)(2,1)S(1)}, bf16[10,128,128]{2,1,0:T(8,128)(2,1)S(1)}, u32[]{:S(2)}, u32[]{:S(2)}) collective-permute-start(bf16[10,128,128]{2,1,0:T(8,128)(2,1)S(1)} %get-tuple-element.33), channel_id=1, source_target_pairs={{0,16},{1,17},{2,502},{3,503},{8,24},{9,25},{10,510},{11,511},{16,... | collective-permute-start | bytes 983048 | tf_op jit(solution)/shard_map/ppermute | solution.py:261

commit v9 on v7

--- a/solution.py
+++ b/solution.py
@@ -102,6 +102,7 @@
     def where(sends, stock):
         return np.array([[src.index(b) if b is not None else 0 for b in q] for q, src in zip(sends, stock)], np.int32)
 
+    sent_s, got_s = [pad(q, 24) for q in sent_s], [pad(q, 24) for q in got_s]
     arrived = join(stock4, got_s, got_a, got_d, got_b, got_f)
     spots = np.full((n, len(arrived[0])), DUMMY, np.int32)
     for i in range(n):
@@ -269,13 +270,14 @@
         )(pattern, density)
         got1 = send(send1, "zh")
         x = spread(send2)
-        send_s, send_a = call(
-            functools.partial(gather_kernel, 2, starts[0]), (vmem(ks, BLK, BLK), vmem(ka, BLK, BLK)), 1, 2,
-        )(table, own, x)
-        got1, send_s, send_a, x = lax.optimization_barrier((got1, send_s, send_a, x))
-        got_s, got_a, got_c = send(send_s, "seam"), send(send_a, "z"), send(x, "c")
+        send_s = call(functools.partial(gather_kernel, 2, starts[0]), vmem(ks, BLK, BLK), 1, 2)(table, own, x)
+        got1, send_s, x = lax.optimization_barrier((got1, send_s, x))
+        got_s, got_c = send(send_s, "seam"), send(x, "c")
+        own, x, got_c = lax.optimization_barrier((own, x, got_c))
+        send_a = call(functools.partial(gather_kernel, 2, starts[1]), vmem(ka, BLK, BLK), 1, 2)(table, own, x)
+        got_a = send(send_a, "z")
         w = spread(jnp.broadcast_to(got1, (4, k1, BLK, BLK)))
-        w, got_c, got_s = lax.optimization_barrier((w, got_c, got_s))
+        w, got_s = lax.optimization_barrier((w, got_s))
         send_b, send_f = call(
             functools.partial(gather_kernel, 4, starts[2]), (vmem(kb, BLK, BLK), vmem(kf, BLK, BLK)), 1, 4,
         )(table, own, x, w, got_c)

time: 102 us -> 100 us (0.980)
  starting transfers between devices: 57.9 us -> 54.2 us
  waiting for transfers between devices: 12.9 us -> 14.8 us
    ppermute x7, starting transfers between devices: 53.1 us -> 49.3 us  [send(): return lax.ppermute(array, AXES, moves[name])]
    ppermute x7, waiting for transfers between devices: 12.8 us -> 14.7 us  [send(): return lax.ppermute(array, AXES, moves[name])]
    pallas_call x1 -> x2, Pallas kernels: 1.75 us -> 2.42 us  [the longest x1 1.38 us: body(): call(functools.partial(gather_kernel, 2, starts[1]), vmem(ka, BLK, BLK),...]
  transfers between devices with their start and end apart: 8 -> 8, of which waited for: 3 -> 4; matrix products, arithmetic and copies ran while one was open for 1% -> 1% of each run, Pallas kernels for 7% -> 8%
where the time goes in v9:
time: 100 us
  starting transfers between devices  54.2 us (54%)
  Pallas kernels  15.2 us (15%)
  waiting for transfers between devices  14.8 us (15%)
  blocking collectives  12 us (12%)
  local copies, waits for them, and re-layouts  3.77 us (4%)
    ppermute x7, starting transfers between devices, send(): return lax.ppermute(array, AXES, moves[name])  49.3 us
    ppermute x7, waiting for transfers between devices, send(): return lax.ppermute(array, AXES, moves[name])  14.7 us
    all_to_all x1, blocking collectives, spread(): return lax.all_to_all(copies, 'x', 0, 0).reshape(-1, BLK, BLK)  12 us
    pallas_call x1, Pallas kernels, body(): pl.pallas_call(functools.partial(final_kernel, late), out_shape=(vmem(1,...  6.68 us
    all_to_all x1, starting transfers between devices, spread(): return lax.all_to_all(copies, 'x', 0, 0).reshape(-1, BLK, BLK)  4.84 us
    pallas_call x1, Pallas kernels, body(): call(functools.partial(early_kernel, starts[4]), vmem(DUMMY, BLK, BLK), 1...  3.55 us
    unnamed x8, local copies, waits for them, and re-layouts  2.91 us
  transfers between devices with their start and end apart: 8, of which 4 were waited for; matrix products, arithmetic and copies ran while one was open for 1% of the time, Pallas kernels for 8%

profile of v9, /device:TPU:1, one launch (start us, length us, event | category | flops | bytes accessed | tf_op | source)
XLA Modules:
  0.0 100.0 jit_solution(16459474496043675873)
XLA Ops:
  0.0 1.1 %copy-done.1 = bf16[1,128,2176]{2,1,0:T(8,128)(2,1)S(1)} copy-done((bf16[1,128,2176]{2,1,0:T(8,128)(2,1)S(1)}, bf16[1,128,2176]{2,1,0:T(8,128)(2,1)}, u32[]{:S(2)}) %copy-start.1) | copy-done | bytes 557080
  1.1 0.7 copy-done.2
  1.7 1.0 shard_map.46
  2.7 1.2 %copy-done = bf16[4,13,128,128]{3,2,1,0:T(8,128)(2,1)} copy-done((bf16[4,13,128,128]{3,2,1,0:T(8,128)(2,1)}, bf16[4,13,128,128]{3,2,1,0:T(8,128)(2,1)S(1)}, u32[]{:S(2)}) %copy-start) | copy-done | bytes 1703960
  3.9 4.8 %all-to-all-start = ((bf16[4,13,128,128]{3,2,1,0:T(8,128)(2,1)}), bf16[4,13,128,128]{3,2,1,0:T(8,128)(2,1)S(1)}, u32[]{:S(2)}, u32[]{:S(2)}) async-start(bf16[4,13,128,128]{3,2,1,0:T(8,128)(2,1)} %copy-done), calls=%async_computation | async-start | bytes 3407872 | tf_op jit(solution)/shard_map/all_to_all | solution.py:263
  8.7 15.4 %collective-permute-start = (bf16[5,128,128]{2,1,0:T(8,128)(2,1)S(1)}, bf16[5,128,128]{2,1,0:T(8,128)(2,1)S(1)}, u32[]{:S(2)}, u32[]{:S(2)}) collective-permute-start(bf16[5,128,128]{2,1,0:T(8,128)(2,1)S(1)} %get-tuple-element.21), channel_id=1, source_target_pairs={{0,4},{1,5},{2,6},{3,7},{4,0},{5,1},{6,2},{7,3},{8,12},{9,13},{10,... | collective-permute-start | bytes 491528 | tf_op jit(solution)/shard_map/ppermute | solution.py:260
  24.2 0.7 dynamic-slice_reduce_fusion.table.spots
  24.9 0.1 all-to-all-done
  25.0 1.0 %shard_map.47 = bf16[24,128,128]{2,1,0:T(8,128)(2,1)S(1)} custom-call(s32[351]{0:T(512)S(1)} %dynamic-slice_reduce_fusion.table.spots, bf16[17,128,128]{2,1,0:T(8,128)(2,1)S(1)} %get-tuple-element.28.refs_0_, bf16[52,128,128]{2,1,0:T(8,128)(2,1)S(1)} %bitcast.2), custom_call_target="tpu_custom_call" | custom-call | tf_op jit(solution)/shard_map/pallas_call | solution.py:273
  26.1 1.1 %collective-permute-done = bf16[5,128,128]{2,1,0:T(8,128)(2,1)S(1)} collective-permute-done((bf16[5,128,128]{2,1,0:T(8,128)(2,1)S(1)}, bf16[5,128,128]{2,1,0:T(8,128)(2,1)S(1)}, u32[]{:S(2)}, u32[]{:S(2)}) %collective-permute-start) | collective-permute-done | bytes 163872 | tf_op jit(solution)/shard_map/ppermute | solution.py:260
  27.2 7.6 %collective-permute-start.3 = (bf16[52,128,128]{2,1,0:T(8,128)(2,1)S(1)}, bf16[52,128,128]{2,1,0:T(8,128)(2,1)S(1)}, u32[]{:S(2)}, u32[]{:S(2)}) collective-permute-start(bf16[52,128,128]{2,1,0:T(8,128)(2,1)S(1)} %bitcast.3), channel_id=1, source_target_pairs={{0,8},{1,9},{2,10},{3,11},{4,12},{5,13},{6,14},{7,15},{8,0},{9,1},... | collective-permute-start | bytes 5111816 | tf_op jit(solution)/shard_map/ppermute | solution.py:260
  34.8 0.7 collective-permute-start.1
  35.5 2.5 %collective-permute-done.3.refs_3_ = bf16[52,128,128]{2,1,0:T(8,128)(2,1)S(1)} collective-permute-done((bf16[52,128,128]{2,1,0:T(8,128)(2,1)S(1)}, bf16[52,128,128]{2,1,0:T(8,128)(2,1)S(1)}, u32[]{:S(2)}, u32[]{:S(2)}) %collective-permute-start.3) | collective-permute-done | bytes 1703968 | tf_op jit(solution)/shard_map/ppermute | solution.py:260
  38.0 1.4 %shard_map.49 = bf16[40,128,128]{2,1,0:T(8,128)(2,1)S(1)} custom-call(s32[351]{0:T(512)S(1)} %dynamic-slice_reduce_fusion.table.spots, bf16[17,128,128]{2,1,0:T(8,128)(2,1)S(1)} %get-tuple-element.28.refs_0_, bf16[52,128,128]{2,1,0:T(8,128)(2,1)S(1)} %bitcast.4), custom_call_target="tpu_custom_call" | custom-call | tf_op jit(solution)/shard_map/pallas_call | solution.py:277
  39.4 9.1 %collective-permute-start.6 = (bf16[40,128,128]{2,1,0:T(8,128)(2,1)S(1)}, bf16[40,128,128]{2,1,0:T(8,128)(2,1)S(1)}, u32[]{:S(2)}, u32[]{:S(2)}) collective-permute-start(bf16[40,128,128]{2,1,0:T(8,128)(2,1)S(1)} %shard_map.49), channel_id=1, source_target_pairs={{0,508},{1,509},{2,510},{3,511},{4,504},{5,505},{6,506},{7,507},{8... | collective-permute-start | bytes 3932168 | tf_op jit(solution)/shard_map/ppermute | solution.py:260
  48.5 0.1 broadcast_in_dim.3
  48.6 12.0 %all_to_all.10 = bf16[4,5,128,128]{3,2,1,0:T(8,128)(2,1)S(1)} all-to-all(bf16[4,5,128,128]{3,2,1,0:T(8,128)(2,1)S(1)} %broadcast_in_dim.3), channel_id=1, replica_groups=mesh['y'=4,'zl'=8,'c'=2,'zh'=2,'x'=4] {'x'}, dimensions={0} | all-to-all | bytes 1310720 | tf_op jit(solution)/shard_map/all_to_all | solution.py:263
  60.6 1.6 %shard_map.48 = (bf16[21,128,128]{2,1,0:T(8,128)(2,1)S(1)}, bf16[10,128,128]{2,1,0:T(8,128)(2,1)S(1)}) custom-call(s32[351]{0:T(512)S(1)} %dynamic-slice_reduce_fusion.table.spots, bf16[17,128,128]{2,1,0:T(8,128)(2,1)S(1)} %get-tuple-element.28.refs_0_, bf16[52,128,128]{2,1,0:T(8,128)(2,1)S(1)} %bitcast.5, bf16[20,128,128]{2,1,0:T(8,128)(2,1)S(1)} %bitcast.7, ...), custom_call_target="tpu_custom_call" | custom-call | tf_op jit(solution)/shard_map/pallas_call | solution.py:281
  62.2 5.5 %collective-permute-start.4 = (bf16[21,128,128]{2,1,0:T(8,128)(2,1)S(1)}, bf16[21,128,128]{2,1,0:T(8,128)(2,1)S(1)}, u32[]{:S(2)}, u32[]{:S(2)}) collective-permute-start(bf16[21,128,128]{2,1,0:T(8,128)(2,1)S(1)} %get-tuple-element.31), channel_id=1, source_target_pairs={{0,508},{1,509},{2,510},{3,511},{4,504},{5,505},{6,506},{7,507},{8... | collective-permute-start | bytes 2064392 | tf_op jit(solution)/shard_map/ppermute | solution.py:260
  67.6 9.1 %collective-permute-start.2 = (bf16[20,128,128]{2,1,0:T(8,128)(2,1)S(1)}, bf16[20,128,128]{2,1,0:T(8,128)(2,1)S(1)}, u32[]{:S(2)}, u32[]{:S(2)}) collective-permute-start(bf16[20,128,128]{2,1,0:T(8,128)(2,1)S(1)} %bitcast.8), channel_id=1, source_target_pairs={{0,8},{1,9},{2,10},{3,11},{4,12},{5,13},{6,14},{7,15},{8,0},{9,1},... | collective-permute-start | bytes 1966088 | tf_op jit(solution)/shard_map/ppermute | solution.py:260
  76.8 1.9 %collective-permute-start.5 = (bf16[10,128,128]{2,1,0:T(8,128)(2,1)S(1)}, bf16[10,128,128]{2,1,0:T(8,128)(2,1)S(1)}, u32[]{:S(2)}, u32[]{:S(2)}) collective-permute-start(bf16[10,128,128]{2,1,0:T(8,128)(2,1)S(1)} %get-tuple-element.32), channel_id=1, source_target_pairs={{0,16},{1,17},{2,502},{3,503},{8,24},{9,25},{10,510},{11,511},{16,... | collective-permute-start | bytes 983048 | tf_op jit(solution)/shard_map/ppermute | solution.py:260
  78.7 3.5 %shard_map.50.refs_3_ = bf16[189,128,128]{2,1,0:T(8,128)(2,1)S(1)} custom-call(s32[351]{0:T(512)S(1)} %dynamic-slice_reduce_fusion.table.spots, bf16[17,128,128]{2,1,0:T(8,128)(2,1)S(1)} %get-tuple-element.28.refs_0_, bf16[52,128,128]{2,1,0:T(8,128)(2,1)S(1)} %bitcast.6, bf16[20,128,128]{2,1,0:T(8,128)(2,1)S(1)} %bitcast.9, ...), custom_call_target="tpu_custom_call" | custom-call | tf_op jit(solution)/shard_map/pallas_call | solution.py:286
  82.3 11.1 %collective-permute-done.5.refs_2_ = bf16[10,128,128]{2,1,0:T(8,128)(2,1)S(1)} collective-permute-done((bf16[10,128,128]{2,1,0:T(8,128)(2,1)S(1)}, bf16[10,128,128]{2,1,0:T(8,128)(2,1)S(1)}, u32[]{:S(2)}, u32[]{:S(2)}) %collective-permute-start.5) | collective-permute-done | bytes 327712 | tf_op jit(solution)/shard_map/ppermute | solution.py:260
  93.3 6.7 %shard_map.51 = (f32[1,128,2688]{2,1,0:T(8,128)}, bf16[189,128,128]{2,1,0:T(8,128)(2,1)S(1)}) custom-call(s32[351]{0:T(512)S(1)} %dynamic-slice_reduce_fusion.table.spots, s32[1,21]{1,0:T(1,128)S(1)} %copy-done.3, bf16[128,2176]{1,0:T(8,128)(2,1)S(1)} %get-tuple-element.20.masked, ...), custom_call_target="tpu_custom_call", output_to_operand_aliasing={{1}: (6, {})} | custom-call | tf_op jit(solution)/shard_map/pallas_call | solution.py:288
  (9 shorter events, 0.0 us)
Async XLA Ops:
  0.0 1.1 %copy-start.1 = (bf16[1,128,2176]{2,1,0:T(8,128)(2,1)S(1)}, bf16[1,128,2176]{2,1,0:T(8,128)(2,1)}, u32[]{:S(2)}) copy-start(bf16[1,128,2176]{2,1,0:T(8,128)(2,1)} %strip.1) | copy-start | bytes 1671172
  1.1 0.7 copy-start.2
  2.7 1.2 %copy-start = (bf16[4,13,128,128]{3,2,1,0:T(8,128)(2,1)}, bf16[4,13,128,128]{3,2,1,0:T(8,128)(2,1)S(1)}, u32[]{:S(2)}) copy-start(bf16[4,13,128,128]{3,2,1,0:T(8,128)(2,1)S(1)} %get-tuple-element.23) | copy-start | bytes 5111812
  3.9 21.1 %all-to-all-start = ((bf16[4,13,128,128]{3,2,1,0:T(8,128)(2,1)}), bf16[4,13,128,128]{3,2,1,0:T(8,128)(2,1)S(1)}, u32[]{:S(2)}, u32[]{:S(2)}) async-start(bf16[4,13,128,128]{3,2,1,0:T(8,128)(2,1)} %copy-done), calls=%async_computation | async-start | bytes 3407872 | tf_op jit(solution)/shard_map/all_to_all | solution.py:263
  8.7 18.4 %collective-permute-start = (bf16[5,128,128]{2,1,0:T(8,128)(2,1)S(1)}, bf16[5,128,128]{2,1,0:T(8,128)(2,1)S(1)}, u32[]{:S(2)}, u32[]{:S(2)}) collective-permute-start(bf16[5,128,128]{2,1,0:T(8,128)(2,1)S(1)} %get-tuple-element.21), channel_id=1, source_target_pairs={{0,4},{1,5},{2,6},{3,7},{4,0},{5,1},{6,2},{7,3},{8,12},{9,13},{10,... | collective-permute-start | bytes 491528 | tf_op jit(solution)/shard_map/ppermute | solution.py:260
  27.2 10.8 %collective-permute-start.3 = (bf16[52,128,128]{2,1,0:T(8,128)(2,1)S(1)}, bf16[52,128,128]{2,1,0:T(8,128)(2,1)S(1)}, u32[]{:S(2)}, u32[]{:S(2)}) collective-permute-start(bf16[52,128,128]{2,1,0:T(8,128)(2,1)S(1)} %bitcast.3), channel_id=1, source_target_pairs={{0,8},{1,9},{2,10},{3,11},{4,12},{5,13},{6,14},{7,15},{8,0},{9,1},... | collective-permute-start | bytes 5111816 | tf_op jit(solution)/shard_map/ppermute | solution.py:260
  34.8 25.8 %collective-permute-start.1 = (bf16[24,128,128]{2,1,0:T(8,128)(2,1)S(1)}, bf16[24,128,128]{2,1,0:T(8,128)(2,1)S(1)}, u32[]{:S(2)}, u32[]{:S(2)}) collective-permute-start(bf16[24,128,128]{2,1,0:T(8,128)(2,1)S(1)} %shard_map.47), channel_id=1, source_target_pairs={{0,4},{1,5},{2,6},{3,7},{116,128},{117,129},{118,130},{119,131},{1... | collective-permute-start | bytes 2359304 | tf_op jit(solution)/shard_map/ppermute | solution.py:260
  39.4 39.3 %collective-permute-start.6 = (bf16[40,128,128]{2,1,0:T(8,128)(2,1)S(1)}, bf16[40,128,128]{2,1,0:T(8,128)(2,1)S(1)}, u32[]{:S(2)}, u32[]{:S(2)}) collective-permute-start(bf16[40,128,128]{2,1,0:T(8,128)(2,1)S(1)} %shard_map.49), channel_id=1, source_target_pairs={{0,508},{1,509},{2,510},{3,511},{4,504},{5,505},{6,506},{7,507},{8... | collective-permute-start | bytes 3932168 | tf_op jit(solution)/shard_map/ppermute | solution.py:260
  62.2 31.1 %collective-permute-start.4 = (bf16[21,128,128]{2,1,0:T(8,128)(2,1)S(1)}, bf16[21,128,128]{2,1,0:T(8,128)(2,1)S(1)}, u32[]{:S(2)}, u32[]{:S(2)}) collective-permute-start(bf16[21,128,128]{2,1,0:T(8,128)(2,1)S(1)} %get-tuple-element.31), channel_id=1, source_target_pairs={{0,508},{1,509},{2,510},{3,511},{4,504},{5,505},{6,506},{7,507},{8... | collective-permute-start | bytes 2064392 | tf_op jit(solution)/shard_map/ppermute | solution.py:260
  67.6 14.6 %collective-permute-start.2 = (bf16[20,128,128]{2,1,0:T(8,128)(2,1)S(1)}, bf16[20,128,128]{2,1,0:T(8,128)(2,1)S(1)}, u32[]{:S(2)}, u32[]{:S(2)}) collective-permute-start(bf16[20,128,128]{2,1,0:T(8,128)(2,1)S(1)} %bitcast.8), channel_id=1, source_target_pairs={{0,8},{1,9},{2,10},{3,11},{4,12},{5,13},{6,14},{7,15},{8,0},{9,1},... | collective-permute-start | bytes 1966088 | tf_op jit(solution)/shard_map/ppermute | solution.py:260
  76.7 16.6 %copy-start.3 = (s32[1,21]{1,0:T(1,128)S(1)}, s32[1,21]{1,0:T(1,128)}, u32[]{:S(2)}) copy-start(s32[1,21]{1,0:T(1,128)} %keep.1) | copy-start | bytes 256
  76.8 16.6 %collective-permute-start.5 = (bf16[10,128,128]{2,1,0:T(8,128)(2,1)S(1)}, bf16[10,128,128]{2,1,0:T(8,128)(2,1)S(1)}, u32[]{:S(2)}, u32[]{:S(2)}) collective-permute-start(bf16[10,128,128]{2,1,0:T(8,128)(2,1)S(1)} %get-tuple-element.32), channel_id=1, source_target_pairs={{0,16},{1,17},{2,502},{3,503},{8,24},{9,25},{10,510},{11,511},{16,... | collective-permute-start | bytes 983048 | tf_op jit(solution)/shard_map/ppermute | solution.py:260

commit v10 on v9

--- a/solution.py
+++ b/solution.py
@@ -23,6 +23,10 @@
 
 def own_lists(p):
     return list(range(0, 4 - p)) + list(range(8 - p, 9)), list(range(-p - 4, -p)) + list(range(4 - p, 8 - p))
+
+
+def is_edge(nzl, zl, zh, x):
+    return ((zl == nzl - 1) & (zh == 1) & (x >= 2)) | ((zl == 0) & (zh == 0) & (x < 2))
 
 
 def make_plan(ny, nzl):
@@ -50,7 +54,7 @@
     moves = {}
     moves["zh"] = [(i, place(y, zl, c, 1 - zh, x)) for i, (y, zl, c, zh, x) in enumerate(coords)]
     moves["c"] = [(i, place(y, zl, 1 - c, zh, x)) for i, (y, zl, c, zh, x) in enumerate(coords)]
-    moves["seam"], moves["z"], moves["far"] = [], [], []
+    moves["seam"], moves["z"], moves["far"], moves["wide"] = [], [], [], []
     for i, (y, zl, c, zh, x) in enumerate(coords):
         if (zl, c, zh) in ((0, 0, 0), (nzl - 1, 1, 1)):
             moves["seam"].append((i, place(y, zl, c, 1 - zh, x)))
@@ -58,10 +62,12 @@
             moves["seam"].append((i, place(y + 1, 0, 0, 0, x)))
         y2, zl2, zh2 = ring(y, zl, zh, 1 if c else -1)
         moves["z"].append((i, place(y2, zl2, 1 - c, zh2, x)))
-        for step in (1, -1):
-            y2, zl2, zh2 = ring(y, zl, zh, step)
-            if (zh2 == 0 and x < 2 and step == 1) or (zh2 == 1 and x >= 2 and step == -1):
-                moves["far"].append((i, place(y2, zl2, c, zh2, x)))
+        step = 1 if x >= 2 else -1
+        y2, zl2, zh2 = ring(y, zl, zh, step)
+        if (zh2 == 0) == (step == 1):
+            moves["far"].append((i, place(y2, zl2, c, zh2, x - 2 * step)))
+            if x in (0, 3):
+                moves["wide"].append((i, place(y2, zl2, c, zh2, 3 - x)))
 
     def moved(sends, name):
         got = [[None] * len(sends[0]) for _ in range(n)]
@@ -80,7 +86,9 @@
     got_c = moved(join(*got2), "c")
     got_d = moved(join(*got3), "c")
     stock4 = join(stock3, got_c)
-    known = [set(row) for row in join(stock4, got_d)]
+    edge = [(sent1 if is_edge(nzl, zl, zh, x) else got1)[i] for i, (y, zl, c, zh, x) in enumerate(coords)]
+    got_f, got_w = moved(edge, "far"), moved(edge, "wide")
+    known = [set(row) for row in join(stock4, got_d, got_f, got_w)]
 
     def choose(name, stock):
         sends = [[] for _ in range(n)]
@@ -96,14 +104,13 @@
     sent_s, got_s = choose("seam", stock2)
     sent_a, got_a = choose("z", stock2)
     sent_b, got_b = choose("z", stock4)
-    sent_f, got_f = choose("far", stock4)
     assert all(set(need[d]) <= known[d] for d in range(n))
 
     def where(sends, stock):
         return np.array([[src.index(b) if b is not None else 0 for b in q] for q, src in zip(sends, stock)], np.int32)
 
     sent_s, got_s = [pad(q, 24) for q in sent_s], [pad(q, 24) for q in got_s]
-    arrived = join(stock4, got_s, got_a, got_d, got_b, got_f)
+    arrived = join(stock4, got_s, got_a, got_d, got_b, got_f, got_w)
     spots = np.full((n, len(arrived[0])), DUMMY, np.int32)
     for i in range(n):
         seen = set()
@@ -111,7 +118,7 @@
             if b in need[i] and b not in seen:
                 seen.add(b)
                 spots[i, k] = need[i][b]
-    parts = [where(sent_s, stock2), where(sent_a, stock2), where(sent_b, stock4), where(sent_f, stock4), spots]
+    parts = [where(sent_s, stock2), where(sent_a, stock2), where(sent_b, stock4), spots]
     starts = np.cumsum([0] + [q.shape[1] for q in parts])
     sizes = [len(lists[0][0]), len(sent2[0])] + [q.shape[1] for q in parts]
     return moves, np.concatenate(parts, axis=1), sizes, [int(q) for q in starts]
@@ -129,7 +136,7 @@
     return pl.BlockSpec(memory_space=pltpu.SMEM)
 
 
-def call(kernel, outs, n_scalar, n_vector, scratch=(), mib=8):
+def call(kernel, outs, n_scalar, n_vector, scratch=(), mib=4):
     return pl.pallas_call(
         kernel,
         out_shape=outs,
@@ -253,7 +260,7 @@
 def solution(mesh):
     ny, nzl = mesh.shape["row"], mesh.shape["col"] // 2
     moves, tables, counts, starts = make_plan(ny, nzl)
-    k1, k2, ks, ka, kb, kf, _ = counts
+    k1, k2, ks, ka, kb, _ = counts
     fine = Mesh(mesh.devices.reshape(ny, nzl, 2, 2, 4), AXES)
 
     def send(array, name):
@@ -276,24 +283,25 @@
         own, x, got_c = lax.optimization_barrier((own, x, got_c))
         send_a = call(functools.partial(gather_kernel, 2, starts[1]), vmem(ka, BLK, BLK), 1, 2)(table, own, x)
         got_a = send(send_a, "z")
+        at = lax.axis_index
+        edge = jnp.where(is_edge(nzl, at("zl"), at("zh"), at("x")), send1, got1)
+        got_f, got_w = send(edge, "far"), send(edge, "wide")
         w = spread(jnp.broadcast_to(got1, (4, k1, BLK, BLK)))
         w, got_s = lax.optimization_barrier((w, got_s))
-        send_b, send_f = call(
-            functools.partial(gather_kernel, 4, starts[2]), (vmem(kb, BLK, BLK), vmem(kf, BLK, BLK)), 1, 4,
-        )(table, own, x, w, got_c)
-        got_b, got_f, got_d = send(send_b, "z"), send(send_f, "far"), send(w, "c")
+        send_b = call(functools.partial(gather_kernel, 4, starts[2]), vmem(kb, BLK, BLK), 1, 4)(table, own, x, w, got_c)
+        got_b, got_d = send(send_b, "z"), send(w, "c")
         first = [own, x, w, got_c, got_s, got_a]
-        pool = call(functools.partial(early_kernel, starts[4]), vmem(DUMMY, BLK, BLK), 1, len(first))(table, *first)
-        late = starts[4] + sum(q.shape[0] for q in first)
+        pool = call(functools.partial(early_kernel, starts[3]), vmem(DUMMY, BLK, BLK), 1, len(first))(table, *first)
+        late = starts[3] + sum(q.shape[0] for q in first)
         purified, _ = pl.pallas_call(
             functools.partial(final_kernel, late),
             out_shape=(vmem(1, BLK, KEPT * BLK, dtype=jnp.float32), vmem(DUMMY, BLK, BLK)),
-            in_specs=[scalars()] * 2 + [whole()] * 5,
+            in_specs=[scalars()] * 2 + [whole()] * 6,
             out_specs=(whole(), whole()),
             scratch_shapes=[pltpu.VMEM((BLK, KEPT * BLK), jnp.float32), pltpu.VMEM((BLK, KEPT * BLK), jnp.bfloat16)],
-            input_output_aliases={6: 1},
-            compiler_params=pltpu.CompilerParams(vmem_limit_bytes=24 << 20),
-        )(table, keep, masked, got_d, got_b, got_f, pool)
+            input_output_aliases={7: 1},
+            compiler_params=pltpu.CompilerParams(vmem_limit_bytes=10 << 20),
+        )(table, keep, masked, got_d, got_b, got_f, got_w, pool)
         return purified
 
     return jax.shard_map(

time: 100 us -> 107 us (1.070)
  waiting for transfers between devices: 14.8 us -> 8.45 us
  starting transfers between devices: 54.2 us -> 59.7 us
  Pallas kernels: 15.2 us -> 18.3 us
  local copies, waits for them, and re-layouts: 3.77 us -> 6.38 us
    ppermute x7 -> x8, waiting for transfers between devices: 14.7 us -> 8.36 us  [send(): return lax.ppermute(array, AXES, moves[name])]
    ppermute x7 -> x8, starting transfers between devices: 49.3 us -> 54.9 us  [send(): return lax.ppermute(array, AXES, moves[name])]
    unnamed x8 -> x20, local copies, waits for them, and re-layouts: 2.91 us -> 5.52 us
    pallas_call x2, Pallas kernels: 5.11 us -> 6.4 us  [the longest x1 4.31 us: body(): call(functools.partial(early_kernel, starts[3]), vmem(DUMMY, BLK, BLK), 1...]
    pallas_call x1, Pallas kernels: 1.38 us -> 2.45 us  [body(): call(functools.partial(gather_kernel, 2, starts[1]), vmem(ka, BLK, BLK),...]
  transfers between devices with their start and end apart: 8 -> 9, of which waited for: 4 -> 4; matrix products, arithmetic and copies ran while one was open for 1% -> 2% of each run, Pallas kernels for 8% -> 9%
where the time goes in v10:
time: 107 us; the launch traced here: 106 us
  starting transfers between devices  59.7 us (56%)
  Pallas kernels  18.3 us (17%)
  blocking collectives  12.1 us (11%)
  waiting for transfers between devices  8.45 us (8%)
  local copies, waits for them, and re-layouts  6.38 us (6%)
    ppermute x8, starting transfers between devices, send(): return lax.ppermute(array, AXES, moves[name])  54.9 us
    all_to_all x1, blocking collectives, spread(): return lax.all_to_all(copies, 'x', 0, 0).reshape(-1, BLK, BLK)  12.1 us
    ppermute x8, waiting for transfers between devices, send(): return lax.ppermute(array, AXES, moves[name])  8.36 us
    pallas_call x1, Pallas kernels, body(): pl.pallas_call(functools.partial(final_kernel, late), out_shape=(vmem(1,...  7.4 us
    unnamed x20, local copies, waits for them, and re-layouts  5.52 us
    all_to_all x1, starting transfers between devices, spread(): return lax.all_to_all(copies, 'x', 0, 0).reshape(-1, BLK, BLK)  4.84 us
    pallas_call x1, Pallas kernels, body(): call(functools.partial(early_kernel, starts[3]), vmem(DUMMY, BLK, BLK), 1...  4.31 us
    pallas_call x1, Pallas kernels, body(): call(functools.partial(gather_kernel, 2, starts[1]), vmem(ka, BLK, BLK),...  2.45 us
  transfers between devices with their start and end apart: 9, of which 4 were waited for; matrix products, arithmetic and copies ran while one was open for 2% of the time, Pallas kernels for 9%

profile of v10, /device:TPU:1, one launch (start us, length us, event | category | flops | bytes accessed | tf_op | source)
XLA Modules:
  0.0 106.0 jit_solution(4258548270820225629)
XLA Ops:
  0.0 1.1 copy-done.5
  1.7 1.0 shard_map.46
  2.7 1.2 %copy-done.2 = bf16[4,13,128,128]{3,2,1,0:T(8,128)(2,1)} copy-done((bf16[4,13,128,128]{3,2,1,0:T(8,128)(2,1)}, bf16[4,13,128,128]{3,2,1,0:T(8,128)(2,1)S(1)}, u32[]{:S(2)}) %copy-start.2) | copy-done | bytes 1703960
  3.9 4.8 %all-to-all-start = ((bf16[4,13,128,128]{3,2,1,0:T(8,128)(2,1)}), bf16[4,13,128,128]{3,2,1,0:T(8,128)(2,1)S(1)}, u32[]{:S(2)}, u32[]{:S(2)}) async-start(bf16[4,13,128,128]{3,2,1,0:T(8,128)(2,1)} %copy-done.2), calls=%async_computation | async-start | bytes 3407872 | tf_op jit(solution)/shard_map/all_to_all | solution.py:270
  8.8 15.4 %collective-permute-start = (bf16[5,128,128]{2,1,0:T(8,128)(2,1)S(1)}, bf16[5,128,128]{2,1,0:T(8,128)(2,1)S(1)}, u32[]{:S(2)}, u32[]{:S(2)}) collective-permute-start(bf16[5,128,128]{2,1,0:T(8,128)(2,1)S(1)} %get-tuple-element.19), channel_id=1, source_target_pairs={{0,4},{1,5},{2,6},{3,7},{4,0},{5,1},{6,2},{7,3},{8,12},{9,13},{10,... | collective-permute-start | bytes 491528 | tf_op jit(solution)/shard_map/ppermute | solution.py:267
  24.2 0.7 dynamic-slice_reduce_fusion.table.spots
  25.0 1.0 shard_map.47
  26.1 1.1 %collective-permute-done = bf16[5,128,128]{2,1,0:T(8,128)(2,1)S(1)} collective-permute-done((bf16[5,128,128]{2,1,0:T(8,128)(2,1)S(1)}, bf16[5,128,128]{2,1,0:T(8,128)(2,1)S(1)}, u32[]{:S(2)}, u32[]{:S(2)}) %collective-permute-start) | collective-permute-done | bytes 163872 | tf_op jit(solution)/shard_map/ppermute | solution.py:267
  27.2 7.6 %collective-permute-start.3 = (bf16[52,128,128]{2,1,0:T(8,128)(2,1)S(1)}, bf16[52,128,128]{2,1,0:T(8,128)(2,1)S(1)}, u32[]{:S(2)}, u32[]{:S(2)}) collective-permute-start(bf16[52,128,128]{2,1,0:T(8,128)(2,1)S(1)} %bitcast.3), channel_id=1, source_target_pairs={{0,8},{1,9},{2,10},{3,11},{4,12},{5,13},{6,14},{7,15},{8,0},{9,1},... | collective-permute-start | bytes 5111816 | tf_op jit(solution)/shard_map/ppermute | solution.py:267
  35.5 2.5 %collective-permute-done.3.refs_3_ = bf16[52,128,128]{2,1,0:T(8,128)(2,1)S(1)} collective-permute-done((bf16[52,128,128]{2,1,0:T(8,128)(2,1)S(1)}, bf16[52,128,128]{2,1,0:T(8,128)(2,1)S(1)}, u32[]{:S(2)}, u32[]{:S(2)}) %collective-permute-start.3) | collective-permute-done | bytes 1703968 | tf_op jit(solution)/shard_map/ppermute | solution.py:267
  38.0 2.5 %shard_map.49 = bf16[40,128,128]{2,1,0:T(8,128)(2,1)} custom-call(s32[339]{0:T(512)S(1)} %dynamic-slice_reduce_fusion.table.spots, bf16[17,128,128]{2,1,0:T(8,128)(2,1)S(1)} %get-tuple-element.26.refs_0_, bf16[52,128,128]{2,1,0:T(8,128)(2,1)S(1)} %bitcast.4), custom_call_target="tpu_custom_call" | custom-call | tf_op jit(solution)/shard_map/pallas_call | solution.py:284
  40.5 9.1 %collective-permute-start.7 = (bf16[40,128,128]{2,1,0:T(8,128)(2,1)}, bf16[40,128,128]{2,1,0:T(8,128)(2,1)}, u32[]{:S(2)}, u32[]{:S(2)}) collective-permute-start(bf16[40,128,128]{2,1,0:T(8,128)(2,1)} %shard_map.49), channel_id=1, source_target_pairs={{0,508},{1,509},{2,510},{3,511},{4,504},{5,505},{6,506},{7,507},{8... | collective-permute-start | bytes 3932168 | tf_op jit(solution)/shard_map/ppermute | solution.py:267
  49.7 12.1 %all_to_all.10 = bf16[4,5,128,128]{3,2,1,0:T(8,128)(2,1)S(1)} all-to-all(bf16[4,5,128,128]{3,2,1,0:T(8,128)(2,1)S(1)} %broadcast_in_dim.3), channel_id=1, replica_groups=mesh['y'=4,'zl'=8,'c'=2,'zh'=2,'x'=4] {'x'}, dimensions={0} | all-to-all | bytes 1310720 | tf_op jit(solution)/shard_map/all_to_all | solution.py:270
  61.8 11.0 %collective-permute-start.2 = (bf16[20,128,128]{2,1,0:T(8,128)(2,1)S(1)}, bf16[20,128,128]{2,1,0:T(8,128)(2,1)}, u32[]{:S(2)}, u32[]{:S(2)}) collective-permute-start(bf16[20,128,128]{2,1,0:T(8,128)(2,1)S(1)} %bitcast.7), channel_id=1, source_target_pairs={{0,8},{1,9},{2,10},{3,11},{4,12},{5,13},{6,14},{7,15},{8,0},{9,1},... | collective-permute-start | bytes 1966088 | tf_op jit(solution)/shard_map/ppermute | solution.py:267
  72.8 2.1 %shard_map.48 = bf16[20,128,128]{2,1,0:T(8,128)(2,1)} custom-call(s32[339]{0:T(512)S(1)} %dynamic-slice_reduce_fusion.table.spots, bf16[17,128,128]{2,1,0:T(8,128)(2,1)S(1)} %get-tuple-element.26.refs_0_, bf16[52,128,128]{2,1,0:T(8,128)(2,1)S(1)} %bitcast.5, bf16[20,128,128]{2,1,0:T(8,128)(2,1)S(1)} %bitcast.8, ...), custom_call_target="tpu_custom_call" | custom-call | tf_op jit(solution)/shard_map/pallas_call | solution.py:291
  74.9 1.9 %collective-permute-start.4 = (bf16[20,128,128]{2,1,0:T(8,128)(2,1)}, bf16[20,128,128]{2,1,0:T(8,128)(2,1)}, u32[]{:S(2)}, u32[]{:S(2)}) collective-permute-start(bf16[20,128,128]{2,1,0:T(8,128)(2,1)} %shard_map.48), channel_id=1, source_target_pairs={{0,508},{1,509},{2,510},{3,511},{4,504},{5,505},{6,506},{7,507},{8... | collective-permute-start | bytes 1966088 | tf_op jit(solution)/shard_map/ppermute | solution.py:267
  76.9 0.9 broadcast_select_fusion
  77.8 7.2 %collective-permute-start.6 = (bf16[5,128,128]{2,1,0:T(8,128)(2,1)S(1)}, bf16[5,128,128]{2,1,0:T(8,128)(2,1)S(1)}, u32[]{:S(2)}, u32[]{:S(2)}) collective-permute-start(bf16[5,128,128]{2,1,0:T(8,128)(2,1)S(1)} %broadcast_select_fusion), channel_id=1, source_target_pairs={{0,503},{3,16},{8,511},{11,24},{19,32},{20,7},{27,40},{28,15},{35,... | collective-permute-start | bytes 491528 | tf_op jit(solution)/shard_map/ppermute | solution.py:267
  85.0 1.9 %collective-permute-start.5 = (bf16[5,128,128]{2,1,0:T(8,128)(2,1)S(1)}, bf16[5,128,128]{2,1,0:T(8,128)(2,1)S(1)}, u32[]{:S(2)}, u32[]{:S(2)}) collective-permute-start(bf16[5,128,128]{2,1,0:T(8,128)(2,1)S(1)} %broadcast_select_fusion), channel_id=1, source_target_pairs={{0,502},{1,503},{2,16},{3,17},{8,510},{9,511},{10,24},{11,25},{18,... | collective-permute-start | bytes 491528 | tf_op jit(solution)/shard_map/ppermute | solution.py:267
  87.0 1.4 %copy-done.1 = bf16[52,128,128]{2,1,0:T(8,128)(2,1)S(1)} copy-done((bf16[52,128,128]{2,1,0:T(8,128)(2,1)S(1)}, bf16[52,128,128]{2,1,0:T(8,128)(2,1)}, u32[]{:S(2)}) %copy-start.1) | copy-done | bytes 1703960
  88.4 1.1 %copy-done.4 = bf16[24,128,128]{2,1,0:T(8,128)(2,1)S(1)} copy-done((bf16[24,128,128]{2,1,0:T(8,128)(2,1)S(1)}, bf16[24,128,128]{2,1,0:T(8,128)(2,1)}, u32[]{:S(2)}) %copy-start.4) | copy-done | bytes 786456
  89.6 4.3 %shard_map.50.refs_4_ = bf16[189,128,128]{2,1,0:T(8,128)(2,1)S(1)} custom-call(s32[339]{0:T(512)S(1)} %dynamic-slice_reduce_fusion.table.spots, bf16[17,128,128]{2,1,0:T(8,128)(2,1)S(1)} %get-tuple-element.26.refs_0_, bf16[52,128,128]{2,1,0:T(8,128)(2,1)S(1)} %bitcast.6, bf16[20,128,128]{2,1,0:T(8,128)(2,1)S(1)} %bitcast.9, ...), custom_call_target="tpu_custom_call" | custom-call | tf_op jit(solution)/shard_map/pallas_call | solution.py:294
  93.9 4.7 %collective-permute-done.5.refs_2_ = bf16[5,128,128]{2,1,0:T(8,128)(2,1)S(1)} collective-permute-done((bf16[5,128,128]{2,1,0:T(8,128)(2,1)S(1)}, bf16[5,128,128]{2,1,0:T(8,128)(2,1)S(1)}, u32[]{:S(2)}, u32[]{:S(2)}) %collective-permute-start.5) | collective-permute-done | bytes 163872 | tf_op jit(solution)/shard_map/ppermute | solution.py:267
  98.7 7.4 %shard_map.51 = (f32[1,128,2688]{2,1,0:T(8,128)}, bf16[189,128,128]{2,1,0:T(8,128)(2,1)S(1)}) custom-call(s32[339]{0:T(512)S(1)} %dynamic-slice_reduce_fusion.table.spots, s32[1,21]{1,0:T(1,128)S(1)} %copy-done.8, bf16[128,2176]{1,0:T(8,128)(2,1)S(1)} %get-tuple-element.18.masked, ...), custom_call_target="tpu_custom_call", output_to_operand_aliasing={{1}: (7, {})} | custom-call | tf_op jit(solution)/shard_map/pallas_call | solution.py:296
  (24 shorter events, 1.6 us)
Async XLA Ops:
  0.0 1.1 copy-start.5
  1.1 0.7 copy-start.7
  2.7 1.2 %copy-start.2 = (bf16[4,13,128,128]{3,2,1,0:T(8,128)(2,1)}, bf16[4,13,128,128]{3,2,1,0:T(8,128)(2,1)S(1)}, u32[]{:S(2)}) copy-start(bf16[4,13,128,128]{3,2,1,0:T(8,128)(2,1)S(1)} %get-tuple-element.21) | copy-start | bytes 5111812
  3.9 4.8 %copy-start.6 = (bf16[5,128,128]{2,1,0:T(8,128)(2,1)}, bf16[5,128,128]{2,1,0:T(8,128)(2,1)S(1)}, u32[]{:S(2)}) copy-start(bf16[5,128,128]{2,1,0:T(8,128)(2,1)S(1)} %get-tuple-element.19) | copy-start | bytes 491524
  3.9 21.1 %all-to-all-start = ((bf16[4,13,128,128]{3,2,1,0:T(8,128)(2,1)}), bf16[4,13,128,128]{3,2,1,0:T(8,128)(2,1)S(1)}, u32[]{:S(2)}, u32[]{:S(2)}) async-start(bf16[4,13,128,128]{3,2,1,0:T(8,128)(2,1)} %copy-done.2), calls=%async_computation | async-start | bytes 3407872 | tf_op jit(solution)/shard_map/all_to_all | solution.py:270
  8.8 18.4 %collective-permute-start = (bf16[5,128,128]{2,1,0:T(8,128)(2,1)S(1)}, bf16[5,128,128]{2,1,0:T(8,128)(2,1)S(1)}, u32[]{:S(2)}, u32[]{:S(2)}) collective-permute-start(bf16[5,128,128]{2,1,0:T(8,128)(2,1)S(1)} %get-tuple-element.19), channel_id=1, source_target_pairs={{0,4},{1,5},{2,6},{3,7},{4,0},{5,1},{6,2},{7,3},{8,12},{9,13},{10,... | collective-permute-start | bytes 491528 | tf_op jit(solution)/shard_map/ppermute | solution.py:267
  27.2 22.4 %copy-start.9 = (bf16[5,128,128]{2,1,0:T(8,128)(2,1)}, bf16[5,128,128]{2,1,0:T(8,128)(2,1)S(1)}, u32[]{:S(2)}) copy-start(bf16[5,128,128]{2,1,0:T(8,128)(2,1)S(1)} %collective-permute-done) | copy-start | bytes 491524
  27.2 10.8 %collective-permute-start.3 = (bf16[52,128,128]{2,1,0:T(8,128)(2,1)S(1)}, bf16[52,128,128]{2,1,0:T(8,128)(2,1)S(1)}, u32[]{:S(2)}, u32[]{:S(2)}) collective-permute-start(bf16[52,128,128]{2,1,0:T(8,128)(2,1)S(1)} %bitcast.3), channel_id=1, source_target_pairs={{0,8},{1,9},{2,10},{3,11},{4,12},{5,13},{6,14},{7,15},{8,0},{9,1},... | collective-permute-start | bytes 5111816 | tf_op jit(solution)/shard_map/ppermute | solution.py:267
  34.8 27.0 %collective-permute-start.1 = (bf16[24,128,128]{2,1,0:T(8,128)(2,1)S(1)}, bf16[24,128,128]{2,1,0:T(8,128)(2,1)S(1)}, u32[]{:S(2)}, u32[]{:S(2)}) collective-permute-start(bf16[24,128,128]{2,1,0:T(8,128)(2,1)S(1)} %shard_map.47), channel_id=1, source_target_pairs={{0,4},{1,5},{2,6},{3,7},{116,128},{117,129},{118,130},{119,131},{1... | collective-permute-start | bytes 2359304 | tf_op jit(solution)/shard_map/ppermute | solution.py:267
  38.0 34.8 %copy-start = (bf16[52,128,128]{2,1,0:T(8,128)(2,1)}, bf16[52,128,128]{2,1,0:T(8,128)(2,1)S(1)}, u32[]{:S(2)}) copy-start(bf16[52,128,128]{2,1,0:T(8,128)(2,1)S(1)} %collective-permute-done.3.refs_3_) | copy-start | bytes 5111812
  40.5 46.5 %collective-permute-start.7 = (bf16[40,128,128]{2,1,0:T(8,128)(2,1)}, bf16[40,128,128]{2,1,0:T(8,128)(2,1)}, u32[]{:S(2)}, u32[]{:S(2)}) collective-permute-start(bf16[40,128,128]{2,1,0:T(8,128)(2,1)} %shard_map.49), channel_id=1, source_target_pairs={{0,508},{1,509},{2,510},{3,511},{4,504},{5,505},{6,506},{7,507},{8... | collective-permute-start | bytes 3932168 | tf_op jit(solution)/shard_map/ppermute | solution.py:267
  61.8 13.1 %copy-start.3 = (bf16[24,128,128]{2,1,0:T(8,128)(2,1)}, bf16[24,128,128]{2,1,0:T(8,128)(2,1)S(1)}, u32[]{:S(2)}) copy-start(bf16[24,128,128]{2,1,0:T(8,128)(2,1)S(1)} %collective-permute-done.1.refs_4_) | copy-start | bytes 2359300
  61.8 36.8 %collective-permute-start.2 = (bf16[20,128,128]{2,1,0:T(8,128)(2,1)S(1)}, bf16[20,128,128]{2,1,0:T(8,128)(2,1)}, u32[]{:S(2)}, u32[]{:S(2)}) collective-permute-start(bf16[20,128,128]{2,1,0:T(8,128)(2,1)S(1)} %bitcast.7), channel_id=1, source_target_pairs={{0,8},{1,9},{2,10},{3,11},{4,12},{5,13},{6,14},{7,15},{8,0},{9,1},... | collective-permute-start | bytes 1966088 | tf_op jit(solution)/shard_map/ppermute | solution.py:267
  74.9 23.7 %collective-permute-start.4 = (bf16[20,128,128]{2,1,0:T(8,128)(2,1)}, bf16[20,128,128]{2,1,0:T(8,128)(2,1)}, u32[]{:S(2)}, u32[]{:S(2)}) collective-permute-start(bf16[20,128,128]{2,1,0:T(8,128)(2,1)} %shard_map.48), channel_id=1, source_target_pairs={{0,508},{1,509},{2,510},{3,511},{4,504},{5,505},{6,506},{7,507},{8... | collective-permute-start | bytes 1966088 | tf_op jit(solution)/shard_map/ppermute | solution.py:267
  76.9 21.8 %copy-start.8 = (s32[1,21]{1,0:T(1,128)S(1)}, s32[1,21]{1,0:T(1,128)}, u32[]{:S(2)}) copy-start(s32[1,21]{1,0:T(1,128)} %keep.1) | copy-start | bytes 256
  77.8 16.0 %collective-permute-start.6 = (bf16[5,128,128]{2,1,0:T(8,128)(2,1)S(1)}, bf16[5,128,128]{2,1,0:T(8,128)(2,1)S(1)}, u32[]{:S(2)}, u32[]{:S(2)}) collective-permute-start(bf16[5,128,128]{2,1,0:T(8,128)(2,1)S(1)} %broadcast_select_fusion), channel_id=1, source_target_pairs={{0,503},{3,16},{8,511},{11,24},{19,32},{20,7},{27,40},{28,15},{35,... | collective-permute-start | bytes 491528 | tf_op jit(solution)/shard_map/ppermute | solution.py:267
  85.0 13.6 %collective-permute-start.5 = (bf16[5,128,128]{2,1,0:T(8,128)(2,1)S(1)}, bf16[5,128,128]{2,1,0:T(8,128)(2,1)S(1)}, u32[]{:S(2)}, u32[]{:S(2)}) collective-permute-start(bf16[5,128,128]{2,1,0:T(8,128)(2,1)S(1)} %broadcast_select_fusion), channel_id=1, source_target_pairs={{0,502},{1,503},{2,16},{3,17},{8,510},{9,511},{10,24},{11,25},{18,... | collective-permute-start | bytes 491528 | tf_op jit(solution)/shard_map/ppermute | solution.py:267
  87.0 1.5 %copy-start.1 = (bf16[52,128,128]{2,1,0:T(8,128)(2,1)S(1)}, bf16[52,128,128]{2,1,0:T(8,128)(2,1)}, u32[]{:S(2)}) copy-start(bf16[52,128,128]{2,1,0:T(8,128)(2,1)} %copy-done) | copy-start | bytes 5111812
  88.4 1.1 %copy-start.4 = (bf16[24,128,128]{2,1,0:T(8,128)(2,1)S(1)}, bf16[24,128,128]{2,1,0:T(8,128)(2,1)}, u32[]{:S(2)}) copy-start(bf16[24,128,128]{2,1,0:T(8,128)(2,1)} %copy-done.3) | copy-start | bytes 2359300

commit v11 on v10

--- a/solution.py
+++ b/solution.py
@@ -189,6 +189,20 @@
     gather(start, table, refs[:n_sources], refs[n_sources:])
 
 
+def third_kernel(nzl, start, table, own, x, send1, got1, z, edge):
+    gather(start, table, [own, x], [z])
+    at = lax.axis_index
+    swap = is_edge(nzl, at("zl"), at("zh"), at("x"))
+
+    @pl.when(swap)
+    def _():
+        edge[...] = send1[...]
+
+    @pl.when(jnp.logical_not(swap))
+    def _():
+        edge[...] = got1[...]
+
+
 def product(left, first, pool, v, width):
     last = KEPT - 1 - first
     blank = jnp.zeros((BLK, BLK), jnp.bfloat16)
@@ -281,10 +295,10 @@
         got1, send_s, x = lax.optimization_barrier((got1, send_s, x))
         got_s, got_c = send(send_s, "seam"), send(x, "c")
         own, x, got_c = lax.optimization_barrier((own, x, got_c))
-        send_a = call(functools.partial(gather_kernel, 2, starts[1]), vmem(ka, BLK, BLK), 1, 2)(table, own, x)
+        send_a, edge = call(
+            functools.partial(third_kernel, nzl, starts[1]), (vmem(ka, BLK, BLK), vmem(k1, BLK, BLK)), 1, 4,
+        )(table, own, x, send1, got1)
         got_a = send(send_a, "z")
-        at = lax.axis_index
-        edge = jnp.where(is_edge(nzl, at("zl"), at("zh"), at("x")), send1, got1)
         got_f, got_w = send(edge, "far"), send(edge, "wide")
         w = spread(jnp.broadcast_to(got1, (4, k1, BLK, BLK)))
         w, got_s = lax.optimization_barrier((w, got_s))

time: 107 us -> 103 us (0.963)
  Pallas kernels: 18.3 us -> 14.7 us
  waiting for transfers between devices: 8.45 us -> 11.8 us
  local copies, waits for them, and re-layouts: 6.38 us -> 3.77 us
    ppermute x8, waiting for transfers between devices: 8.36 us -> 11.7 us  [send(): return lax.ppermute(array, AXES, moves[name])]
    unnamed x20 -> x8, local copies, waits for them, and re-layouts: 5.52 us -> 2.91 us
  transfers between devices with their start and end apart: 9 -> 9, of which waited for: 4 -> 5; matrix products, arithmetic and copies ran while one was open for 2% -> 1% of each run, Pallas kernels for 9% -> 7%
where the time goes in v11:
time: 103 us; the launch traced here: 102 us
  starting transfers between devices  59.8 us (58%)
  Pallas kernels  14.7 us (14%)
  blocking collectives  12 us (12%)
  waiting for transfers between devices  11.8 us (11%)
  local copies, waits for them, and re-layouts  3.77 us (4%)
    ppermute x8, starting transfers between devices, send(): return lax.ppermute(array, AXES, moves[name])  55 us
    all_to_all x1, blocking collectives, spread(): return lax.all_to_all(copies, 'x', 0, 0).reshape(-1, BLK, BLK)  12 us
    ppermute x8, waiting for transfers between devices, send(): return lax.ppermute(array, AXES, moves[name])  11.7 us
    pallas_call x1, Pallas kernels, body(): pl.pallas_call(functools.partial(final_kernel, late), out_shape=(vmem(1,...  6.53 us
    all_to_all x1, starting transfers between devices, spread(): return lax.all_to_all(copies, 'x', 0, 0).reshape(-1, BLK, BLK)  4.84 us
    pallas_call x1, Pallas kernels, body(): call(functools.partial(early_kernel, starts[3]), vmem(DUMMY, BLK, BLK), 1...  3.55 us
    unnamed x8, local copies, waits for them, and re-layouts  2.91 us
  transfers between devices with their start and end apart: 9, of which 5 were waited for; matrix products, arithmetic and copies ran while one was open for 1% of the time, Pallas kernels for 7%

profile of v11, /device:TPU:1, one launch (start us, length us, event | category | flops | bytes accessed | tf_op | source)
XLA Modules:
  0.0 102.3 jit_solution(16217473272814337878)
XLA Ops:
  0.0 1.1 %copy-done.1 = bf16[1,128,2176]{2,1,0:T(8,128)(2,1)S(1)} copy-done((bf16[1,128,2176]{2,1,0:T(8,128)(2,1)S(1)}, bf16[1,128,2176]{2,1,0:T(8,128)(2,1)}, u32[]{:S(2)}) %copy-start.1) | copy-done | bytes 557080
  1.1 0.7 copy-done.2
  1.7 1.0 shard_map.46
  2.7 1.2 %copy-done = bf16[4,13,128,128]{3,2,1,0:T(8,128)(2,1)} copy-done((bf16[4,13,128,128]{3,2,1,0:T(8,128)(2,1)}, bf16[4,13,128,128]{3,2,1,0:T(8,128)(2,1)S(1)}, u32[]{:S(2)}) %copy-start) | copy-done | bytes 1703960
  3.9 4.8 %all-to-all-start = ((bf16[4,13,128,128]{3,2,1,0:T(8,128)(2,1)}), bf16[4,13,128,128]{3,2,1,0:T(8,128)(2,1)S(1)}, u32[]{:S(2)}, u32[]{:S(2)}) async-start(bf16[4,13,128,128]{3,2,1,0:T(8,128)(2,1)} %copy-done), calls=%async_computation | async-start | bytes 3407872 | tf_op jit(solution)/shard_map/all_to_all | solution.py:284
  8.7 15.4 %collective-permute-start = (bf16[5,128,128]{2,1,0:T(8,128)(2,1)S(1)}, bf16[5,128,128]{2,1,0:T(8,128)(2,1)S(1)}, u32[]{:S(2)}, u32[]{:S(2)}) collective-permute-start(bf16[5,128,128]{2,1,0:T(8,128)(2,1)S(1)} %get-tuple-element.21.send1), channel_id=1, source_target_pairs={{0,4},{1,5},{2,6},{3,7},{4,0},{5,1},{6,2},{7,3},{8,12},{9,13},{10,... | collective-permute-start | bytes 491528 | tf_op jit(solution)/shard_map/ppermute | solution.py:281
  24.2 0.7 dynamic-slice_reduce_fusion.table.spots
  25.0 1.0 %shard_map.47 = bf16[24,128,128]{2,1,0:T(8,128)(2,1)S(1)} custom-call(s32[339]{0:T(512)S(1)} %dynamic-slice_reduce_fusion.table.spots, bf16[17,128,128]{2,1,0:T(8,128)(2,1)S(1)} %get-tuple-element.28.refs_0_.own, bf16[52,128,128]{2,1,0:T(8,128)(2,1)S(1)} %bitcast.2), custom_call_target="tpu_custom_call" | custom-call | tf_op jit(solution)/shard_map/pallas_call | solution.py:294
  26.1 1.1 %collective-permute-done.got1 = bf16[5,128,128]{2,1,0:T(8,128)(2,1)S(1)} collective-permute-done((bf16[5,128,128]{2,1,0:T(8,128)(2,1)S(1)}, bf16[5,128,128]{2,1,0:T(8,128)(2,1)S(1)}, u32[]{:S(2)}, u32[]{:S(2)}) %collective-permute-start) | collective-permute-done | bytes 163872 | tf_op jit(solution)/shard_map/ppermute | solution.py:281
  27.2 7.6 %collective-permute-start.3 = (bf16[52,128,128]{2,1,0:T(8,128)(2,1)S(1)}, bf16[52,128,128]{2,1,0:T(8,128)(2,1)S(1)}, u32[]{:S(2)}, u32[]{:S(2)}) collective-permute-start(bf16[52,128,128]{2,1,0:T(8,128)(2,1)S(1)} %bitcast.3), channel_id=1, source_target_pairs={{0,8},{1,9},{2,10},{3,11},{4,12},{5,13},{6,14},{7,15},{8,0},{9,1},... | collective-permute-start | bytes 5111816 | tf_op jit(solution)/shard_map/ppermute | solution.py:281
  34.8 0.7 collective-permute-start.1
  35.5 2.5 %collective-permute-done.3.refs_3_ = bf16[52,128,128]{2,1,0:T(8,128)(2,1)S(1)} collective-permute-done((bf16[52,128,128]{2,1,0:T(8,128)(2,1)S(1)}, bf16[52,128,128]{2,1,0:T(8,128)(2,1)S(1)}, u32[]{:S(2)}, u32[]{:S(2)}) %collective-permute-start.3) | collective-permute-done | bytes 1703968 | tf_op jit(solution)/shard_map/ppermute | solution.py:281
  38.0 1.4 %shard_map.49 = (bf16[40,128,128]{2,1,0:T(8,128)(2,1)S(1)}, bf16[5,128,128]{2,1,0:T(8,128)(2,1)S(1)}) custom-call(s32[339]{0:T(512)S(1)} %dynamic-slice_reduce_fusion.table.spots, bf16[17,128,128]{2,1,0:T(8,128)(2,1)S(1)} %get-tuple-element.28.refs_0_.own, bf16[52,128,128]{2,1,0:T(8,128)(2,1)S(1)} %bitcast.4, ...), custom_call_target="tpu_custom_call" | custom-call | tf_op jit(solution)/shard_map/pallas_call | solution.py:298
  39.4 9.1 %collective-permute-start.7 = (bf16[40,128,128]{2,1,0:T(8,128)(2,1)S(1)}, bf16[40,128,128]{2,1,0:T(8,128)(2,1)S(1)}, u32[]{:S(2)}, u32[]{:S(2)}) collective-permute-start(bf16[40,128,128]{2,1,0:T(8,128)(2,1)S(1)} %get-tuple-element.33), channel_id=1, source_target_pairs={{0,508},{1,509},{2,510},{3,511},{4,504},{5,505},{6,506},{7,507},{8... | collective-permute-start | bytes 3932168 | tf_op jit(solution)/shard_map/ppermute | solution.py:281
  48.7 12.0 %all_to_all.10 = bf16[4,5,128,128]{3,2,1,0:T(8,128)(2,1)S(1)} all-to-all(bf16[4,5,128,128]{3,2,1,0:T(8,128)(2,1)S(1)} %broadcast_in_dim.3), channel_id=1, replica_groups=mesh['y'=4,'zl'=8,'c'=2,'zh'=2,'x'=4] {'x'}, dimensions={0} | all-to-all | bytes 1310720 | tf_op jit(solution)/shard_map/all_to_all | solution.py:284
  60.7 11.1 %collective-permute-start.2 = (bf16[20,128,128]{2,1,0:T(8,128)(2,1)S(1)}, bf16[20,128,128]{2,1,0:T(8,128)(2,1)S(1)}, u32[]{:S(2)}, u32[]{:S(2)}) collective-permute-start(bf16[20,128,128]{2,1,0:T(8,128)(2,1)S(1)} %bitcast.7), channel_id=1, source_target_pairs={{0,8},{1,9},{2,10},{3,11},{4,12},{5,13},{6,14},{7,15},{8,0},{9,1},... | collective-permute-start | bytes 1966088 | tf_op jit(solution)/shard_map/ppermute | solution.py:281
  71.8 1.2 %shard_map.48 = bf16[20,128,128]{2,1,0:T(8,128)(2,1)S(1)} custom-call(s32[339]{0:T(512)S(1)} %dynamic-slice_reduce_fusion.table.spots, bf16[17,128,128]{2,1,0:T(8,128)(2,1)S(1)} %get-tuple-element.28.refs_0_.own, bf16[52,128,128]{2,1,0:T(8,128)(2,1)S(1)} %bitcast.5, bf16[20,128,128]{2,1,0:T(8,128)(2,1)S(1)} %bitcast.8, ...), custom_call_target="tpu_custom_call" | custom-call | tf_op jit(solution)/shard_map/pallas_call | solution.py:305
  73.0 1.9 %collective-permute-start.4 = (bf16[20,128,128]{2,1,0:T(8,128)(2,1)S(1)}, bf16[20,128,128]{2,1,0:T(8,128)(2,1)S(1)}, u32[]{:S(2)}, u32[]{:S(2)}) collective-permute-start(bf16[20,128,128]{2,1,0:T(8,128)(2,1)S(1)} %shard_map.48), channel_id=1, source_target_pairs={{0,508},{1,509},{2,510},{3,511},{4,504},{5,505},{6,506},{7,507},{8... | collective-permute-start | bytes 1966088 | tf_op jit(solution)/shard_map/ppermute | solution.py:281
  74.9 7.2 %collective-permute-start.6 = (bf16[5,128,128]{2,1,0:T(8,128)(2,1)S(1)}, bf16[5,128,128]{2,1,0:T(8,128)(2,1)S(1)}, u32[]{:S(2)}, u32[]{:S(2)}) collective-permute-start(bf16[5,128,128]{2,1,0:T(8,128)(2,1)S(1)} %get-tuple-element.31), channel_id=1, source_target_pairs={{0,503},{3,16},{8,511},{11,24},{19,32},{20,7},{27,40},{28,15},{35,... | collective-permute-start | bytes 491528 | tf_op jit(solution)/shard_map/ppermute | solution.py:281
  82.1 1.9 %collective-permute-start.5 = (bf16[5,128,128]{2,1,0:T(8,128)(2,1)S(1)}, bf16[5,128,128]{2,1,0:T(8,128)(2,1)S(1)}, u32[]{:S(2)}, u32[]{:S(2)}) collective-permute-start(bf16[5,128,128]{2,1,0:T(8,128)(2,1)S(1)} %get-tuple-element.31), channel_id=1, source_target_pairs={{0,502},{1,503},{2,16},{3,17},{8,510},{9,511},{10,24},{11,25},{18,... | collective-permute-start | bytes 491528 | tf_op jit(solution)/shard_map/ppermute | solution.py:281
  84.1 3.5 %shard_map.50.refs_4_ = bf16[189,128,128]{2,1,0:T(8,128)(2,1)S(1)} custom-call(s32[339]{0:T(512)S(1)} %dynamic-slice_reduce_fusion.table.spots, bf16[17,128,128]{2,1,0:T(8,128)(2,1)S(1)} %get-tuple-element.28.refs_0_.own, bf16[52,128,128]{2,1,0:T(8,128)(2,1)S(1)} %bitcast.6, bf16[20,128,128]{2,1,0:T(8,128)(2,1)S(1)} %bitcast.9, ...), custom_call_target="tpu_custom_call" | custom-call | tf_op jit(solution)/shard_map/pallas_call | solution.py:308
  87.6 3.8 %collective-permute-done.6.refs_3_ = bf16[5,128,128]{2,1,0:T(8,128)(2,1)S(1)} collective-permute-done((bf16[5,128,128]{2,1,0:T(8,128)(2,1)S(1)}, bf16[5,128,128]{2,1,0:T(8,128)(2,1)S(1)}, u32[]{:S(2)}, u32[]{:S(2)}) %collective-permute-start.6) | collective-permute-done | bytes 163872 | tf_op jit(solution)/shard_map/ppermute | solution.py:281
  91.4 4.3 %collective-permute-done.5.refs_2_ = bf16[5,128,128]{2,1,0:T(8,128)(2,1)S(1)} collective-permute-done((bf16[5,128,128]{2,1,0:T(8,128)(2,1)S(1)}, bf16[5,128,128]{2,1,0:T(8,128)(2,1)S(1)}, u32[]{:S(2)}, u32[]{:S(2)}) %collective-permute-start.5) | collective-permute-done | bytes 163872 | tf_op jit(solution)/shard_map/ppermute | solution.py:281
  95.8 6.5 %shard_map.51 = (f32[1,128,2688]{2,1,0:T(8,128)}, bf16[189,128,128]{2,1,0:T(8,128)(2,1)S(1)}) custom-call(s32[339]{0:T(512)S(1)} %dynamic-slice_reduce_fusion.table.spots, s32[1,21]{1,0:T(1,128)S(1)} %copy-done.3, bf16[128,2176]{1,0:T(8,128)(2,1)S(1)} %get-tuple-element.20.masked, ...), custom_call_target="tpu_custom_call", output_to_operand_aliasing={{1}: (7, {})} | custom-call | tf_op jit(solution)/shard_map/pallas_call | solution.py:310
  (11 shorter events, 0.2 us)
Async XLA Ops:
  0.0 1.1 %copy-start.1 = (bf16[1,128,2176]{2,1,0:T(8,128)(2,1)S(1)}, bf16[1,128,2176]{2,1,0:T(8,128)(2,1)}, u32[]{:S(2)}) copy-start(bf16[1,128,2176]{2,1,0:T(8,128)(2,1)} %strip.1) | copy-start | bytes 1671172
  1.1 0.7 copy-start.2
  2.7 1.2 %copy-start = (bf16[4,13,128,128]{3,2,1,0:T(8,128)(2,1)}, bf16[4,13,128,128]{3,2,1,0:T(8,128)(2,1)S(1)}, u32[]{:S(2)}) copy-start(bf16[4,13,128,128]{3,2,1,0:T(8,128)(2,1)S(1)} %get-tuple-element.23) | copy-start | bytes 5111812
  3.9 21.1 %all-to-all-start = ((bf16[4,13,128,128]{3,2,1,0:T(8,128)(2,1)}), bf16[4,13,128,128]{3,2,1,0:T(8,128)(2,1)S(1)}, u32[]{:S(2)}, u32[]{:S(2)}) async-start(bf16[4,13,128,128]{3,2,1,0:T(8,128)(2,1)} %copy-done), calls=%async_computation | async-start | bytes 3407872 | tf_op jit(solution)/shard_map/all_to_all | solution.py:284
  8.7 18.4 %collective-permute-start = (bf16[5,128,128]{2,1,0:T(8,128)(2,1)S(1)}, bf16[5,128,128]{2,1,0:T(8,128)(2,1)S(1)}, u32[]{:S(2)}, u32[]{:S(2)}) collective-permute-start(bf16[5,128,128]{2,1,0:T(8,128)(2,1)S(1)} %get-tuple-element.21.send1), channel_id=1, source_target_pairs={{0,4},{1,5},{2,6},{3,7},{4,0},{5,1},{6,2},{7,3},{8,12},{9,13},{10,... | collective-permute-start | bytes 491528 | tf_op jit(solution)/shard_map/ppermute | solution.py:281
  27.2 10.8 %collective-permute-start.3 = (bf16[52,128,128]{2,1,0:T(8,128)(2,1)S(1)}, bf16[52,128,128]{2,1,0:T(8,128)(2,1)S(1)}, u32[]{:S(2)}, u32[]{:S(2)}) collective-permute-start(bf16[52,128,128]{2,1,0:T(8,128)(2,1)S(1)} %bitcast.3), channel_id=1, source_target_pairs={{0,8},{1,9},{2,10},{3,11},{4,12},{5,13},{6,14},{7,15},{8,0},{9,1},... | collective-permute-start | bytes 5111816 | tf_op jit(solution)/shard_map/ppermute | solution.py:281
  34.8 25.9 %collective-permute-start.1 = (bf16[24,128,128]{2,1,0:T(8,128)(2,1)S(1)}, bf16[24,128,128]{2,1,0:T(8,128)(2,1)S(1)}, u32[]{:S(2)}, u32[]{:S(2)}) collective-permute-start(bf16[24,128,128]{2,1,0:T(8,128)(2,1)S(1)} %shard_map.47), channel_id=1, source_target_pairs={{0,4},{1,5},{2,6},{3,7},{116,128},{117,129},{118,130},{119,131},{1... | collective-permute-start | bytes 2359304 | tf_op jit(solution)/shard_map/ppermute | solution.py:281
  39.4 44.6 %collective-permute-start.7 = (bf16[40,128,128]{2,1,0:T(8,128)(2,1)S(1)}, bf16[40,128,128]{2,1,0:T(8,128)(2,1)S(1)}, u32[]{:S(2)}, u32[]{:S(2)}) collective-permute-start(bf16[40,128,128]{2,1,0:T(8,128)(2,1)S(1)} %get-tuple-element.33), channel_id=1, source_target_pairs={{0,508},{1,509},{2,510},{3,511},{4,504},{5,505},{6,506},{7,507},{8... | collective-permute-start | bytes 3932168 | tf_op jit(solution)/shard_map/ppermute | solution.py:281
  60.7 27.0 %collective-permute-start.2 = (bf16[20,128,128]{2,1,0:T(8,128)(2,1)S(1)}, bf16[20,128,128]{2,1,0:T(8,128)(2,1)S(1)}, u32[]{:S(2)}, u32[]{:S(2)}) collective-permute-start(bf16[20,128,128]{2,1,0:T(8,128)(2,1)S(1)} %bitcast.7), channel_id=1, source_target_pairs={{0,8},{1,9},{2,10},{3,11},{4,12},{5,13},{6,14},{7,15},{8,0},{9,1},... | collective-permute-start | bytes 1966088 | tf_op jit(solution)/shard_map/ppermute | solution.py:281
  73.0 22.8 %collective-permute-start.4 = (bf16[20,128,128]{2,1,0:T(8,128)(2,1)S(1)}, bf16[20,128,128]{2,1,0:T(8,128)(2,1)S(1)}, u32[]{:S(2)}, u32[]{:S(2)}) collective-permute-start(bf16[20,128,128]{2,1,0:T(8,128)(2,1)S(1)} %shard_map.48), channel_id=1, source_target_pairs={{0,508},{1,509},{2,510},{3,511},{4,504},{5,505},{6,506},{7,507},{8... | collective-permute-start | bytes 1966088 | tf_op jit(solution)/shard_map/ppermute | solution.py:281
  74.9 20.8 %copy-start.3 = (s32[1,21]{1,0:T(1,128)S(1)}, s32[1,21]{1,0:T(1,128)}, u32[]{:S(2)}) copy-start(s32[1,21]{1,0:T(1,128)} %keep.1) | copy-start | bytes 256
  74.9 16.5 %collective-permute-start.6 = (bf16[5,128,128]{2,1,0:T(8,128)(2,1)S(1)}, bf16[5,128,128]{2,1,0:T(8,128)(2,1)S(1)}, u32[]{:S(2)}, u32[]{:S(2)}) collective-permute-start(bf16[5,128,128]{2,1,0:T(8,128)(2,1)S(1)} %get-tuple-element.31), channel_id=1, source_target_pairs={{0,503},{3,16},{8,511},{11,24},{19,32},{20,7},{27,40},{28,15},{35,... | collective-permute-start | bytes 491528 | tf_op jit(solution)/shard_map/ppermute | solution.py:281
  82.1 13.6 %collective-permute-start.5 = (bf16[5,128,128]{2,1,0:T(8,128)(2,1)S(1)}, bf16[5,128,128]{2,1,0:T(8,128)(2,1)S(1)}, u32[]{:S(2)}, u32[]{:S(2)}) collective-permute-start(bf16[5,128,128]{2,1,0:T(8,128)(2,1)S(1)} %get-tuple-element.31), channel_id=1, source_target_pairs={{0,502},{1,503},{2,16},{3,17},{8,510},{9,511},{10,24},{11,25},{18,... | collective-permute-start | bytes 491528 | tf_op jit(solution)/shard_map/ppermute | solution.py:281

commit v12 on v9

--- a/solution.py
+++ b/solution.py
@@ -273,11 +273,10 @@
         send_s = call(functools.partial(gather_kernel, 2, starts[0]), vmem(ks, BLK, BLK), 1, 2)(table, own, x)
         got1, send_s, x = lax.optimization_barrier((got1, send_s, x))
         got_s, got_c = send(send_s, "seam"), send(x, "c")
-        own, x, got_c = lax.optimization_barrier((own, x, got_c))
         send_a = call(functools.partial(gather_kernel, 2, starts[1]), vmem(ka, BLK, BLK), 1, 2)(table, own, x)
         got_a = send(send_a, "z")
         w = spread(jnp.broadcast_to(got1, (4, k1, BLK, BLK)))
-        w, got_s = lax.optimization_barrier((w, got_s))
+        w, got_s, got_c = lax.optimization_barrier((w, got_s, got_c))
         send_b, send_f = call(
             functools.partial(gather_kernel, 4, starts[2]), (vmem(kb, BLK, BLK), vmem(kf, BLK, BLK)), 1, 4,
         )(table, own, x, w, got_c)

time: 100 us -> 100 us (level)
  waiting for transfers between devices: 14.8 us -> 12 us
  starting transfers between devices: 54.2 us -> 56.9 us
    ppermute x7, starting transfers between devices: 49.3 us -> 52.1 us  [send(): return lax.ppermute(array, AXES, moves[name])]
    ppermute x7, waiting for transfers between devices: 14.7 us -> 11.9 us  [send(): return lax.ppermute(array, AXES, moves[name])]
  transfers between devices with their start and end apart: 8 -> 8, of which waited for: 4 -> 3; matrix products, arithmetic and copies ran while one was open for 1% -> 1% of each run, Pallas kernels for 8% -> 8%
where the time goes in v12:
time: 100 us; the launch traced here: 99.9 us
  starting transfers between devices  56.9 us (57%)
  Pallas kernels  15.1 us (15%)
  waiting for transfers between devices  12 us (12%)
  blocking collectives  12 us (12%)
  local copies, waits for them, and re-layouts  3.78 us (4%)
    ppermute x7, starting transfers between devices, send(): return lax.ppermute(array, AXES, moves[name])  52.1 us
    all_to_all x1, blocking collectives, spread(): return lax.all_to_all(copies, 'x', 0, 0).reshape(-1, BLK, BLK)  12 us
    ppermute x7, waiting for transfers between devices, send(): return lax.ppermute(array, AXES, moves[name])  11.9 us
    pallas_call x1, Pallas kernels, body(): pl.pallas_call(functools.partial(final_kernel, late), out_shape=(vmem(1,...  6.55 us
    all_to_all x1, starting transfers between devices, spread(): return lax.all_to_all(copies, 'x', 0, 0).reshape(-1, BLK, BLK)  4.84 us
    pallas_call x1, Pallas kernels, body(): call(functools.partial(early_kernel, starts[4]), vmem(DUMMY, BLK, BLK), 1...  3.55 us
    unnamed x8, local copies, waits for them, and re-layouts  2.91 us
  transfers between devices with their start and end apart: 8, of which 3 were waited for; matrix products, arithmetic and copies ran while one was open for 1% of the time, Pallas kernels for 8%

profile of v12, /device:TPU:1, one launch (start us, length us, event | category | flops | bytes accessed | tf_op | source)
XLA Modules:
  0.0 99.9 jit_solution(4509363644693566104)
XLA Ops:
  0.0 1.1 %copy-done.1 = bf16[1,128,2176]{2,1,0:T(8,128)(2,1)S(1)} copy-done((bf16[1,128,2176]{2,1,0:T(8,128)(2,1)S(1)}, bf16[1,128,2176]{2,1,0:T(8,128)(2,1)}, u32[]{:S(2)}) %copy-start.1) | copy-done | bytes 557080
  1.1 0.7 copy-done.2
  1.7 1.0 shard_map.46
  2.7 1.2 %copy-done = bf16[4,13,128,128]{3,2,1,0:T(8,128)(2,1)} copy-done((bf16[4,13,128,128]{3,2,1,0:T(8,128)(2,1)}, bf16[4,13,128,128]{3,2,1,0:T(8,128)(2,1)S(1)}, u32[]{:S(2)}) %copy-start) | copy-done | bytes 1703960
  3.9 4.8 %all-to-all-start = ((bf16[4,13,128,128]{3,2,1,0:T(8,128)(2,1)}), bf16[4,13,128,128]{3,2,1,0:T(8,128)(2,1)S(1)}, u32[]{:S(2)}, u32[]{:S(2)}) async-start(bf16[4,13,128,128]{3,2,1,0:T(8,128)(2,1)} %copy-done), calls=%async_computation | async-start | bytes 3407872 | tf_op jit(solution)/shard_map/all_to_all | solution.py:263
  8.7 15.4 %collective-permute-start = (bf16[5,128,128]{2,1,0:T(8,128)(2,1)S(1)}, bf16[5,128,128]{2,1,0:T(8,128)(2,1)S(1)}, u32[]{:S(2)}, u32[]{:S(2)}) collective-permute-start(bf16[5,128,128]{2,1,0:T(8,128)(2,1)S(1)} %get-tuple-element.19), channel_id=1, source_target_pairs={{0,4},{1,5},{2,6},{3,7},{4,0},{5,1},{6,2},{7,3},{8,12},{9,13},{10,... | collective-permute-start | bytes 491528 | tf_op jit(solution)/shard_map/ppermute | solution.py:260
  24.2 0.7 dynamic-slice_reduce_fusion.table.spots
  24.9 0.1 all-to-all-done
  25.0 1.0 %shard_map.47 = bf16[24,128,128]{2,1,0:T(8,128)(2,1)S(1)} custom-call(s32[351]{0:T(512)S(1)} %dynamic-slice_reduce_fusion.table.spots, bf16[17,128,128]{2,1,0:T(8,128)(2,1)S(1)} %get-tuple-element.20.refs_0_, bf16[52,128,128]{2,1,0:T(8,128)(2,1)S(1)} %bitcast.2), custom_call_target="tpu_custom_call" | custom-call | tf_op jit(solution)/shard_map/pallas_call | solution.py:273
  26.1 1.1 %collective-permute-done = bf16[5,128,128]{2,1,0:T(8,128)(2,1)S(1)} collective-permute-done((bf16[5,128,128]{2,1,0:T(8,128)(2,1)S(1)}, bf16[5,128,128]{2,1,0:T(8,128)(2,1)S(1)}, u32[]{:S(2)}, u32[]{:S(2)}) %collective-permute-start) | collective-permute-done | bytes 163872 | tf_op jit(solution)/shard_map/ppermute | solution.py:260
  27.2 7.6 %collective-permute-start.2 = (bf16[52,128,128]{2,1,0:T(8,128)(2,1)S(1)}, bf16[52,128,128]{2,1,0:T(8,128)(2,1)S(1)}, u32[]{:S(2)}, u32[]{:S(2)}) collective-permute-start(bf16[52,128,128]{2,1,0:T(8,128)(2,1)S(1)} %bitcast.3), channel_id=1, source_target_pairs={{0,8},{1,9},{2,10},{3,11},{4,12},{5,13},{6,14},{7,15},{8,0},{9,1},... | collective-permute-start | bytes 5111816 | tf_op jit(solution)/shard_map/ppermute | solution.py:260
  34.8 0.7 collective-permute-start.1
  35.5 1.4 %shard_map.49 = bf16[40,128,128]{2,1,0:T(8,128)(2,1)S(1)} custom-call(s32[351]{0:T(512)S(1)} %dynamic-slice_reduce_fusion.table.spots, bf16[17,128,128]{2,1,0:T(8,128)(2,1)S(1)} %get-tuple-element.20.refs_0_, bf16[52,128,128]{2,1,0:T(8,128)(2,1)S(1)} %bitcast.4), custom_call_target="tpu_custom_call" | custom-call | tf_op jit(solution)/shard_map/pallas_call | solution.py:276
  36.9 8.8 %collective-permute-start.6 = (bf16[40,128,128]{2,1,0:T(8,128)(2,1)S(1)}, bf16[40,128,128]{2,1,0:T(8,128)(2,1)S(1)}, u32[]{:S(2)}, u32[]{:S(2)}) collective-permute-start(bf16[40,128,128]{2,1,0:T(8,128)(2,1)S(1)} %shard_map.49), channel_id=1, source_target_pairs={{0,508},{1,509},{2,510},{3,511},{4,504},{5,505},{6,506},{7,507},{8... | collective-permute-start | bytes 3932168 | tf_op jit(solution)/shard_map/ppermute | solution.py:260
  45.7 0.1 broadcast_in_dim.3
  45.8 12.0 %all_to_all.10 = bf16[4,5,128,128]{3,2,1,0:T(8,128)(2,1)S(1)} all-to-all(bf16[4,5,128,128]{3,2,1,0:T(8,128)(2,1)S(1)} %broadcast_in_dim.3), channel_id=1, replica_groups=mesh['y'=4,'zl'=8,'c'=2,'zh'=2,'x'=4] {'x'}, dimensions={0} | all-to-all | bytes 1310720 | tf_op jit(solution)/shard_map/all_to_all | solution.py:263
  57.8 1.6 %shard_map.48 = (bf16[21,128,128]{2,1,0:T(8,128)(2,1)S(1)}, bf16[10,128,128]{2,1,0:T(8,128)(2,1)S(1)}) custom-call(s32[351]{0:T(512)S(1)} %dynamic-slice_reduce_fusion.table.spots, bf16[17,128,128]{2,1,0:T(8,128)(2,1)S(1)} %get-tuple-element.20.refs_0_, bf16[52,128,128]{2,1,0:T(8,128)(2,1)S(1)} %bitcast.5, bf16[20,128,128]{2,1,0:T(8,128)(2,1)S(1)} %bitcast.7, ...), custom_call_target="tpu_custom_call" | custom-call | tf_op jit(solution)/shard_map/pallas_call | solution.py:280
  59.3 5.8 %collective-permute-start.4 = (bf16[21,128,128]{2,1,0:T(8,128)(2,1)S(1)}, bf16[21,128,128]{2,1,0:T(8,128)(2,1)S(1)}, u32[]{:S(2)}, u32[]{:S(2)}) collective-permute-start(bf16[21,128,128]{2,1,0:T(8,128)(2,1)S(1)} %get-tuple-element.27), channel_id=1, source_target_pairs={{0,508},{1,509},{2,510},{3,511},{4,504},{5,505},{6,506},{7,507},{8... | collective-permute-start | bytes 2064392 | tf_op jit(solution)/shard_map/ppermute | solution.py:260
  65.2 11.9 %collective-permute-start.3 = (bf16[20,128,128]{2,1,0:T(8,128)(2,1)S(1)}, bf16[20,128,128]{2,1,0:T(8,128)(2,1)S(1)}, u32[]{:S(2)}, u32[]{:S(2)}) collective-permute-start(bf16[20,128,128]{2,1,0:T(8,128)(2,1)S(1)} %bitcast.8), channel_id=1, source_target_pairs={{0,8},{1,9},{2,10},{3,11},{4,12},{5,13},{6,14},{7,15},{8,0},{9,1},... | collective-permute-start | bytes 1966088 | tf_op jit(solution)/shard_map/ppermute | solution.py:260
  77.0 0.0 copy-start.3
  77.0 1.9 %collective-permute-start.5 = (bf16[10,128,128]{2,1,0:T(8,128)(2,1)S(1)}, bf16[10,128,128]{2,1,0:T(8,128)(2,1)S(1)}, u32[]{:S(2)}, u32[]{:S(2)}) collective-permute-start(bf16[10,128,128]{2,1,0:T(8,128)(2,1)S(1)} %get-tuple-element.28), channel_id=1, source_target_pairs={{0,16},{1,17},{2,502},{3,503},{8,24},{9,25},{10,510},{11,511},{16,... | collective-permute-start | bytes 983048 | tf_op jit(solution)/shard_map/ppermute | solution.py:260
  79.0 3.5 %shard_map.50.refs_3_ = bf16[189,128,128]{2,1,0:T(8,128)(2,1)S(1)} custom-call(s32[351]{0:T(512)S(1)} %dynamic-slice_reduce_fusion.table.spots, bf16[17,128,128]{2,1,0:T(8,128)(2,1)S(1)} %get-tuple-element.20.refs_0_, bf16[52,128,128]{2,1,0:T(8,128)(2,1)S(1)} %bitcast.6, bf16[20,128,128]{2,1,0:T(8,128)(2,1)S(1)} %bitcast.9, ...), custom_call_target="tpu_custom_call" | custom-call | tf_op jit(solution)/shard_map/pallas_call | solution.py:285
  82.5 10.8 %collective-permute-done.5.refs_2_ = bf16[10,128,128]{2,1,0:T(8,128)(2,1)S(1)} collective-permute-done((bf16[10,128,128]{2,1,0:T(8,128)(2,1)S(1)}, bf16[10,128,128]{2,1,0:T(8,128)(2,1)S(1)}, u32[]{:S(2)}, u32[]{:S(2)}) %collective-permute-start.5) | collective-permute-done | bytes 327712 | tf_op jit(solution)/shard_map/ppermute | solution.py:260
  93.3 6.5 %shard_map.51 = (f32[1,128,2688]{2,1,0:T(8,128)}, bf16[189,128,128]{2,1,0:T(8,128)(2,1)S(1)}) custom-call(s32[351]{0:T(512)S(1)} %dynamic-slice_reduce_fusion.table.spots, s32[1,21]{1,0:T(1,128)S(1)} %copy-done.3, bf16[128,2176]{1,0:T(8,128)(2,1)S(1)} %get-tuple-element.18.masked, ...), custom_call_target="tpu_custom_call", output_to_operand_aliasing={{1}: (6, {})} | custom-call | tf_op jit(solution)/shard_map/pallas_call | solution.py:287
  (9 shorter events, 0.0 us)
Async XLA Ops:
  0.0 1.1 %copy-start.1 = (bf16[1,128,2176]{2,1,0:T(8,128)(2,1)S(1)}, bf16[1,128,2176]{2,1,0:T(8,128)(2,1)}, u32[]{:S(2)}) copy-start(bf16[1,128,2176]{2,1,0:T(8,128)(2,1)} %strip.1) | copy-start | bytes 1671172
  1.1 0.7 copy-start.2
  2.7 1.2 %copy-start = (bf16[4,13,128,128]{3,2,1,0:T(8,128)(2,1)}, bf16[4,13,128,128]{3,2,1,0:T(8,128)(2,1)S(1)}, u32[]{:S(2)}) copy-start(bf16[4,13,128,128]{3,2,1,0:T(8,128)(2,1)S(1)} %get-tuple-element.21) | copy-start | bytes 5111812
  3.9 21.1 %all-to-all-start = ((bf16[4,13,128,128]{3,2,1,0:T(8,128)(2,1)}), bf16[4,13,128,128]{3,2,1,0:T(8,128)(2,1)S(1)}, u32[]{:S(2)}, u32[]{:S(2)}) async-start(bf16[4,13,128,128]{3,2,1,0:T(8,128)(2,1)} %copy-done), calls=%async_computation | async-start | bytes 3407872 | tf_op jit(solution)/shard_map/all_to_all | solution.py:263
  8.7 18.4 %collective-permute-start = (bf16[5,128,128]{2,1,0:T(8,128)(2,1)S(1)}, bf16[5,128,128]{2,1,0:T(8,128)(2,1)S(1)}, u32[]{:S(2)}, u32[]{:S(2)}) collective-permute-start(bf16[5,128,128]{2,1,0:T(8,128)(2,1)S(1)} %get-tuple-element.19), channel_id=1, source_target_pairs={{0,4},{1,5},{2,6},{3,7},{4,0},{5,1},{6,2},{7,3},{8,12},{9,13},{10,... | collective-permute-start | bytes 491528 | tf_op jit(solution)/shard_map/ppermute | solution.py:260
  27.2 30.6 %collective-permute-start.2 = (bf16[52,128,128]{2,1,0:T(8,128)(2,1)S(1)}, bf16[52,128,128]{2,1,0:T(8,128)(2,1)S(1)}, u32[]{:S(2)}, u32[]{:S(2)}) collective-permute-start(bf16[52,128,128]{2,1,0:T(8,128)(2,1)S(1)} %bitcast.3), channel_id=1, source_target_pairs={{0,8},{1,9},{2,10},{3,11},{4,12},{5,13},{6,14},{7,15},{8,0},{9,1},... | collective-permute-start | bytes 5111816 | tf_op jit(solution)/shard_map/ppermute | solution.py:260
  34.8 23.0 %collective-permute-start.1 = (bf16[24,128,128]{2,1,0:T(8,128)(2,1)S(1)}, bf16[24,128,128]{2,1,0:T(8,128)(2,1)S(1)}, u32[]{:S(2)}, u32[]{:S(2)}) collective-permute-start(bf16[24,128,128]{2,1,0:T(8,128)(2,1)S(1)} %shard_map.47), channel_id=1, source_target_pairs={{0,4},{1,5},{2,6},{3,7},{116,128},{117,129},{118,130},{119,131},{1... | collective-permute-start | bytes 2359304 | tf_op jit(solution)/shard_map/ppermute | solution.py:260
  36.9 42.1 %collective-permute-start.6 = (bf16[40,128,128]{2,1,0:T(8,128)(2,1)S(1)}, bf16[40,128,128]{2,1,0:T(8,128)(2,1)S(1)}, u32[]{:S(2)}, u32[]{:S(2)}) collective-permute-start(bf16[40,128,128]{2,1,0:T(8,128)(2,1)S(1)} %shard_map.49), channel_id=1, source_target_pairs={{0,508},{1,509},{2,510},{3,511},{4,504},{5,505},{6,506},{7,507},{8... | collective-permute-start | bytes 3932168 | tf_op jit(solution)/shard_map/ppermute | solution.py:260
  59.3 34.0 %collective-permute-start.4 = (bf16[21,128,128]{2,1,0:T(8,128)(2,1)S(1)}, bf16[21,128,128]{2,1,0:T(8,128)(2,1)S(1)}, u32[]{:S(2)}, u32[]{:S(2)}) collective-permute-start(bf16[21,128,128]{2,1,0:T(8,128)(2,1)S(1)} %get-tuple-element.27), channel_id=1, source_target_pairs={{0,508},{1,509},{2,510},{3,511},{4,504},{5,505},{6,506},{7,507},{8... | collective-permute-start | bytes 2064392 | tf_op jit(solution)/shard_map/ppermute | solution.py:260
  65.2 28.1 %collective-permute-start.3 = (bf16[20,128,128]{2,1,0:T(8,128)(2,1)S(1)}, bf16[20,128,128]{2,1,0:T(8,128)(2,1)S(1)}, u32[]{:S(2)}, u32[]{:S(2)}) collective-permute-start(bf16[20,128,128]{2,1,0:T(8,128)(2,1)S(1)} %bitcast.8), channel_id=1, source_target_pairs={{0,8},{1,9},{2,10},{3,11},{4,12},{5,13},{6,14},{7,15},{8,0},{9,1},... | collective-permute-start | bytes 1966088 | tf_op jit(solution)/shard_map/ppermute | solution.py:260
  77.0 16.3 %copy-start.3 = (s32[1,21]{1,0:T(1,128)S(1)}, s32[1,21]{1,0:T(1,128)}, u32[]{:S(2)}) copy-start(s32[1,21]{1,0:T(1,128)} %keep.1) | copy-start | bytes 256
  77.0 16.3 %collective-permute-start.5 = (bf16[10,128,128]{2,1,0:T(8,128)(2,1)S(1)}, bf16[10,128,128]{2,1,0:T(8,128)(2,1)S(1)}, u32[]{:S(2)}, u32[]{:S(2)}) collective-permute-start(bf16[10,128,128]{2,1,0:T(8,128)(2,1)S(1)} %get-tuple-element.28), channel_id=1, source_target_pairs={{0,16},{1,17},{2,502},{3,503},{8,24},{9,25},{10,510},{11,511},{16,... | collective-permute-start | bytes 983048 | tf_op jit(solution)/shard_map/ppermute | solution.py:260

commit v13 on v12

--- a/solution.py
+++ b/solution.py
@@ -218,15 +218,10 @@
     for source in sources:
 
         def put(k, carry, source=source, low=low):
-            at = spots[low + k]
-
-            @pl.when(at < DUMMY)
-            def _():
-                pool[at] = source[k]
-
+            pool[spots[low + k]] = source[k]
             return carry
 
-        lax.fori_loop(0, source.shape[0], put, 0)
+        lax.fori_loop(0, source.shape[0], put, 0, unroll=True)
         low += source.shape[0]
 
 
@@ -282,11 +277,11 @@
         )(table, own, x, w, got_c)
         got_b, got_f, got_d = send(send_b, "z"), send(send_f, "far"), send(w, "c")
         first = [own, x, w, got_c, got_s, got_a]
-        pool = call(functools.partial(early_kernel, starts[4]), vmem(DUMMY, BLK, BLK), 1, len(first))(table, *first)
+        pool = call(functools.partial(early_kernel, starts[4]), vmem(DUMMY + 1, BLK, BLK), 1, len(first))(table, *first)
         late = starts[4] + sum(q.shape[0] for q in first)
         purified, _ = pl.pallas_call(
             functools.partial(final_kernel, late),
-            out_shape=(vmem(1, BLK, KEPT * BLK, dtype=jnp.float32), vmem(DUMMY, BLK, BLK)),
+            out_shape=(vmem(1, BLK, KEPT * BLK, dtype=jnp.float32), vmem(DUMMY + 1, BLK, BLK)),
             in_specs=[scalars()] * 2 + [whole()] * 5,
             out_specs=(whole(), whole()),
             scratch_shapes=[pltpu.VMEM((BLK, KEPT * BLK), jnp.float32), pltpu.VMEM((BLK, KEPT * BLK), jnp.bfloat16)],

time: 100 us -> 99.7 us (level)
  Pallas kernels: 15.1 us -> 11.9 us
  waiting for transfers between devices: 12 us -> 14.5 us
    ppermute x7, waiting for transfers between devices: 11.9 us -> 14.5 us  [send(): return lax.ppermute(array, AXES, moves[name])]
    pallas_call x1, Pallas kernels: 3.55 us -> 1 us  [body(): call(functools.partial(early_kernel, starts[4]), vmem(DUMMY + 1, BLK, BLK...]
  transfers between devices with their start and end apart: 8 -> 8, of which waited for: 3 -> 3; matrix products, arithmetic and copies ran while one was open for 1% -> 1% of each run, Pallas kernels for 8% -> 5%
where the time goes in v13:
time: 99.7 us; the launch traced here: 99.2 us
  starting transfers between devices  56.9 us (57%)
  waiting for transfers between devices  14.5 us (15%)
  blocking collectives  12 us (12%)
  Pallas kernels  11.9 us (12%)
  local copies, waits for them, and re-layouts  3.78 us (4%)
    ppermute x7, starting transfers between devices, send(): return lax.ppermute(array, AXES, moves[name])  52.1 us
    ppermute x7, waiting for transfers between devices, send(): return lax.ppermute(array, AXES, moves[name])  14.5 us
    all_to_all x1, blocking collectives, spread(): return lax.all_to_all(copies, 'x', 0, 0).reshape(-1, BLK, BLK)  12 us
    pallas_call x1, Pallas kernels, body(): pl.pallas_call(functools.partial(final_kernel, late), out_shape=(vmem(1,...  5.91 us
    all_to_all x1, starting transfers between devices, spread(): return lax.all_to_all(copies, 'x', 0, 0).reshape(-1, BLK, BLK)  4.84 us
    unnamed x8, local copies, waits for them, and re-layouts  2.91 us
  transfers between devices with their start and end apart: 8, of which 3 were waited for; matrix products, arithmetic and copies ran while one was open for 1% of the time, Pallas kernels for 5%

profile of v13, /device:TPU:1, one launch (start us, length us, event | category | flops | bytes accessed | tf_op | source)
XLA Modules:
  0.0 99.2 jit_solution(8591072488097181966)
XLA Ops:
  0.0 1.1 %copy-done.1 = bf16[1,128,2176]{2,1,0:T(8,128)(2,1)S(1)} copy-done((bf16[1,128,2176]{2,1,0:T(8,128)(2,1)S(1)}, bf16[1,128,2176]{2,1,0:T(8,128)(2,1)}, u32[]{:S(2)}) %copy-start.1) | copy-done | bytes 557080
  1.1 0.7 copy-done.2
  1.7 1.0 shard_map.46
  2.7 1.2 %copy-done = bf16[4,13,128,128]{3,2,1,0:T(8,128)(2,1)} copy-done((bf16[4,13,128,128]{3,2,1,0:T(8,128)(2,1)}, bf16[4,13,128,128]{3,2,1,0:T(8,128)(2,1)S(1)}, u32[]{:S(2)}) %copy-start) | copy-done | bytes 1703960
  3.9 4.8 %all-to-all-start = ((bf16[4,13,128,128]{3,2,1,0:T(8,128)(2,1)}), bf16[4,13,128,128]{3,2,1,0:T(8,128)(2,1)S(1)}, u32[]{:S(2)}, u32[]{:S(2)}) async-start(bf16[4,13,128,128]{3,2,1,0:T(8,128)(2,1)} %copy-done), calls=%async_computation | async-start | bytes 3407872 | tf_op jit(solution)/shard_map/all_to_all | solution.py:258
  8.7 15.4 %collective-permute-start = (bf16[5,128,128]{2,1,0:T(8,128)(2,1)S(1)}, bf16[5,128,128]{2,1,0:T(8,128)(2,1)S(1)}, u32[]{:S(2)}, u32[]{:S(2)}) collective-permute-start(bf16[5,128,128]{2,1,0:T(8,128)(2,1)S(1)} %get-tuple-element.19), channel_id=1, source_target_pairs={{0,4},{1,5},{2,6},{3,7},{4,0},{5,1},{6,2},{7,3},{8,12},{9,13},{10,... | collective-permute-start | bytes 491528 | tf_op jit(solution)/shard_map/ppermute | solution.py:255
  24.2 0.7 dynamic-slice_reduce_fusion.table.spots
  24.9 0.1 all-to-all-done
  25.0 1.0 %shard_map.47 = bf16[24,128,128]{2,1,0:T(8,128)(2,1)S(1)} custom-call(s32[351]{0:T(512)S(1)} %dynamic-slice_reduce_fusion.table.spots, bf16[17,128,128]{2,1,0:T(8,128)(2,1)S(1)} %get-tuple-element.20.refs_0_, bf16[52,128,128]{2,1,0:T(8,128)(2,1)S(1)} %bitcast.2), custom_call_target="tpu_custom_call" | custom-call | tf_op jit(solution)/shard_map/pallas_call | solution.py:268
  26.1 1.1 %collective-permute-done = bf16[5,128,128]{2,1,0:T(8,128)(2,1)S(1)} collective-permute-done((bf16[5,128,128]{2,1,0:T(8,128)(2,1)S(1)}, bf16[5,128,128]{2,1,0:T(8,128)(2,1)S(1)}, u32[]{:S(2)}, u32[]{:S(2)}) %collective-permute-start) | collective-permute-done | bytes 163872 | tf_op jit(solution)/shard_map/ppermute | solution.py:255
  27.2 7.6 %collective-permute-start.2 = (bf16[52,128,128]{2,1,0:T(8,128)(2,1)S(1)}, bf16[52,128,128]{2,1,0:T(8,128)(2,1)S(1)}, u32[]{:S(2)}, u32[]{:S(2)}) collective-permute-start(bf16[52,128,128]{2,1,0:T(8,128)(2,1)S(1)} %bitcast.3), channel_id=1, source_target_pairs={{0,8},{1,9},{2,10},{3,11},{4,12},{5,13},{6,14},{7,15},{8,0},{9,1},... | collective-permute-start | bytes 5111816 | tf_op jit(solution)/shard_map/ppermute | solution.py:255
  34.8 0.7 collective-permute-start.1
  35.5 1.4 %shard_map.49 = bf16[40,128,128]{2,1,0:T(8,128)(2,1)S(1)} custom-call(s32[351]{0:T(512)S(1)} %dynamic-slice_reduce_fusion.table.spots, bf16[17,128,128]{2,1,0:T(8,128)(2,1)S(1)} %get-tuple-element.20.refs_0_, bf16[52,128,128]{2,1,0:T(8,128)(2,1)S(1)} %bitcast.4), custom_call_target="tpu_custom_call" | custom-call | tf_op jit(solution)/shard_map/pallas_call | solution.py:271
  36.9 8.8 %collective-permute-start.6 = (bf16[40,128,128]{2,1,0:T(8,128)(2,1)S(1)}, bf16[40,128,128]{2,1,0:T(8,128)(2,1)S(1)}, u32[]{:S(2)}, u32[]{:S(2)}) collective-permute-start(bf16[40,128,128]{2,1,0:T(8,128)(2,1)S(1)} %shard_map.49), channel_id=1, source_target_pairs={{0,508},{1,509},{2,510},{3,511},{4,504},{5,505},{6,506},{7,507},{8... | collective-permute-start | bytes 3932168 | tf_op jit(solution)/shard_map/ppermute | solution.py:255
  45.7 0.1 broadcast_in_dim.3
  45.8 12.0 %all_to_all.10 = bf16[4,5,128,128]{3,2,1,0:T(8,128)(2,1)S(1)} all-to-all(bf16[4,5,128,128]{3,2,1,0:T(8,128)(2,1)S(1)} %broadcast_in_dim.3), channel_id=1, replica_groups=mesh['y'=4,'zl'=8,'c'=2,'zh'=2,'x'=4] {'x'}, dimensions={0} | all-to-all | bytes 1310720 | tf_op jit(solution)/shard_map/all_to_all | solution.py:258
  57.8 1.6 %shard_map.48 = (bf16[21,128,128]{2,1,0:T(8,128)(2,1)S(1)}, bf16[10,128,128]{2,1,0:T(8,128)(2,1)S(1)}) custom-call(s32[351]{0:T(512)S(1)} %dynamic-slice_reduce_fusion.table.spots, bf16[17,128,128]{2,1,0:T(8,128)(2,1)S(1)} %get-tuple-element.20.refs_0_, bf16[52,128,128]{2,1,0:T(8,128)(2,1)S(1)} %bitcast.5, bf16[20,128,128]{2,1,0:T(8,128)(2,1)S(1)} %bitcast.7, ...), custom_call_target="tpu_custom_call" | custom-call | tf_op jit(solution)/shard_map/pallas_call | solution.py:275
  59.3 5.8 %collective-permute-start.4 = (bf16[21,128,128]{2,1,0:T(8,128)(2,1)S(1)}, bf16[21,128,128]{2,1,0:T(8,128)(2,1)S(1)}, u32[]{:S(2)}, u32[]{:S(2)}) collective-permute-start(bf16[21,128,128]{2,1,0:T(8,128)(2,1)S(1)} %get-tuple-element.27), channel_id=1, source_target_pairs={{0,508},{1,509},{2,510},{3,511},{4,504},{5,505},{6,506},{7,507},{8... | collective-permute-start | bytes 2064392 | tf_op jit(solution)/shard_map/ppermute | solution.py:255
  65.2 11.9 %collective-permute-start.3 = (bf16[20,128,128]{2,1,0:T(8,128)(2,1)S(1)}, bf16[20,128,128]{2,1,0:T(8,128)(2,1)S(1)}, u32[]{:S(2)}, u32[]{:S(2)}) collective-permute-start(bf16[20,128,128]{2,1,0:T(8,128)(2,1)S(1)} %bitcast.8), channel_id=1, source_target_pairs={{0,8},{1,9},{2,10},{3,11},{4,12},{5,13},{6,14},{7,15},{8,0},{9,1},... | collective-permute-start | bytes 1966088 | tf_op jit(solution)/shard_map/ppermute | solution.py:255
  77.0 0.0 copy-start.3
  77.0 1.9 %collective-permute-start.5 = (bf16[10,128,128]{2,1,0:T(8,128)(2,1)S(1)}, bf16[10,128,128]{2,1,0:T(8,128)(2,1)S(1)}, u32[]{:S(2)}, u32[]{:S(2)}) collective-permute-start(bf16[10,128,128]{2,1,0:T(8,128)(2,1)S(1)} %get-tuple-element.28), channel_id=1, source_target_pairs={{0,16},{1,17},{2,502},{3,503},{8,24},{9,25},{10,510},{11,511},{16,... | collective-permute-start | bytes 983048 | tf_op jit(solution)/shard_map/ppermute | solution.py:255
  79.0 1.0 %shard_map.50.refs_3_ = bf16[190,128,128]{2,1,0:T(8,128)(2,1)S(1)} custom-call(s32[351]{0:T(512)S(1)} %dynamic-slice_reduce_fusion.table.spots, bf16[17,128,128]{2,1,0:T(8,128)(2,1)S(1)} %get-tuple-element.20.refs_0_, bf16[52,128,128]{2,1,0:T(8,128)(2,1)S(1)} %bitcast.6, bf16[20,128,128]{2,1,0:T(8,128)(2,1)S(1)} %bitcast.9, ...), custom_call_target="tpu_custom_call" | custom-call | tf_op jit(solution)/shard_map/pallas_call | solution.py:280
  80.0 13.3 %collective-permute-done.5.refs_2_ = bf16[10,128,128]{2,1,0:T(8,128)(2,1)S(1)} collective-permute-done((bf16[10,128,128]{2,1,0:T(8,128)(2,1)S(1)}, bf16[10,128,128]{2,1,0:T(8,128)(2,1)S(1)}, u32[]{:S(2)}, u32[]{:S(2)}) %collective-permute-start.5) | collective-permute-done | bytes 327712 | tf_op jit(solution)/shard_map/ppermute | solution.py:255
  93.3 5.9 %shard_map.51 = (f32[1,128,2688]{2,1,0:T(8,128)}, bf16[190,128,128]{2,1,0:T(8,128)(2,1)S(1)}) custom-call(s32[351]{0:T(512)S(1)} %dynamic-slice_reduce_fusion.table.spots, s32[1,21]{1,0:T(1,128)S(1)} %copy-done.3, bf16[128,2176]{1,0:T(8,128)(2,1)S(1)} %get-tuple-element.18.masked, ...), custom_call_target="tpu_custom_call", output_to_operand_aliasing={{1}: (6, {})} | custom-call | tf_op jit(solution)/shard_map/pallas_call | solution.py:282
  (9 shorter events, 0.0 us)
Async XLA Ops:
  0.0 1.1 %copy-start.1 = (bf16[1,128,2176]{2,1,0:T(8,128)(2,1)S(1)}, bf16[1,128,2176]{2,1,0:T(8,128)(2,1)}, u32[]{:S(2)}) copy-start(bf16[1,128,2176]{2,1,0:T(8,128)(2,1)} %strip.1) | copy-start | bytes 1671172
  1.1 0.7 copy-start.2
  2.7 1.2 %copy-start = (bf16[4,13,128,128]{3,2,1,0:T(8,128)(2,1)}, bf16[4,13,128,128]{3,2,1,0:T(8,128)(2,1)S(1)}, u32[]{:S(2)}) copy-start(bf16[4,13,128,128]{3,2,1,0:T(8,128)(2,1)S(1)} %get-tuple-element.21) | copy-start | bytes 5111812
  3.9 21.1 %all-to-all-start = ((bf16[4,13,128,128]{3,2,1,0:T(8,128)(2,1)}), bf16[4,13,128,128]{3,2,1,0:T(8,128)(2,1)S(1)}, u32[]{:S(2)}, u32[]{:S(2)}) async-start(bf16[4,13,128,128]{3,2,1,0:T(8,128)(2,1)} %copy-done), calls=%async_computation | async-start | bytes 3407872 | tf_op jit(solution)/shard_map/all_to_all | solution.py:258
  8.7 18.4 %collective-permute-start = (bf16[5,128,128]{2,1,0:T(8,128)(2,1)S(1)}, bf16[5,128,128]{2,1,0:T(8,128)(2,1)S(1)}, u32[]{:S(2)}, u32[]{:S(2)}) collective-permute-start(bf16[5,128,128]{2,1,0:T(8,128)(2,1)S(1)} %get-tuple-element.19), channel_id=1, source_target_pairs={{0,4},{1,5},{2,6},{3,7},{4,0},{5,1},{6,2},{7,3},{8,12},{9,13},{10,... | collective-permute-start | bytes 491528 | tf_op jit(solution)/shard_map/ppermute | solution.py:255
  27.2 30.6 %collective-permute-start.2 = (bf16[52,128,128]{2,1,0:T(8,128)(2,1)S(1)}, bf16[52,128,128]{2,1,0:T(8,128)(2,1)S(1)}, u32[]{:S(2)}, u32[]{:S(2)}) collective-permute-start(bf16[52,128,128]{2,1,0:T(8,128)(2,1)S(1)} %bitcast.3), channel_id=1, source_target_pairs={{0,8},{1,9},{2,10},{3,11},{4,12},{5,13},{6,14},{7,15},{8,0},{9,1},... | collective-permute-start | bytes 5111816 | tf_op jit(solution)/shard_map/ppermute | solution.py:255
  34.8 23.0 %collective-permute-start.1 = (bf16[24,128,128]{2,1,0:T(8,128)(2,1)S(1)}, bf16[24,128,128]{2,1,0:T(8,128)(2,1)S(1)}, u32[]{:S(2)}, u32[]{:S(2)}) collective-permute-start(bf16[24,128,128]{2,1,0:T(8,128)(2,1)S(1)} %shard_map.47), channel_id=1, source_target_pairs={{0,4},{1,5},{2,6},{3,7},{116,128},{117,129},{118,130},{119,131},{1... | collective-permute-start | bytes 2359304 | tf_op jit(solution)/shard_map/ppermute | solution.py:255
  36.9 42.1 %collective-permute-start.6 = (bf16[40,128,128]{2,1,0:T(8,128)(2,1)S(1)}, bf16[40,128,128]{2,1,0:T(8,128)(2,1)S(1)}, u32[]{:S(2)}, u32[]{:S(2)}) collective-permute-start(bf16[40,128,128]{2,1,0:T(8,128)(2,1)S(1)} %shard_map.49), channel_id=1, source_target_pairs={{0,508},{1,509},{2,510},{3,511},{4,504},{5,505},{6,506},{7,507},{8... | collective-permute-start | bytes 3932168 | tf_op jit(solution)/shard_map/ppermute | solution.py:255
  59.3 34.0 %collective-permute-start.4 = (bf16[21,128,128]{2,1,0:T(8,128)(2,1)S(1)}, bf16[21,128,128]{2,1,0:T(8,128)(2,1)S(1)}, u32[]{:S(2)}, u32[]{:S(2)}) collective-permute-start(bf16[21,128,128]{2,1,0:T(8,128)(2,1)S(1)} %get-tuple-element.27), channel_id=1, source_target_pairs={{0,508},{1,509},{2,510},{3,511},{4,504},{5,505},{6,506},{7,507},{8... | collective-permute-start | bytes 2064392 | tf_op jit(solution)/shard_map/ppermute | solution.py:255
  65.2 28.1 %collective-permute-start.3 = (bf16[20,128,128]{2,1,0:T(8,128)(2,1)S(1)}, bf16[20,128,128]{2,1,0:T(8,128)(2,1)S(1)}, u32[]{:S(2)}, u32[]{:S(2)}) collective-permute-start(bf16[20,128,128]{2,1,0:T(8,128)(2,1)S(1)} %bitcast.8), channel_id=1, source_target_pairs={{0,8},{1,9},{2,10},{3,11},{4,12},{5,13},{6,14},{7,15},{8,0},{9,1},... | collective-permute-start | bytes 1966088 | tf_op jit(solution)/shard_map/ppermute | solution.py:255
  77.0 16.3 %copy-start.3 = (s32[1,21]{1,0:T(1,128)S(1)}, s32[1,21]{1,0:T(1,128)}, u32[]{:S(2)}) copy-start(s32[1,21]{1,0:T(1,128)} %keep.1) | copy-start | bytes 256
  77.0 16.3 %collective-permute-start.5 = (bf16[10,128,128]{2,1,0:T(8,128)(2,1)S(1)}, bf16[10,128,128]{2,1,0:T(8,128)(2,1)S(1)}, u32[]{:S(2)}, u32[]{:S(2)}) collective-permute-start(bf16[10,128,128]{2,1,0:T(8,128)(2,1)S(1)} %get-tuple-element.28), channel_id=1, source_target_pairs={{0,16},{1,17},{2,502},{3,503},{8,24},{9,25},{10,510},{11,511},{16,... | collective-permute-start | bytes 983048 | tf_op jit(solution)/shard_map/ppermute | solution.py:255
